TPU v7x, 256 devices: a whole 4x4x8 slice. The times are simulated.
256 devices in a mesh: ctx: 16 (over y_lo, x, core), tp: 16 (over y_hi, z).
Axes of the slice: x: 4, y: 4 (y_hi: 2, y_lo: 2; y = y_hi * 2 + y_lo), z: 8, core: 2. Of those that a mesh axis runs over, the one named last changes fastest.
Arguments:
- query: bfloat16 [4096, 32768], P('tp', 'ctx'), may hold values from -6 to 6
- key_in: bfloat16 [4096, 32768], P('tp', 'ctx'), may hold values from -6 to 6
- value: bfloat16 [4096, 32768], P('tp', 'ctx'), may hold values from -6 to 6
- grad_out: bfloat16 [4096, 32768], P('tp', 'ctx'), may hold values from -6 to 6
- filter_raw: float32 [256, 32768], P('ctx'), may hold values from -6 to 6
Outputs:
- grad_query: bfloat16 [4096, 32768], P('tp', 'ctx')
- grad_key: bfloat16 [4096, 32768], P('tp', 'ctx')
- grad_value: bfloat16 [4096, 32768], P('tp', 'ctx')
- filter_grad: float32 [256, 32768], P('ctx', 'tp')
All inputs are finite; a program needn't handle non-finite values.
Results may differ from a plain program's by a relative error of at most 0.0058.
Values may be sent and summed in bfloat16 or wider, within the bound.
No kernel may reach another device: no remote copies, remote signals or barrier semaphores. Data moves between devices by JAX's collectives and lax.ppermute only.
A program may use at most 128 MiB of HBM per device.

v0:
```python
import functools
import math

import jax
import jax.numpy as jnp
import ml_dtypes
import numpy as np
from jax import lax
from jax.experimental import pallas as pl
from jax.experimental.pallas import tpu as pltpu
from jax.sharding import PartitionSpec as P

LANES = 128
VMEM_LIMIT = 56 * 2**20
f32 = jnp.float32
bf16 = jnp.bfloat16


def split_parts(table):
    high = table.astype(np.float32).astype(ml_dtypes.bfloat16)
    low = (table - high.astype(np.float64)).astype(np.float32).astype(ml_dtypes.bfloat16)
    return high, low


@functools.lru_cache(maxsize=None)
def make_tables(length):
    rows = length // LANES
    total = 2 * length
    a = np.arange(rows, dtype=np.float64)
    k1 = np.arange(rows, dtype=np.float64) + 0.5
    b = np.arange(LANES, dtype=np.float64)
    first = 2.0 * np.pi * np.outer(k1, a) / (2 * rows)
    turn = 2.0 * np.pi * np.outer(k1, b) / total
    second = 2.0 * np.pi * np.outer(b, b) / LANES
    c2, s2 = np.cos(second), np.sin(second)
    w_high, w_low = split_parts(np.concatenate([np.cos(first), -np.sin(first)], 0))
    m_high, m_low = split_parts(np.block([[c2, -s2], [s2, c2]]))
    mi_high, mi_low = split_parts(np.block([[c2, s2], [-s2, c2]]))
    wi_high, wi_low = split_parts(np.concatenate([np.cos(first).T, -np.sin(first).T], 1))
    scale = 2.0 / total
    return dict(
        w=np.concatenate([w_high, w_low, w_high], 1),
        m=np.concatenate([m_high, m_low, m_high], 0),
        mi=np.concatenate([mi_high, mi_low], 0),
        wi=np.concatenate([wi_high, wi_low], 1),
        turn_cos=np.cos(turn).astype(np.float32),
        turn_sin=np.sin(turn).astype(np.float32),
        back_cos=(scale * np.cos(turn)).astype(np.float32),
        back_sin=(scale * np.sin(turn)).astype(np.float32),
    )


def dot(x, y):
    return jnp.dot(x, y, preferred_element_type=f32)


def whole(table):
    return pl.BlockSpec(table.shape, lambda *_: (0,) * table.ndim)


def params(grid_rank):
    return pltpu.CompilerParams(
        dimension_semantics=("arbitrary",) * grid_rank, vmem_limit_bytes=VMEM_LIMIT
    )


def gate_kernel(q_ref, k_ref, v_ref, g_ref, out_ref, s0, s1):
    group, length = k_ref.shape
    cuts = length // LANES
    for j in range(cuts):
        lanes = slice(j * LANES, (j + 1) * LANES)
        rows = slice(j * group, (j + 1) * group)
        s0[rows, :] = k_ref[:, lanes].astype(f32) * v_ref[:, lanes].astype(f32)
        s1[rows, :] = g_ref[:, lanes].astype(f32) * q_ref[:, lanes].astype(f32)
    for c in range(group):
        out_ref[0, 0, c] = s0[pl.ds(c, cuts, stride=group), :].astype(bf16)
        out_ref[0, 1, c] = s1[pl.ds(c, cuts, stride=group), :].astype(bf16)


def gate(query, key_in, value, grad_out, n):
    channels, length = query.shape
    group = channels // n
    cuts = length // LANES
    spec = pl.BlockSpec((group, length), lambda i: (i, 0))
    return pl.pallas_call(
        gate_kernel,
        grid=(n,),
        in_specs=[spec] * 4,
        out_specs=pl.BlockSpec((1, 2, group, cuts, LANES), lambda i: (i, 0, 0, 0, 0)),
        out_shape=jax.ShapeDtypeStruct((n, 2, group, cuts, LANES), bf16),
        scratch_shapes=[pltpu.VMEM((group * cuts, LANES), f32)] * 2,
        compiler_params=params(1),
        cost_estimate=pl.CostEstimate(
            flops=2 * channels * length, bytes_accessed=12 * channels * length, transcendentals=0
        ),
        name="gate",
    )(query, key_in, value, grad_out)


def finish_kernel(tok_ref, k_ref, v_ref, g_ref, gq_ref, gk_ref, gv_ref, s0, s1):
    group, length = k_ref.shape
    cuts = length // LANES
    for c in range(group):
        rows = slice(c * cuts, (c + 1) * cuts)
        s0[rows, :] = tok_ref[0, 0, c].astype(f32)
        s1[rows, :] = tok_ref[0, 1, c].astype(f32)
    for j in range(cuts):
        lanes = slice(j * LANES, (j + 1) * LANES)
        conv = s0[pl.ds(j, group, stride=cuts), :]
        dgated = s1[pl.ds(j, group, stride=cuts), :]
        gq_ref[:, lanes] = (g_ref[:, lanes].astype(f32) * conv).astype(bf16)
        gk_ref[:, lanes] = (dgated * v_ref[:, lanes].astype(f32)).astype(bf16)
        gv_ref[:, lanes] = (dgated * k_ref[:, lanes].astype(f32)).astype(bf16)


def finish(tok, key_in, value, grad_out):
    n, _, group, cuts, _ = tok.shape
    channels, length = key_in.shape
    spec = pl.BlockSpec((group, length), lambda i: (i, 0))
    return pl.pallas_call(
        finish_kernel,
        grid=(n,),
        in_specs=[pl.BlockSpec((1, 2, group, cuts, LANES), lambda i: (i, 0, 0, 0, 0))] + [spec] * 3,
        out_specs=[spec] * 3,
        out_shape=[jax.ShapeDtypeStruct((channels, length), bf16)] * 3,
        scratch_shapes=[pltpu.VMEM((group * cuts, LANES), f32)] * 2,
        compiler_params=params(1),
        cost_estimate=pl.CostEstimate(
            flops=3 * channels * length, bytes_accessed=16 * channels * length, transcendentals=0
        ),
        name="finish",
    )(tok, key_in, value, grad_out)


def turned(stage, turn_cos, turn_sin, rows, at):
    lanes = slice(at * LANES, (at + 1) * LANES)
    re, im = stage[:rows, lanes], stage[rows:, lanes]
    return jnp.concatenate([re * turn_cos + im * turn_sin, im * turn_cos - re * turn_sin], 1)


def filter_kernel(x_ref, w_ref, m_ref, tc_ref, ts_ref, out_ref, *, scale):
    pair, rows, _ = x_ref.shape
    x = jnp.concatenate([x_ref[i] for i in range(pair)], 1)
    high = x.astype(bf16)
    low = (x - high.astype(f32)).astype(bf16)
    stage = dot(w_ref[...], jnp.concatenate([high, high, low], 0))
    for i in range(pair):
        u = turned(stage, tc_ref[...], ts_ref[...], rows, i) * scale
        u_high = u.astype(bf16)
        u_low = (u - u_high.astype(f32)).astype(bf16)
        out_ref[i] = dot(jnp.concatenate([u_high, u_high, u_low], 1), m_ref[...])


def filter_spectrum(filt, t, scale):
    n, rows, _ = filt.shape
    pair = 2
    tables = [t["w"], t["m"], t["turn_cos"], t["turn_sin"]]
    return pl.pallas_call(
        functools.partial(filter_kernel, scale=scale),
        grid=(n // pair,),
        in_specs=[pl.BlockSpec((pair, rows, LANES), lambda i: (i, 0, 0))] + [whole(x) for x in tables],
        out_specs=pl.BlockSpec((pair, rows, 2 * LANES), lambda i: (i, 0, 0)),
        out_shape=jax.ShapeDtypeStruct((n, rows, 2 * LANES), f32),
        compiler_params=params(1),
        cost_estimate=pl.CostEstimate(
            flops=12 * n * rows * LANES * 512, bytes_accessed=16 * n * rows * LANES, transcendentals=0
        ),
        name="filter_spectrum",
    )(filt, *tables)


def back(spec, mi_ref, wi_ref, bc, bs, pair, rows):
    stage = dot(jnp.concatenate([spec, spec], 1), mi_ref[...])
    re_parts, im_parts = [], []
    for i in range(pair):
        re = stage[i * rows : (i + 1) * rows, :LANES]
        im = stage[i * rows : (i + 1) * rows, LANES:]
        re_parts.append((re * bc - im * bs).astype(bf16))
        im_parts.append((re * bs + im * bc).astype(bf16))
    v = jnp.concatenate([jnp.concatenate(re_parts, 1), jnp.concatenate(im_parts, 1)], 0)
    return dot(wi_ref[...], jnp.concatenate([v, v], 0))


def spectra_kernel(
    x_ref, f_ref, w_ref, m_ref, tc_ref, ts_ref, mi_ref, wi_ref, bc_ref, bs_ref,
    cross_ref, conv_ref, dgated_ref, *, scale,
):
    n, _, pair, cuts, _ = x_ref.shape
    rows = n * cuts
    x = jnp.concatenate(
        [x_ref[:, s, i].reshape(rows, LANES) for s in range(2) for i in range(pair)], 1
    )
    stage = dot(w_ref[:, : 2 * rows], jnp.concatenate([x, x], 0))
    u = jnp.concatenate(
        [turned(stage, tc_ref[...], ts_ref[...], rows, i).astype(bf16) for i in range(2 * pair)], 0
    )
    spec = dot(jnp.concatenate([u, u], 1), m_ref[: 4 * LANES, :])
    half = pair * rows
    gr, gi = spec[:half, :LANES], spec[:half, LANES:]
    dr, di = spec[half:, :LANES], spec[half:, LANES:]
    cross = jnp.concatenate([dr * gr + di * gi, di * gr - dr * gi], 1).astype(bf16)
    f = f_ref[...].reshape(half, 2 * LANES)
    fr, fi = f[:, :LANES], f[:, LANES:]
    conv_ref[...] = (
        jnp.concatenate([fr * gr - fi * gi, fr * gi + fi * gr], 1).astype(bf16).reshape(conv_ref.shape)
    )
    dgated_ref[...] = (
        jnp.concatenate([dr * fr + di * fi, di * fr - dr * fi], 1).astype(bf16).reshape(dgated_ref.shape)
    )
    out = back(cross, mi_ref, wi_ref, bc_ref[...] * scale, bs_ref[...] * scale, pair, rows)
    runs, halves = cross_ref.shape[:2]
    for h in range(halves):
        for z in range(runs):
            at = (h * runs + z) * cuts
            for i in range(pair):
                cross_ref[z, h, i] = out[at : at + cuts, i * LANES : (i + 1) * LANES]


def spectra(x, f, t, scale, runs, halves):
    n, _, group, cuts, _ = x.shape
    rows = n * cuts
    pair = 2
    tables = [t[k] for k in ("w", "m", "turn_cos", "turn_sin", "mi", "wi", "back_cos", "back_sin")]
    spec_block = pl.BlockSpec((pair, rows, 2 * LANES), lambda i: (i, 0, 0))
    return pl.pallas_call(
        functools.partial(spectra_kernel, scale=scale),
        grid=(group // pair,),
        in_specs=[pl.BlockSpec((n, 2, pair, cuts, LANES), lambda i: (0, 0, i, 0, 0)), spec_block]
        + [whole(v) for v in tables],
        out_specs=[
            pl.BlockSpec((runs, halves, pair, cuts, LANES), lambda i: (0, 0, i, 0, 0)),
            spec_block,
            spec_block,
        ],
        out_shape=[
            jax.ShapeDtypeStruct((runs, halves, group, cuts, LANES), f32),
            jax.ShapeDtypeStruct((group, rows, 2 * LANES), bf16),
            jax.ShapeDtypeStruct((group, rows, 2 * LANES), bf16),
        ],
        compiler_params=params(1),
        cost_estimate=pl.CostEstimate(
            flops=24 * group * rows * LANES * 512, bytes_accessed=32 * group * rows * LANES, transcendentals=0
        ),
        name="spectra",
    )(x, f, *tables)


def signals_kernel(conv_ref, dgated_ref, mi_ref, wi_ref, bc_ref, bs_ref, out_ref):
    n, _, pair, cuts, _ = out_ref.shape
    rows = n * cuts
    both = jnp.concatenate(
        [r[...].reshape(pair * rows, 2 * LANES) for r in (conv_ref, dgated_ref)], 0
    )
    out = back(both, mi_ref, wi_ref, bc_ref[...], bs_ref[...], 2 * pair, rows).astype(bf16)
    for s in range(2):
        for i in range(pair):
            lanes = slice((s * pair + i) * LANES, (s * pair + i + 1) * LANES)
            out_ref[:, s, i] = out[:, lanes].reshape(n, cuts, LANES)


def signals(conv, dgated, t, n):
    group, rows, _ = conv.shape
    cuts = rows // n
    pair = 2
    tables = [t[k] for k in ("mi", "wi", "back_cos", "back_sin")]
    spec_block = pl.BlockSpec((pair, rows, 2 * LANES), lambda i: (i, 0, 0))
    return pl.pallas_call(
        signals_kernel,
        grid=(group // pair,),
        in_specs=[spec_block] * 2 + [whole(v) for v in tables],
        out_specs=pl.BlockSpec((n, 2, pair, cuts, LANES), lambda i: (0, 0, i, 0, 0)),
        out_shape=jax.ShapeDtypeStruct((n, 2, group, cuts, LANES), bf16),
        compiler_params=params(1),
        cost_estimate=pl.CostEstimate(
            flops=16 * group * rows * LANES * 512, bytes_accessed=12 * group * rows * LANES, transcendentals=0
        ),
        name="signals",
    )(conv, dgated, *tables)


def body(query, key_in, value, grad_out, filter_raw, *, n_ctx, n_tp):
    group, length = filter_raw.shape
    rows = length // LANES
    root = 1.0 / math.sqrt(length)
    t = {k: jnp.asarray(v) for k, v in make_tables(length).items()}
    halves = 2
    runs = n_tp // halves

    sent = gate(query, key_in, value, grad_out, n_ctx)
    got = lax.all_to_all(sent, "ctx", split_axis=0, concat_axis=0, tiled=True)
    filt = filter_spectrum(filter_raw.reshape(group, rows, LANES), t, root)
    cross, conv, dgated = spectra(got, filt, t, root, runs, halves)
    near = [[h * runs + z for z in range(runs)] for h in range(halves)]
    part = lax.psum_scatter(cross, "tp", scatter_dimension=0, tiled=True, axis_index_groups=near)
    tok = lax.all_to_all(signals(conv, dgated, t, n_ctx), "ctx", split_axis=0, concat_axis=0, tiled=True)
    grad_query, grad_key, grad_value = finish(tok, key_in, value, grad_out)
    side = lax.axis_index("tp") // runs
    mine = lax.dynamic_index_in_dim(part[0], side, 0, keepdims=False)
    other = lax.dynamic_index_in_dim(part[0], 1 - side, 0, keepdims=False)
    far = [(i, (i + runs) % n_tp) for i in range(n_tp)]
    filter_grad = (mine + lax.ppermute(other, "tp", far)).reshape(group, length // n_tp)
    return (grad_query, grad_key, grad_value, filter_grad)


def solution(mesh):
    placed = (P("tp", "ctx"), P("tp", "ctx"), P("tp", "ctx"), P("tp", "ctx"), P("ctx", None))
    return jax.shard_map(
        functools.partial(body, n_ctx=mesh.shape["ctx"], n_tp=mesh.shape["tp"]),
        mesh=mesh,
        in_specs=placed,
        out_specs=(P("tp", "ctx"), P("tp", "ctx"), P("tp", "ctx"), P("ctx", "tp")),
        check_vma=False,
    )
```

profile of v0, /device:TPU:4, one launch (start us, length us, event | category | flops | bytes accessed | tf_op | source)
XLA Modules:
  0.0 136.0 jit_solution(17311152035480751476)
XLA Ops:
  7.2 10.3 %gate.1 = bf16[16,2,16,16,128]{4,3,2,1,0:T(8,128)(2,1)} custom-call(bf16[256,2048]{1,0:T(8,128)(2,1)} %q_ref.1, bf16[256,2048]{1,0:T(8,128)(2,1)} %k_ref.3, bf16[256,2048]{1,0:T(8,128)(2,1)} %v_ref.3, bf16[256,2048]{1,0:T(8,128)(2,1)} %g_ref.3), custom_call_target="tpu_custom_call" | custom-call | flops 1048576 | bytes 6291456 | tf_op jit(solution)/shard_map/gate/pallas_call | solution.py:85
  17.5 0.0 copy-start.1
  17.5 6.5 %all-to-all-start = ((bf16[16,2,16,16,128]{4,3,2,1,0:T(8,128)(2,1)}), bf16[16,2,16,16,128]{4,3,2,1,0:T(8,128)(2,1)}, u32[]{:S(2)}, u32[]{:S(2)}) async-start(bf16[16,2,16,16,128]{4,3,2,1,0:T(8,128)(2,1)} %gate.1), calls=%async_computation | async-start | bytes 4194304 | tf_op jit(solution)/shard_map/all_to_all | solution.py:290
  24.0 0.0 reduce-scatter.2.cloned.1.call-start
  24.1 0.0 copy-done.1
  24.1 1.8 %copy.17 = f32[2,8,256,128]{3,2,1,0:T(8,128)} copy(f32[2,8,256,128]{3,1,2,0:T(8,128)S(1)} %bitcast.10) | data formatting | bytes 4194304
  25.9 10.8 %filter_spectrum.1.f_ref = f32[16,256,256]{2,1,0:T(8,128)} custom-call(f32[16,256,128]{2,1,0:T(8,128)} %bitcast.11, bf16[512,768]{1,0:T(8,128)(2,1)} %constant.47.clone.w_ref, bf16[768,256]{1,0:T(8,128)(2,1)} %constant.48.clone.m_ref, f32[256,128]{1,0:T(8,128)} %constant.51.clone.tc_ref, f32[256,128]{1,0:T(8,128)} %constant.52.clone.ts_ref), custom_call_target="tpu_custom_call" | custom-call | flops 3221225472 | bytes 8388608 | tf_op jit(solution)/shard_map/filter_spectrum/pallas_call | solution.py:158
  36.6 14.2 %all-to-all-done.x_ref = bf16[16,2,16,16,128]{4,3,2,1,0:T(8,128)(2,1)} async-done(((bf16[16,2,16,16,128]{4,3,2,1,0:T(8,128)(2,1)}), bf16[16,2,16,16,128]{4,3,2,1,0:T(8,128)(2,1)}, u32[]{:S(2)}, u32[]{:S(2)}) %all-to-all-start) | async-done | bytes 2097184 | tf_op jit(solution)/shard_map/all_to_all | solution.py:290
  50.9 17.0 %spectra.1 = (f32[8,2,16,16,128]{4,3,2,1,0:T(8,128)}, bf16[16,256,256]{2,1,0:T(8,128)(2,1)}, bf16[16,256,256]{2,1,0:T(8,128)(2,1)}) custom-call(bf16[16,2,16,16,128]{4,3,2,1,0:T(8,128)(2,1)} %all-to-all-done.x_ref, f32[16,256,256]{2,1,0:T(8,128)} %filter_spectrum.1.f_ref, bf16[512,768]{1,0:T(8,128)(2,1)} %constant.47.clone.w_ref, ...), custom_call_target="tpu_custom_call" | custom-call | flops 6442450944 | bytes 16777216 | tf_op jit(solution)/shard_map/spectra/pallas_call | solution.py:225
  67.9 0.0 reduce-scatter.2.cloned.1.call-update
  67.9 12.1 %signals.1 = bf16[16,2,16,16,128]{4,3,2,1,0:T(8,128)(2,1)} custom-call(bf16[16,256,256]{2,1,0:T(8,128)(2,1)} %get-tuple-element.10.conv_ref, bf16[16,256,256]{2,1,0:T(8,128)(2,1)} %get-tuple-element.11.dgated_ref, bf16[512,256]{1,0:T(8,128)(2,1)} %constant.49.clone.mi_ref, bf16[256,1024]{1,0:T(8,128)(2,1)} %constant.50.clone.wi_ref, ...), custom_call_target="tpu_custom_call" | custom-call | flops 4294967296 | bytes 6291456 | tf_op jit(solution)/shard_map/signals/pallas_call | solution.py:267
  80.0 6.0 %all-to-all-start.1 = ((bf16[16,2,16,16,128]{4,3,2,1,0:T(8,128)(2,1)}), bf16[16,2,16,16,128]{4,3,2,1,0:T(8,128)(2,1)S(1)}, u32[]{:S(2)}, u32[]{:S(2)}) async-start(bf16[16,2,16,16,128]{4,3,2,1,0:T(8,128)(2,1)} %signals.1), calls=%async_computation.1 | async-start | bytes 4194304 | tf_op jit(solution)/shard_map/all_to_all | solution.py:295
  86.0 26.9 %reduce-scatter.2.cloned.1.call-done = f32[1,2,16,16,128]{4,3,2,1,0:T(8,128)} async-done(((f32[8,2,16,16,128]{4,3,2,1,0:T(8,128)}), f32[1,2,16,16,128]{4,3,2,1,0:T(8,128)}) %reduce-scatter.2.cloned.1.call-update) | async-done | bytes 262160 | tf_op jit(solution)/shard_map/reduce_scatter | solution.py:294
  112.9 0.9 dynamic-slice_bitcast_fusion
  113.8 2.8 %collective-permute-start = (f32[16,16,128]{2,1,0:T(8,128)S(1)}, f32[16,16,128]{2,1,0:T(8,128)S(1)}, u32[]{:S(2)}, u32[]{:S(2)}) collective-permute-start(f32[16,16,128]{2,1,0:T(8,128)S(1)} %dynamic-slice_bitcast_fusion), channel_id=1, source_target_pairs={{0,8},{1,9},{2,10},{3,11},{4,12},{5,13},{6,14},{7,15},{8,0},{9,1},... | collective-permute-start | bytes 393224 | tf_op jit(solution)/shard_map/ppermute | solution.py:301
  116.6 0.0 copy-start.2
  116.6 0.0 all-to-all-done.1.tok_ref
  116.6 0.0 copy-start
  116.6 1.3 copy-done
  117.9 10.5 %finish.1 = (bf16[256,2048]{1,0:T(8,128)(2,1)}, bf16[256,2048]{1,0:T(8,128)(2,1)}, bf16[256,2048]{1,0:T(8,128)(2,1)}) custom-call(bf16[16,2,16,16,128]{4,3,2,1,0:T(8,128)(2,1)} %copy-done, bf16[256,2048]{1,0:T(8,128)(2,1)} %k_ref.3, bf16[256,2048]{1,0:T(8,128)(2,1)} %v_ref.3, bf16[256,2048]{1,0:T(8,128)(2,1)} %g_ref.3), custom_call_target="tpu_custom_call" | custom-call | flops 1572864 | bytes 8388608 | tf_op jit(solution)/shard_map/finish/pallas_call | solution.py:120
  128.4 0.0 collective-permute-done
  128.5 0.0 copy-done.2
  128.5 0.7 copy.20
  (1 shorter events, 0.0 us)
Async XLA Ops:
  17.5 6.6 %copy-start.1 = (f32[16,32768]{1,0:T(8,128)S(1)}, f32[16,32768]{1,0:T(8,128)}, u32[]{:S(2)}) copy-start(f32[16,32768]{1,0:T(8,128)} %param.17) | copy-start | bytes 6291460
  17.5 33.4 %all-to-all-start = ((bf16[16,2,16,16,128]{4,3,2,1,0:T(8,128)(2,1)}), bf16[16,2,16,16,128]{4,3,2,1,0:T(8,128)(2,1)}, u32[]{:S(2)}, u32[]{:S(2)}) async-start(bf16[16,2,16,16,128]{4,3,2,1,0:T(8,128)(2,1)} %gate.1), calls=%async_computation | async-start | bytes 4194304 | tf_op jit(solution)/shard_map/all_to_all | solution.py:290
  24.0 88.8 %reduce-scatter.2.cloned.1.call-start = ((), (), s32[]{:S(2)}) async-start(), calls=%async_computation.3 | async-start | bytes 2359296 | tf_op jit(solution)/shard_map/reduce_scatter | solution.py:294
  80.0 36.6 %all-to-all-start.1 = ((bf16[16,2,16,16,128]{4,3,2,1,0:T(8,128)(2,1)}), bf16[16,2,16,16,128]{4,3,2,1,0:T(8,128)(2,1)S(1)}, u32[]{:S(2)}, u32[]{:S(2)}) async-start(bf16[16,2,16,16,128]{4,3,2,1,0:T(8,128)(2,1)} %signals.1), calls=%async_computation.1 | async-start | bytes 4194304 | tf_op jit(solution)/shard_map/all_to_all | solution.py:295
  113.8 14.7 %collective-permute-start = (f32[16,16,128]{2,1,0:T(8,128)S(1)}, f32[16,16,128]{2,1,0:T(8,128)S(1)}, u32[]{:S(2)}, u32[]{:S(2)}) collective-permute-start(f32[16,16,128]{2,1,0:T(8,128)S(1)} %dynamic-slice_bitcast_fusion), channel_id=1, source_target_pairs={{0,8},{1,9},{2,10},{3,11},{4,12},{5,13},{6,14},{7,15},{8,0},{9,1},... | collective-permute-start | bytes 393224 | tf_op jit(solution)/shard_map/ppermute | solution.py:301
  116.6 11.9 %copy-start.2 = (f32[1,2,16,16,128]{4,3,2,1,0:T(8,128)S(1)}, f32[1,2,16,16,128]{4,3,2,1,0:T(8,128)}, u32[]{:S(2)}) copy-start(f32[1,2,16,16,128]{4,3,2,1,0:T(8,128)} %reduce-scatter.2.cloned.1.call-done) | copy-start | bytes 786436
  116.6 1.3 copy-start
Sparse Core Ops, SparseCore 0:
  68.0 44.7 reduce-scatter.1
where the time goes:
time: 137 us; the launch traced here: 136 us
  Pallas kernels  60.8 us (44%)
  waiting for transfers between devices  41.1 us (30%)
  starting transfers between devices  15.4 us (11%)
  between operations  14.1 us (10%)
  local copies, waits for them, and re-layouts  4.72 us (3%)
    reduce_scatter x1, waiting for transfers between devices, body(): lax.psum_scatter(cross, 'tp', scatter_dimension=0, tiled=True, axis_index...  26.9 us
    pallas_call x1, Pallas kernels, spectra(): pl.pallas_call(functools.partial(spectra_kernel, scale=scale), grid=(grou...  17 us
    all_to_all x1, waiting for transfers between devices, body(): got = lax.all_to_all(sent, 'ctx', split_axis=0, concat_axis=0, tiled=True)  14.2 us
    pallas_call x1, Pallas kernels, signals(): pl.pallas_call(signals_kernel, grid=(group // pair,), in_specs=[spec_bloc...  12.1 us
    pallas_call x1, Pallas kernels, filter_spectrum(): pl.pallas_call(functools.partial(filter_kernel, scale=scale), grid=(n //...  10.8 us
    pallas_call x1, Pallas kernels, finish(): pl.pallas_call(finish_kernel, grid=(n,), in_specs=[pl.BlockSpec((1, 2, gr...  10.5 us
    pallas_call x1, Pallas kernels, gate(): pl.pallas_call(gate_kernel, grid=(n,), in_specs=[spec] * 4, out_specs=pl....  10.3 us
    all_to_all x1, starting transfers between devices, body(): got = lax.all_to_all(sent, 'ctx', split_axis=0, concat_axis=0, tiled=True)  6.55 us
  transfers between devices with their start and end apart: 4, of which 2 were waited for; matrix products, arithmetic and copies ran while one was open for 2% of the time, Pallas kernels for 25%

commit v1 on v0

v1 whole, which is shorter than its diff:
```python
import functools
import math

import jax
import jax.numpy as jnp
import ml_dtypes
import numpy as np
from jax import lax
from jax.experimental import pallas as pl
from jax.experimental.pallas import tpu as pltpu
from jax.sharding import PartitionSpec as P

LANES = 128
VMEM_LIMIT = 56 * 2**20
TOKEN_STEPS = 4
PAIR = 8
CROSS_BACK = ("mi2", "wi2")
TOKEN_BACK = ("mi", "wi")
f32 = jnp.float32
bf16 = jnp.bfloat16


def split_parts(table):
    high = table.astype(np.float32).astype(ml_dtypes.bfloat16)
    low = (table - high.astype(np.float64)).astype(np.float32).astype(ml_dtypes.bfloat16)
    return high, low


@functools.lru_cache(maxsize=None)
def make_tables(length):
    rows = length // LANES
    total = 2 * length
    a = np.arange(rows, dtype=np.float64)
    k1 = np.arange(rows, dtype=np.float64) + 0.5
    b = np.arange(LANES, dtype=np.float64)
    first = 2.0 * np.pi * np.outer(k1, a) / (2 * rows)
    turn = 2.0 * np.pi * np.outer(k1, b) / total
    second = 2.0 * np.pi * np.outer(b, b) / LANES
    c2, s2 = np.cos(second), np.sin(second)
    w_high, w_low = split_parts(np.concatenate([np.cos(first), -np.sin(first)], 0))
    m_high, m_low = split_parts(np.block([[c2, -s2], [s2, c2]]))
    mi_high, mi_low = split_parts(np.block([[c2, s2], [-s2, c2]]))
    wi_high, wi_low = split_parts(np.concatenate([np.cos(first).T, -np.sin(first).T], 1))
    return dict(
        w3=np.concatenate([w_high, w_low, w_high], 1),
        m3=np.concatenate([m_high, m_low, m_high], 0),
        w=w_high,
        m=m_high,
        mi=mi_high,
        wi=wi_high,
        mi2=np.concatenate([mi_high, mi_low], 0),
        wi2=np.concatenate([wi_high, wi_low], 1),
        turn_cos=np.cos(turn).astype(np.float32),
        turn_sin=np.sin(turn).astype(np.float32),
    )


def dot(x, y):
    return jnp.dot(x, y, preferred_element_type=f32)


def whole(table):
    return pl.BlockSpec(table.shape, lambda *_: (0,) * table.ndim)


def params(grid_rank, limit=VMEM_LIMIT):
    return pltpu.CompilerParams(
        dimension_semantics=("arbitrary",) * grid_rank if grid_rank else None,
        vmem_limit_bytes=limit,
    )


def swap_table(size):
    index = np.arange(size * size).reshape(size, size)
    table = np.zeros((size * size, size * size), np.float32)
    table[index.T.reshape(-1), index.reshape(-1)] = 1.0
    return table.astype(ml_dtypes.bfloat16)


def copies(pairs, sems, at):
    return [pltpu.make_async_copy(src, dst, sems.at[at, i]) for i, (src, dst) in enumerate(pairs)]


def start(moves):
    for move in moves:
        move.start()


def wait(moves):
    for move in moves:
        move.wait()


ANY = pl.BlockSpec(memory_space=pl.ANY)
VMEM = pl.BlockSpec(memory_space=pltpu.VMEM)


def gate_kernel(q_ref, k_ref, v_ref, g_ref, swap_ref, out_ref, q, k, v, g, o, in_sems, out_sems):
    n, _, group, cuts, _ = out_ref.shape
    runs = n // TOKEN_STEPS

    def loads(step):
        rows = pl.ds(step * runs * group, runs * group)
        pairs = [(r.at[rows], s.at[rows]) for r, s in ((k_ref, k), (v_ref, v), (g_ref, g), (q_ref, q))]
        return copies(pairs, in_sems, step)

    def stores(step):
        at = pl.ds(step * runs, runs)
        return copies([(o.at[at], out_ref.at[at])], out_sems, step)

    for step in range(TOKEN_STEPS):
        start(loads(step))
    for step in range(TOKEN_STEPS):
        wait(loads(step))
        for run in range(step * runs, (step + 1) * runs):
            rows = slice(run * group, (run + 1) * group)

            def product(x, y):
                z = (x[rows, :].astype(f32) * y[rows, :].astype(f32)).astype(bf16)
                return jnp.concatenate([z[:, j * LANES : (j + 1) * LANES] for j in range(cuts)], 0)

            both = jnp.concatenate([product(k, v), product(g, q)], 1)
            out = dot(swap_ref[...], both).astype(bf16)
            for s in range(2):
                o[run, s] = out[:, s * LANES : (s + 1) * LANES].reshape(group, cuts, LANES)
        start(stores(step))
    for step in range(TOKEN_STEPS):
        wait(stores(step))


def gate(query, key_in, value, grad_out, n):
    channels, length = query.shape
    group = channels // n
    cuts = length // LANES
    swap = jnp.asarray(swap_table(group))
    sent = (n, 2, group, cuts, LANES)
    return pl.pallas_call(
        gate_kernel,
        in_specs=[ANY] * 4 + [VMEM],
        out_specs=ANY,
        out_shape=jax.ShapeDtypeStruct(sent, bf16),
        scratch_shapes=[pltpu.VMEM(query.shape, bf16)] * 4
        + [pltpu.VMEM(sent, bf16), pltpu.SemaphoreType.DMA((TOKEN_STEPS, 4)), pltpu.SemaphoreType.DMA((TOKEN_STEPS, 1))],
        compiler_params=params(0),
        cost_estimate=pl.CostEstimate(
            flops=2 * channels * length, bytes_accessed=12 * channels * length, transcendentals=0
        ),
        name="gate",
    )(query, key_in, value, grad_out, swap)


def finish_kernel(
    tok_ref, k_ref, v_ref, g_ref, swap_ref, gq_ref, gk_ref, gv_ref, tok, k, v, g, gq, gk, gv, in_sems, out_sems
):
    n, _, group, cuts, _ = tok_ref.shape
    runs = n // TOKEN_STEPS

    def loads(step):
        rows = pl.ds(step * runs * group, runs * group)
        at = pl.ds(step * runs, runs)
        pairs = [(tok_ref.at[at], tok.at[at])]
        pairs += [(r.at[rows], s.at[rows]) for r, s in ((g_ref, g), (v_ref, v), (k_ref, k))]
        return copies(pairs, in_sems, step)

    def stores(step):
        rows = pl.ds(step * runs * group, runs * group)
        pairs = [(s.at[rows], r.at[rows]) for r, s in ((gq_ref, gq), (gk_ref, gk), (gv_ref, gv))]
        return copies(pairs, out_sems, step)

    for step in range(TOKEN_STEPS):
        start(loads(step))
    for step in range(TOKEN_STEPS):
        wait(loads(step))
        for run in range(step * runs, (step + 1) * runs):
            rows = slice(run * group, (run + 1) * group)
            both = jnp.concatenate([tok[run, s].reshape(group * cuts, LANES) for s in range(2)], 1)
            out = dot(swap_ref[...], both)
            for j in range(cuts):
                lanes = slice(j * LANES, (j + 1) * LANES)
                conv = out[j * group : (j + 1) * group, :LANES]
                dgated = out[j * group : (j + 1) * group, LANES:]
                gq[rows, lanes] = (g[rows, lanes].astype(f32) * conv).astype(bf16)
                gk[rows, lanes] = (dgated * v[rows, lanes].astype(f32)).astype(bf16)
                gv[rows, lanes] = (dgated * k[rows, lanes].astype(f32)).astype(bf16)
        start(stores(step))
    for step in range(TOKEN_STEPS):
        wait(stores(step))


def finish(tok, key_in, value, grad_out):
    group = tok.shape[2]
    channels, length = key_in.shape
    swap = jnp.asarray(swap_table(group))
    return pl.pallas_call(
        finish_kernel,
        in_specs=[ANY] * 4 + [VMEM],
        out_specs=[ANY] * 3,
        out_shape=[jax.ShapeDtypeStruct((channels, length), bf16)] * 3,
        scratch_shapes=[pltpu.VMEM(tok.shape, bf16)]
        + [pltpu.VMEM(key_in.shape, bf16)] * 6
        + [pltpu.SemaphoreType.DMA((TOKEN_STEPS, 4)), pltpu.SemaphoreType.DMA((TOKEN_STEPS, 3))],
        compiler_params=params(0, 50 * 2**20),
        cost_estimate=pl.CostEstimate(
            flops=3 * channels * length, bytes_accessed=16 * channels * length, transcendentals=0
        ),
        name="finish",
    )(tok, key_in, value, grad_out, swap)


def turned(stage, turn_cos, turn_sin, rows, at):
    lanes = slice(at * LANES, (at + 1) * LANES)
    re, im = stage[:rows, lanes], stage[rows:, lanes]
    return jnp.concatenate([re * turn_cos + im * turn_sin, im * turn_cos - re * turn_sin], 1)


def filter_kernel(x_ref, w_ref, m_ref, tc_ref, ts_ref, out_ref, *, scale):
    pair, rows, _ = x_ref.shape
    x = jnp.concatenate([x_ref[i] for i in range(pair)], 1)
    high = x.astype(bf16)
    low = (x - high.astype(f32)).astype(bf16)
    stage = dot(w_ref[...], jnp.concatenate([high, high, low], 0))
    for i in range(pair):
        u = turned(stage, tc_ref[...], ts_ref[...], rows, i) * scale
        u_high = u.astype(bf16)
        u_low = (u - u_high.astype(f32)).astype(bf16)
        out_ref[i] = dot(jnp.concatenate([u_high, u_high, u_low], 1), m_ref[...])


def filter_spectrum(filt, t, scale):
    n, rows, _ = filt.shape
    pair = 2
    tables = [t["w3"], t["m3"], t["turn_cos"], t["turn_sin"]]
    return pl.pallas_call(
        functools.partial(filter_kernel, scale=scale),
        grid=(n // pair,),
        in_specs=[pl.BlockSpec((pair, rows, LANES), lambda i: (i, 0, 0))] + [whole(x) for x in tables],
        out_specs=pl.BlockSpec((pair, rows, 2 * LANES), lambda i: (i, 0, 0)),
        out_shape=jax.ShapeDtypeStruct((n, rows, 2 * LANES), f32),
        compiler_params=params(1),
        cost_estimate=pl.CostEstimate(
            flops=12 * n * rows * LANES * 512, bytes_accessed=16 * n * rows * LANES, transcendentals=0
        ),
        name="filter_spectrum",
    )(filt, *tables)


def back(spec, mi_ref, wi_ref, bc, bs, pair, rows):
    parts = mi_ref.shape[0] // (2 * LANES)
    stage = dot(jnp.concatenate([spec] * parts, 1), mi_ref[...])
    re_parts, im_parts = [], []
    for i in range(pair):
        re = stage[i * rows : (i + 1) * rows, :LANES]
        im = stage[i * rows : (i + 1) * rows, LANES:]
        re_parts.append((re * bc - im * bs).astype(bf16))
        im_parts.append((re * bs + im * bc).astype(bf16))
    v = jnp.concatenate([jnp.concatenate(re_parts, 1), jnp.concatenate(im_parts, 1)], 0)
    return dot(wi_ref[...], jnp.concatenate([v] * parts, 0))


def spectra_kernel(
    place_ref, x_ref, f_ref, w_hbm, m_hbm, tc_hbm, ts_hbm, mi_hbm, wi_hbm,
    stay_ref, leave0_ref, leave1_ref, conv_ref, dgated_ref,
    x_buf, f_buf, cross_buf, conv_buf, dgated_buf, w_ref, m_ref, tc_ref, ts_ref, mi_ref, wi_ref,
    in_sems, out_sems, leave_sems, table_sems, *, scale,
):
    n, _, group, cuts, _ = x_ref.shape
    pair = x_buf.shape[3]
    rows = n * cuts
    steps = group // pair
    _, _, ring, halves = cross_buf.shape[:4]

    def loads(step):
        at = pl.ds(step * pair, pair)
        return copies([(x_ref.at[:, :, at], x_buf.at[step]), (f_ref.at[at], f_buf.at[step])], in_sems, step)

    def stores(step):
        at = pl.ds(step * pair, pair)
        pairs = [(cross_buf.at[step, 0], stay_ref.at[step])]
        pairs += [(conv_buf.at[step], conv_ref.at[at]), (dgated_buf.at[step], dgated_ref.at[at])]
        return copies(pairs, out_sems, step)

    def leaving(step, leave_ref):
        return copies([(cross_buf.at[step, 1], leave_ref)], leave_sems, step)

    tables = copies(
        [(w_hbm, w_ref), (tc_hbm, tc_ref), (ts_hbm, ts_ref), (m_hbm, m_ref), (mi_hbm, mi_ref), (wi_hbm, wi_ref)],
        table_sems, 0,
    )
    start(loads(0))
    start(tables)
    for step in range(1, steps):
        start(loads(step))
    wait(tables)

    @pl.loop(0, steps)
    def _(step):
        wait(loads(step))
        x = jnp.concatenate(
            [x_buf[step, :, s, i].reshape(rows, LANES) for s in range(2) for i in range(pair)], 1
        )
        stage = dot(w_ref[...], x)
        u = jnp.concatenate(
            [turned(stage, tc_ref[...], ts_ref[...], rows, i).astype(bf16) for i in range(2 * pair)], 0
        )
        spec = dot(u, m_ref[...])
        half = pair * rows
        gr, gi = spec[:half, :LANES], spec[:half, LANES:]
        dr, di = spec[half:, :LANES], spec[half:, LANES:]
        cross = (jnp.concatenate([dr * gr + di * gi, di * gr - dr * gi], 1) * scale).astype(bf16)
        f = f_buf[step].reshape(half, 2 * LANES)
        fr, fi = f[:, :LANES], f[:, LANES:]
        conv_buf[step] = (
            jnp.concatenate([fr * gr - fi * gi, fr * gi + fi * gr], 1).astype(bf16).reshape(pair, rows, 2 * LANES)
        )
        dgated_buf[step] = (
            jnp.concatenate([dr * fr + di * fi, di * fr - dr * fi], 1).astype(bf16).reshape(pair, rows, 2 * LANES)
        )
        out = back(cross, mi_ref, wi_ref, tc_ref[...], ts_ref[...], pair, rows)
        for place in range(2 * ring * halves):
            at = place * cuts
            side, turns, half = order(place, 2 * ring * halves, step)
            to = (side ^ place_ref[step, 0], (turns - place_ref[step, 1]) & (ring - 1), half ^ place_ref[step, 2])
            for i in range(pair):
                cross_buf[step, *to, i] = out[at : at + cuts, i * LANES : (i + 1) * LANES].astype(bf16)
        start(stores(step))
        for one, leave_ref in enumerate((leave0_ref, leave1_ref)):

            @pl.when(step == one)
            def _():
                start(leaving(one, leave_ref))

    for step in range(steps):
        wait(stores(step))
    for one, leave_ref in enumerate((leave0_ref, leave1_ref)):
        wait(leaving(one, leave_ref))


def spectra(place, x, f, t, scale, n_tp):
    n, _, group, cuts, _ = x.shape
    rows = n * cuts
    pair = PAIR
    steps = group // pair
    tables = [t[k] for k in ("w", "m", "turn_cos", "turn_sin", CROSS_BACK[0], CROSS_BACK[1])]
    spec = (pair, rows, 2 * LANES)
    kept = (n_tp // 4, 2, pair, cuts, LANES)
    return pl.pallas_call(
        functools.partial(spectra_kernel, scale=scale),
        in_specs=[pl.BlockSpec(memory_space=pltpu.SMEM)] + [ANY] * (2 + len(tables)),
        out_specs=[ANY] * 5,
        out_shape=[
            jax.ShapeDtypeStruct((steps, *kept), bf16),
            jax.ShapeDtypeStruct(kept, bf16),
            jax.ShapeDtypeStruct(kept, bf16),
            jax.ShapeDtypeStruct((group, rows, 2 * LANES), bf16),
            jax.ShapeDtypeStruct((group, rows, 2 * LANES), bf16),
        ],
        scratch_shapes=[
            pltpu.VMEM((steps, n, 2, pair, cuts, LANES), bf16),
            pltpu.VMEM((steps, *spec), f32),
            pltpu.VMEM((steps, 2, *kept), bf16),
            pltpu.VMEM((steps, *spec), bf16),
            pltpu.VMEM((steps, *spec), bf16),
            *[pltpu.VMEM(v.shape, v.dtype) for v in tables],
            pltpu.SemaphoreType.DMA((steps, 2)),
            pltpu.SemaphoreType.DMA((steps, 3)),
            pltpu.SemaphoreType.DMA((steps, 1)),
            pltpu.SemaphoreType.DMA((1, len(tables))),
        ],
        compiler_params=params(0),
        cost_estimate=pl.CostEstimate(
            flops=24 * group * rows * LANES * 512, bytes_accessed=32 * group * rows * LANES, transcendentals=0
        ),
        name="spectra",
    )(place, x, f, *tables)


def signals_kernel(
    conv_ref, dgated_ref, mi_hbm, wi_hbm, tc_hbm, ts_hbm, out_ref,
    spec_buf, out_buf, mi_ref, wi_ref, tc_ref, ts_ref, in_sems, out_sems, table_sems,
):
    n, _, group, cuts, _ = out_ref.shape
    steps, _, pair, rows, _ = spec_buf.shape

    def loads(step):
        at = pl.ds(step * pair, pair)
        pairs = [(conv_ref.at[at], spec_buf.at[step, 0]), (dgated_ref.at[at], spec_buf.at[step, 1])]
        return copies(pairs, in_sems, step)

    def stores(step):
        return copies([(out_buf.at[step], out_ref.at[:, :, pl.ds(step * pair, pair)])], out_sems, step)

    tables = copies(
        [(mi_hbm, mi_ref), (tc_hbm, tc_ref), (ts_hbm, ts_ref), (wi_hbm, wi_ref)], table_sems, 0
    )
    start(loads(0))
    start(tables)
    for step in range(1, steps):
        start(loads(step))
    wait(tables)

    @pl.loop(0, steps)
    def _(step):
        wait(loads(step))
        both = spec_buf[step].reshape(2 * pair * rows, 2 * LANES)
        out = back(both, mi_ref, wi_ref, tc_ref[...], ts_ref[...], 2 * pair, rows).astype(bf16)
        for s in range(2):
            for i in range(pair):
                lanes = slice((s * pair + i) * LANES, (s * pair + i + 1) * LANES)
                out_buf[step, :, s, i] = out[:, lanes].reshape(n, cuts, LANES)
        start(stores(step))

    for step in range(steps):
        wait(stores(step))


def signals(conv, dgated, t, n):
    group, rows, _ = conv.shape
    cuts = rows // n
    pair = PAIR
    steps = group // pair
    tables = [t[k] for k in (*TOKEN_BACK, "turn_cos", "turn_sin")]
    return pl.pallas_call(
        signals_kernel,
        in_specs=[ANY] * (2 + len(tables)),
        out_specs=ANY,
        out_shape=jax.ShapeDtypeStruct((n, 2, group, cuts, LANES), bf16),
        scratch_shapes=[
            pltpu.VMEM((steps, 2, pair, rows, 2 * LANES), bf16),
            pltpu.VMEM((steps, n, 2, pair, cuts, LANES), bf16),
            *[pltpu.VMEM(v.shape, v.dtype) for v in tables],
            pltpu.SemaphoreType.DMA((steps, 2)),
            pltpu.SemaphoreType.DMA((steps, 1)),
            pltpu.SemaphoreType.DMA((1, len(tables))),
        ],
        compiler_params=params(0),
        cost_estimate=pl.CostEstimate(
            flops=16 * group * rows * LANES * 512, bytes_accessed=12 * group * rows * LANES, transcendentals=0
        ),
        name="signals",
    )(conv, dgated, *tables)


def order(place, n, shift):
    runs = n // 2
    half, z = place // runs, (place + shift) % runs
    return z % 2, z // 2, half


def sum_ring(stay, got, n):
    runs = n // 2
    steps = runs // 2
    total = stay[:, 0].astype(f32) + got[:, 0].astype(f32)
    for step in range(1, steps):
        share = (stay[:, step].astype(f32) + got[:, step].astype(f32)).astype(bf16)
        pairs = [(i, i // runs * runs + (i + 2 * step) % runs) for i in range(n)]
        total = total + lax.ppermute(share, "tp", pairs).astype(f32)
    return total


def body(query, key_in, value, grad_out, filter_raw, *, n_ctx, n_tp):
    group, length = filter_raw.shape
    rows = length // LANES
    root = 1.0 / math.sqrt(length)
    runs = n_tp // 2
    t = {k: jnp.asarray(v) for k, v in make_tables(length).items()}

    sent = gate(query, key_in, value, grad_out, n_ctx)
    got = lax.all_to_all(sent, "ctx", split_axis=0, concat_axis=0, tiled=True)
    filt = filter_spectrum(filter_raw.reshape(group, rows, LANES), t, root / length)
    me = lax.axis_index("tp")
    place = jnp.stack([jnp.stack(order(me, n_tp, shift)) for shift in range(2)]).astype(jnp.int32)
    stay, *leave, conv, dgated = spectra(place, got, filt, t, root / length, n_tp)
    near = []
    for shift, x in enumerate(leave):
        pairs = [(i, i // runs * runs + (((i + shift) % runs ^ 1) - shift) % runs) for i in range(n_tp)]
        near.append(lax.ppermute(x, "tp", pairs))
    made = signals(conv, dgated, t, n_ctx)
    made, *near = lax.optimization_barrier((made, *near))
    tok = lax.all_to_all(made, "ctx", split_axis=0, concat_axis=0, tiled=True)
    part = sum_ring(stay, jnp.stack(near), n_tp)
    far = lax.ppermute(part[:, 1], "tp", [(i, (i + runs) % n_tp) for i in range(n_tp)])
    grad_query, grad_key, grad_value = finish(tok, key_in, value, grad_out)
    mine = part[:, 0]
    mine, grad_query = lax.optimization_barrier((mine, grad_query))
    filter_grad = (mine + far).reshape(group, length // n_tp)
    return (grad_query, grad_key, grad_value, filter_grad)


def solution(mesh):
    placed = (P("tp", "ctx"), P("tp", "ctx"), P("tp", "ctx"), P("tp", "ctx"), P("ctx", None))
    return jax.shard_map(
        functools.partial(body, n_ctx=mesh.shape["ctx"], n_tp=mesh.shape["tp"]),
        mesh=mesh,
        in_specs=placed,
        out_specs=(P("tp", "ctx"), P("tp", "ctx"), P("tp", "ctx"), P("ctx", "tp")),
        check_vma=False,
    )
```

time: 137 us -> 102 us (0.74)
  the two profiles are of different devices: /device:TPU:4 before, /device:TPU:1 now
where the time goes in v1:
time: 102 us
  Pallas kernels  36.4 us (36%)
  waiting for transfers between devices  28.8 us (28%)
  starting transfers between devices  28.6 us (28%)
  other arithmetic  3.94 us (4%)
  local copies, waits for them, and re-layouts  3.2 us (3%)
    all_to_all x1, waiting for transfers between devices, body(): got = lax.all_to_all(sent, 'ctx', split_axis=0, concat_axis=0, tiled=True)  14.3 us
    pallas_call x1, Pallas kernels, spectra(): pl.pallas_call(functools.partial(spectra_kernel, scale=scale), in_specs=[...  11.3 us
    pallas_call x1, Pallas kernels, filter_spectrum(): pl.pallas_call(functools.partial(filter_kernel, scale=scale), grid=(n //...  10.8 us
    ppermute x3, waiting for transfers between devices, sum_ring(): total = total + lax.ppermute(share, 'tp', pairs).astype(f32)  7.56 us
    all_to_all x1, starting transfers between devices, body(): got = lax.all_to_all(sent, 'ctx', split_axis=0, concat_axis=0, tiled=True)  7.55 us
    all_to_all x1, waiting for transfers between devices, body(): tok = lax.all_to_all(made, 'ctx', split_axis=0, concat_axis=0, tiled=True)  6.96 us
    ppermute x3, starting transfers between devices, sum_ring(): total = total + lax.ppermute(share, 'tp', pairs).astype(f32)  6.55 us
    pallas_call x1, Pallas kernels, signals(): pl.pallas_call(signals_kernel, in_specs=[ANY] * (2 + len(tables)), out_sp...  6.1 us
  transfers between devices with their start and end apart: 8, of which 5 were waited for; matrix products, arithmetic and copies ran while one was open for 6% of the time, Pallas kernels for 20%

profile of v1, /device:TPU:1, one launch (start us, length us, event | category | flops | bytes accessed | tf_op | source)
XLA Modules:
  0.0 101.7 jit_solution(1335003662200906260)
XLA Ops:
  0.6 4.5 %gate.1 = bf16[16,2,16,16,128]{4,3,2,1,0:T(8,128)(2,1)} custom-call(bf16[256,2048]{1,0:T(8,128)(2,1)} %q_ref.1, bf16[256,2048]{1,0:T(8,128)(2,1)} %k_ref.3, bf16[256,2048]{1,0:T(8,128)(2,1)} %v_ref.3, bf16[256,2048]{1,0:T(8,128)(2,1)} %g_ref.3, bf16[256,256]{1,0:T(8,128)(2,1)} %constant.97.clone.swap_ref), custom_call_target="tpu_custom_call" | custom-call | flops 1048576 | bytes 6291456 | tf_op jit(solution)/shard_map/gate/pallas_call | solution.py:137
  5.1 7.5 %all-to-all-start = ((bf16[16,2,16,16,128]{4,3,2,1,0:T(8,128)(2,1)}), bf16[16,2,16,16,128]{4,3,2,1,0:T(8,128)(2,1)}, u32[]{:S(2)}, u32[]{:S(2)}) async-start(bf16[16,2,16,16,128]{4,3,2,1,0:T(8,128)(2,1)} %gate.1), calls=%async_computation | async-start | bytes 4194304 | tf_op jit(solution)/shard_map/all_to_all | solution.py:468
  12.7 1.8 %copy.32 = f32[2,8,256,128]{3,2,1,0:T(8,128)} copy(f32[2,8,256,128]{3,1,2,0:T(8,128)S(1)} %bitcast.52) | data formatting | bytes 4194304
  14.5 0.6 pad_add_fusion.place_ref
  15.1 10.8 %filter_spectrum.1.f_ref = f32[16,256,256]{2,1,0:T(8,128)} custom-call(f32[16,256,128]{2,1,0:T(8,128)} %bitcast.53, bf16[512,768]{1,0:T(8,128)(2,1)} %constant.87.clone.w_ref, bf16[768,256]{1,0:T(8,128)(2,1)} %constant.88.clone.m_ref, f32[256,128]{1,0:T(8,128)} %constant.95.clone.tc_ref.tc_hbm, f32[256,128]{1,0:T(8,128)} %constant.96.clone.ts_ref.ts_hbm), custom_call_target="tpu_custom_call" | custom-call | flops 3221225472 | bytes 8388608 | tf_op jit(solution)/shard_map/filter_spectrum/pallas_call | solution.py:233
  25.9 14.3 %all-to-all-done.x_ref = bf16[16,2,16,16,128]{4,3,2,1,0:T(8,128)(2,1)} async-done(((bf16[16,2,16,16,128]{4,3,2,1,0:T(8,128)(2,1)}), bf16[16,2,16,16,128]{4,3,2,1,0:T(8,128)(2,1)}, u32[]{:S(2)}, u32[]{:S(2)}) %all-to-all-start) | async-done | bytes 2097184 | tf_op jit(solution)/shard_map/all_to_all | solution.py:468
  40.2 11.3 %spectra.1 = (bf16[2,4,2,8,16,128]{5,4,3,2,1,0:T(8,128)(2,1)}, bf16[4,2,8,16,128]{4,3,2,1,0:T(8,128)(2,1)}, bf16[4,2,8,16,128]{4,3,2,1,0:T(8,128)(2,1)}, bf16[16...) custom-call(s32[2,3]{1,0:T(2,128)} %pad_add_fusion.place_ref, bf16[16,2,16,16,128]{4,3,2,1,0:T(8,128)(2,1)} %all-to-all-done.x_ref, ...), custom_call_target="tpu_custom_call" | custom-call | flops 6442450944 | bytes 16777216 | tf_op jit(solution)/shard_map/spectra/pallas_call | solution.py:346
  51.6 1.3 %collective-permute-start = (bf16[4,2,8,16,128]{4,3,2,1,0:T(8,128)(2,1)}, bf16[4,2,8,16,128]{4,3,2,1,0:T(8,128)(2,1)S(1)}, u32[]{:S(2)}, u32[]{:S(2)}) collective-permute-start(bf16[4,2,8,16,128]{4,3,2,1,0:T(8,128)(2,1)} %get-tuple-element.20), channel_id=1, source_target_pairs={{0,1},{1,0},{2,3},{3,2},{4,5},{5,4},{6,7},{7,6},{8,9},{9,8},{10,11... | collective-permute-start | bytes 786440 | tf_op jit(solution)/shard_map/ppermute | solution.py:476
  52.9 4.7 %collective-permute-start.1 = (bf16[4,2,8,16,128]{4,3,2,1,0:T(8,128)(2,1)}, bf16[4,2,8,16,128]{4,3,2,1,0:T(8,128)(2,1)}, u32[]{:S(2)}, u32[]{:S(2)}) collective-permute-start(bf16[4,2,8,16,128]{4,3,2,1,0:T(8,128)(2,1)} %get-tuple-element.21), channel_id=1, source_target_pairs={{0,7},{1,2},{2,1},{3,4},{4,3},{5,6},{6,5},{7,0},{8,15},{9,10},{10,... | collective-permute-start | bytes 786440 | tf_op jit(solution)/shard_map/ppermute | solution.py:476
  57.5 6.1 %signals.1 = bf16[16,2,16,16,128]{4,3,2,1,0:T(8,128)(2,1)} custom-call(bf16[16,256,256]{2,1,0:T(8,128)(2,1)} %get-tuple-element.18.conv_ref, bf16[16,256,256]{2,1,0:T(8,128)(2,1)} %get-tuple-element.19.dgated_ref, bf16[256,256]{1,0:T(8,128)(2,1)} %constant.91.clone.mi_hbm, bf16[256,512]{1,0:T(8,128)(2,1)} %constant.92.clone.wi_hbm, ...), custom_call_target="tpu_custom_call" | custom-call | flops 4294967296 | bytes 6291456 | tf_op jit(solution)/shard_map/signals/pallas_call | solution.py:422
  63.7 5.9 %all-to-all-start.1 = ((bf16[16,2,16,16,128]{4,3,2,1,0:T(8,128)(2,1)}), bf16[16,2,16,16,128]{4,3,2,1,0:T(8,128)(2,1)}, u32[]{:S(2)}, u32[]{:S(2)}) async-start(bf16[16,2,16,16,128]{4,3,2,1,0:T(8,128)(2,1)} %signals.1), calls=%async_computation.1 | async-start | bytes 4194304 | tf_op jit(solution)/shard_map/all_to_all | solution.py:479
  69.6 1.1 %fusion.4 = bf16[2,2,8,16,128]{4,3,2,1,0:T(8,128)(2,1)S(1)} fusion(bf16[1,4,2,8,16,128]{5,4,3,2,1,0:T(8,128)(2,1)} %bitcast.8, bf16[1,4,2,8,16,128]{5,4,3,2,1,0:T(8,128)(2,1)S(1)} %bitcast.49, bf16[2,4,2,8,16,128]{5,4,3,2,1,0:T(8,128)(2,1)} %get-tuple-element.17), kind=kLoop, calls=%fused_computation.14 | loop fusion | flops 327680 | bytes 786432 | tf_op jit(solution)/shard_map/convert_element_type | solution.py:454
  70.7 2.0 %collective-permute-start.4 = (bf16[2,2,8,16,128]{4,3,2,1,0:T(8,128)(2,1)S(1)}, bf16[2,2,8,16,128]{4,3,2,1,0:T(8,128)(2,1)S(1)}, u32[]{:S(2)}, u32[]{:S(2)}) collective-permute-start(bf16[2,2,8,16,128]{4,3,2,1,0:T(8,128)(2,1)S(1)} %fusion.4), channel_id=1, source_target_pairs={{0,6},{1,7},{2,0},{3,1},{4,2},{5,3},{6,4},{7,5},{8,14},{9,15},{10,... | collective-permute-start | bytes 393224 | tf_op jit(solution)/shard_map/ppermute | solution.py:456
  72.7 1.1 %fusion.2 = (bf16[2,2,8,16,128]{4,3,2,1,0:T(8,128)(2,1)S(1)}, bf16[2,2,8,16,128]{4,3,2,1,0:T(8,128)(2,1)S(1)}) fusion(bf16[1,4,2,8,16,128]{5,4,3,2,1,0:T(8,128)(2,1)S(1)} %bitcast.50, bf16[1,4,2,8,16,128]{5,4,3,2,1,0:T(8,128)(2,1)} %bitcast.8, bf16[2,4,2,8,16,128]{5,4,3,2,1,0:T(8,128)(2,1)} %get-tuple-element.17), kind=kLoop, calls=%fused_computation.12 | loop fusion | flops 1048576 | bytes 1048576 | tf_op jit(solution)/shard_map/convert_element_type | solution.py:454
  74.4 4.0 %collective-permute-start.3 = (bf16[2,2,8,16,128]{4,3,2,1,0:T(8,128)(2,1)S(1)}, bf16[2,2,8,16,128]{4,3,2,1,0:T(8,128)(2,1)S(1)}, u32[]{:S(2)}, u32[]{:S(2)}) collective-permute-start(bf16[2,2,8,16,128]{4,3,2,1,0:T(8,128)(2,1)S(1)} %get-tuple-element.31), channel_id=1, source_target_pairs={{0,4},{1,5},{2,6},{3,7},{4,0},{5,1},{6,2},{7,3},{8,12},{9,13},{10,... | collective-permute-start | bytes 393224 | tf_op jit(solution)/shard_map/ppermute | solution.py:456
  78.4 1.0 collective-permute-done.4
  79.4 4.1 %collective-permute-done.2 = bf16[2,2,8,16,128]{4,3,2,1,0:T(8,128)(2,1)S(1)} collective-permute-done((bf16[2,2,8,16,128]{4,3,2,1,0:T(8,128)(2,1)S(1)}, bf16[2,2,8,16,128]{4,3,2,1,0:T(8,128)(2,1)S(1)}, u32[]{:S(2)}, u32[]{:S(2)}) %collective-permute-start.2) | collective-permute-done | bytes 131104 | tf_op jit(solution)/shard_map/ppermute | solution.py:456
  83.4 2.5 %collective-permute-done.3 = bf16[2,2,8,16,128]{4,3,2,1,0:T(8,128)(2,1)S(1)} collective-permute-done((bf16[2,2,8,16,128]{4,3,2,1,0:T(8,128)(2,1)S(1)}, bf16[2,2,8,16,128]{4,3,2,1,0:T(8,128)(2,1)S(1)}, u32[]{:S(2)}, u32[]{:S(2)}) %collective-permute-start.3) | collective-permute-done | bytes 131104 | tf_op jit(solution)/shard_map/ppermute | solution.py:456
  86.0 1.0 %fusion.1 = f32[2,2,8,16,128]{4,3,2,1,0:T(8,128)S(1)} fusion(bf16[2,2,8,16,128]{4,3,2,1,0:T(8,128)(2,1)S(1)} %collective-permute-done.4, bf16[2,2,8,16,128]{4,3,2,1,0:T(8,128)(2,1)S(1)} %collective-permute-done.3, bf16[2,2,8,16,128]{4,3,2,1,0:T(8,128)(2,1)S(1)} %collective-permute-done.2, bf16[1,4,2,8,16,128]{5,4,3,2,1,0:T(8,128)(2,1)S(1)} %bitcast.51, ...), kind=kLoop, calls=%fused_computation.8 | loop fusion | flops 851968 | bytes 1310720 | tf_op jit(solution)/shard_map/add | solution.py:456
  87.0 0.7 slice_bitcast_fusion
  87.7 2.6 %collective-permute-start.5 = (f32[2,8,16,128]{3,2,1,0:T(8,128)}, f32[2,8,16,128]{3,2,1,0:T(8,128)S(1)}, u32[]{:S(2)}, u32[]{:S(2)}) collective-permute-start(f32[2,8,16,128]{3,2,1,0:T(8,128)} %get-tuple-element.32), channel_id=1, source_target_pairs={{0,8},{1,9},{2,10},{3,11},{4,12},{5,13},{6,14},{7,15},{8,0},{9,1},... | collective-permute-start | bytes 393224 | tf_op jit(solution)/shard_map/ppermute | solution.py:481
  90.3 7.0 %all-to-all-done.1.tok_ref = bf16[16,2,16,16,128]{4,3,2,1,0:T(8,128)(2,1)} async-done(((bf16[16,2,16,16,128]{4,3,2,1,0:T(8,128)(2,1)}), bf16[16,2,16,16,128]{4,3,2,1,0:T(8,128)(2,1)}, u32[]{:S(2)}, u32[]{:S(2)}) %all-to-all-start.1) | async-done | bytes 2097184 | tf_op jit(solution)/shard_map/all_to_all | solution.py:479
  97.3 3.6 %finish.1 = (bf16[256,2048]{1,0:T(8,128)(2,1)}, bf16[256,2048]{1,0:T(8,128)(2,1)}, bf16[256,2048]{1,0:T(8,128)(2,1)}) custom-call(bf16[16,2,16,16,128]{4,3,2,1,0:T(8,128)(2,1)} %all-to-all-done.1.tok_ref, bf16[256,2048]{1,0:T(8,128)(2,1)S(1)} %copy-done, bf16[256,2048]{1,0:T(8,128)(2,1)S(1)} %copy-done.1, bf16[256,2048]{1,0:T(8,128)(2,1)S(1)} %copy-done.2, ...), custom_call_target="tpu_custom_call" | custom-call | flops 1572864 | bytes 8388608 | tf_op jit(solution)/shard_map/finish/pallas_call | solution.py:194
  101.0 0.7 copy.39
  (16 shorter events, 0.7 us)
Async XLA Ops:
  5.1 7.6 %copy-start.4 = (f32[16,32768]{1,0:T(8,128)S(1)}, f32[16,32768]{1,0:T(8,128)}, u32[]{:S(2)}) copy-start(f32[16,32768]{1,0:T(8,128)} %param.21) | copy-start | bytes 6291460
  5.1 35.1 %all-to-all-start = ((bf16[16,2,16,16,128]{4,3,2,1,0:T(8,128)(2,1)}), bf16[16,2,16,16,128]{4,3,2,1,0:T(8,128)(2,1)}, u32[]{:S(2)}, u32[]{:S(2)}) async-start(bf16[16,2,16,16,128]{4,3,2,1,0:T(8,128)(2,1)} %gate.1), calls=%async_computation | async-start | bytes 4194304 | tf_op jit(solution)/shard_map/all_to_all | solution.py:468
  51.6 12.1 %collective-permute-start = (bf16[4,2,8,16,128]{4,3,2,1,0:T(8,128)(2,1)}, bf16[4,2,8,16,128]{4,3,2,1,0:T(8,128)(2,1)S(1)}, u32[]{:S(2)}, u32[]{:S(2)}) collective-permute-start(bf16[4,2,8,16,128]{4,3,2,1,0:T(8,128)(2,1)} %get-tuple-element.20), channel_id=1, source_target_pairs={{0,1},{1,0},{2,3},{3,2},{4,5},{5,4},{6,7},{7,6},{8,9},{9,8},{10,11... | collective-permute-start | bytes 786440 | tf_op jit(solution)/shard_map/ppermute | solution.py:476
  52.9 10.8 %collective-permute-start.1 = (bf16[4,2,8,16,128]{4,3,2,1,0:T(8,128)(2,1)}, bf16[4,2,8,16,128]{4,3,2,1,0:T(8,128)(2,1)}, u32[]{:S(2)}, u32[]{:S(2)}) collective-permute-start(bf16[4,2,8,16,128]{4,3,2,1,0:T(8,128)(2,1)} %get-tuple-element.21), channel_id=1, source_target_pairs={{0,7},{1,2},{2,1},{3,4},{4,3},{5,6},{6,5},{7,0},{8,15},{9,10},{10,... | collective-permute-start | bytes 786440 | tf_op jit(solution)/shard_map/ppermute | solution.py:476
  63.7 33.6 %all-to-all-start.1 = ((bf16[16,2,16,16,128]{4,3,2,1,0:T(8,128)(2,1)}), bf16[16,2,16,16,128]{4,3,2,1,0:T(8,128)(2,1)}, u32[]{:S(2)}, u32[]{:S(2)}) async-start(bf16[16,2,16,16,128]{4,3,2,1,0:T(8,128)(2,1)} %signals.1), calls=%async_computation.1 | async-start | bytes 4194304 | tf_op jit(solution)/shard_map/all_to_all | solution.py:479
  69.6 27.7 %copy-start = (bf16[256,2048]{1,0:T(8,128)(2,1)S(1)}, bf16[256,2048]{1,0:T(8,128)(2,1)}, u32[]{:S(2)}) copy-start(bf16[256,2048]{1,0:T(8,128)(2,1)} %k_ref.3) | copy-start | bytes 3145732
  69.6 27.7 %copy-start.1 = (bf16[256,2048]{1,0:T(8,128)(2,1)S(1)}, bf16[256,2048]{1,0:T(8,128)(2,1)}, u32[]{:S(2)}) copy-start(bf16[256,2048]{1,0:T(8,128)(2,1)} %v_ref.3) | copy-start | bytes 3145732
  69.6 27.7 %copy-start.2 = (bf16[256,2048]{1,0:T(8,128)(2,1)S(1)}, bf16[256,2048]{1,0:T(8,128)(2,1)}, u32[]{:S(2)}) copy-start(bf16[256,2048]{1,0:T(8,128)(2,1)} %g_ref.3) | copy-start | bytes 3145732
  69.6 27.7 %copy-start.3 = (bf16[256,256]{1,0:T(8,128)(2,1)S(1)}, bf16[256,256]{1,0:T(8,128)(2,1)}, u32[]{:S(2)}) copy-start(bf16[256,256]{1,0:T(8,128)(2,1)} %constant.97.clone.swap_ref) | copy-start | bytes 393220
  70.7 8.6 %collective-permute-start.4 = (bf16[2,2,8,16,128]{4,3,2,1,0:T(8,128)(2,1)S(1)}, bf16[2,2,8,16,128]{4,3,2,1,0:T(8,128)(2,1)S(1)}, u32[]{:S(2)}, u32[]{:S(2)}) collective-permute-start(bf16[2,2,8,16,128]{4,3,2,1,0:T(8,128)(2,1)S(1)} %fusion.4), channel_id=1, source_target_pairs={{0,6},{1,7},{2,0},{3,1},{4,2},{5,3},{6,4},{7,5},{8,14},{9,15},{10,... | collective-permute-start | bytes 393224 | tf_op jit(solution)/shard_map/ppermute | solution.py:456
  73.9 9.6 %collective-permute-start.2 = (bf16[2,2,8,16,128]{4,3,2,1,0:T(8,128)(2,1)S(1)}, bf16[2,2,8,16,128]{4,3,2,1,0:T(8,128)(2,1)S(1)}, u32[]{:S(2)}, u32[]{:S(2)}) collective-permute-start(bf16[2,2,8,16,128]{4,3,2,1,0:T(8,128)(2,1)S(1)} %get-tuple-element.30), channel_id=1, source_target_pairs={{0,2},{1,3},{2,4},{3,5},{4,6},{5,7},{6,0},{7,1},{8,10},{9,11},{10,... | collective-permute-start | bytes 393224 | tf_op jit(solution)/shard_map/ppermute | solution.py:456
  74.4 11.6 %collective-permute-start.3 = (bf16[2,2,8,16,128]{4,3,2,1,0:T(8,128)(2,1)S(1)}, bf16[2,2,8,16,128]{4,3,2,1,0:T(8,128)(2,1)S(1)}, u32[]{:S(2)}, u32[]{:S(2)}) collective-permute-start(bf16[2,2,8,16,128]{4,3,2,1,0:T(8,128)(2,1)S(1)} %get-tuple-element.31), channel_id=1, source_target_pairs={{0,4},{1,5},{2,6},{3,7},{4,0},{5,1},{6,2},{7,3},{8,12},{9,13},{10,... | collective-permute-start | bytes 393224 | tf_op jit(solution)/shard_map/ppermute | solution.py:456
  87.7 13.2 %collective-permute-start.5 = (f32[2,8,16,128]{3,2,1,0:T(8,128)}, f32[2,8,16,128]{3,2,1,0:T(8,128)S(1)}, u32[]{:S(2)}, u32[]{:S(2)}) collective-permute-start(f32[2,8,16,128]{3,2,1,0:T(8,128)} %get-tuple-element.32), channel_id=1, source_target_pairs={{0,8},{1,9},{2,10},{3,11},{4,12},{5,13},{6,14},{7,15},{8,0},{9,1},... | collective-permute-start | bytes 393224 | tf_op jit(solution)/shard_map/ppermute | solution.py:481

commit v2 on v1

v2 whole, which is shorter than its diff:
```python
import functools
import math

import jax
import jax.numpy as jnp
import ml_dtypes
import numpy as np
from jax import lax
from jax.experimental import pallas as pl
from jax.experimental.pallas import tpu as pltpu
from jax.sharding import PartitionSpec as P

LANES = 128
VMEM_LIMIT = 56 * 2**20
SPLIT = 2
TOKEN_STEPS = 4
FILTERS = 4
FILTER_PAIR = 4
CROSS_BACK = ("mi2", "wi2")
TOKEN_BACK = ("mi", "wi")
f32 = jnp.float32
bf16 = jnp.bfloat16


def split_parts(table):
    high = table.astype(np.float32).astype(ml_dtypes.bfloat16)
    low = (table - high.astype(np.float64)).astype(np.float32).astype(ml_dtypes.bfloat16)
    return high, low


@functools.lru_cache(maxsize=None)
def make_tables(length):
    rows = length // LANES
    total = 2 * length
    a = np.arange(rows, dtype=np.float64)
    k1 = np.arange(rows, dtype=np.float64) + 0.5
    b = np.arange(LANES, dtype=np.float64)
    first = 2.0 * np.pi * np.outer(k1, a) / (2 * rows)
    turn = 2.0 * np.pi * np.outer(k1, b) / total
    second = 2.0 * np.pi * np.outer(b, b) / LANES
    c2, s2 = np.cos(second), np.sin(second)
    w_high, w_low = split_parts(np.concatenate([np.cos(first), -np.sin(first)], 0))
    m_high, m_low = split_parts(np.block([[c2, -s2], [s2, c2]]))
    mi_high, mi_low = split_parts(np.block([[c2, s2], [-s2, c2]]))
    wi_high, wi_low = split_parts(np.concatenate([np.cos(first).T, -np.sin(first).T], 1))
    return dict(
        w3=np.concatenate([w_high, w_low, w_high], 1),
        m3=np.concatenate([m_high, m_low, m_high], 0),
        w=w_high,
        m=m_high,
        mi=mi_high,
        wi=wi_high,
        mi2=np.concatenate([mi_high, mi_low], 0),
        wi2=np.concatenate([wi_high, wi_low], 1),
        turn_cos=np.cos(turn).astype(np.float32),
        turn_sin=np.sin(turn).astype(np.float32),
    )


def dot(x, y):
    return jnp.dot(x, y, preferred_element_type=f32)


def whole(table):
    return pl.BlockSpec(table.shape, lambda *_: (0,) * table.ndim)


def params(grid_rank, limit=VMEM_LIMIT):
    return pltpu.CompilerParams(
        dimension_semantics=("arbitrary",) * grid_rank if grid_rank else None,
        vmem_limit_bytes=limit,
    )


def swap_table(size):
    index = np.arange(size * size).reshape(size, size)
    table = np.zeros((size * size, size * size), np.float32)
    table[index.T.reshape(-1), index.reshape(-1)] = 1.0
    return table.astype(ml_dtypes.bfloat16)


def copies(pairs, sems, at):
    return [pltpu.make_async_copy(src, dst, sems.at[at, i]) for i, (src, dst) in enumerate(pairs)]


def start(moves):
    for move in moves:
        move.start()


def wait(moves):
    for move in moves:
        move.wait()


ANY = pl.BlockSpec(memory_space=pl.ANY)
VMEM = pl.BlockSpec(memory_space=pltpu.VMEM)


def gate_kernel(q_ref, k_ref, v_ref, g_ref, swap_ref, out_ref, q, k, v, g, o, in_sems, out_sems):
    n, split, _, kept, cuts, _ = out_ref.shape
    group = split * kept
    runs = n // TOKEN_STEPS

    def loads(step):
        rows = pl.ds(step * runs * group, runs * group)
        pairs = [(r.at[rows], s.at[rows]) for r, s in ((k_ref, k), (v_ref, v), (g_ref, g), (q_ref, q))]
        return copies(pairs, in_sems, step)

    def stores(step):
        at = pl.ds(step * runs, runs)
        return copies([(o.at[at], out_ref.at[at])], out_sems, step)

    for step in range(TOKEN_STEPS):
        start(loads(step))
    for step in range(TOKEN_STEPS):
        wait(loads(step))
        for run in range(step * runs, (step + 1) * runs):
            rows = slice(run * group, (run + 1) * group)

            def product(x, y):
                z = (x[rows, :].astype(f32) * y[rows, :].astype(f32)).astype(bf16)
                return jnp.concatenate([z[:, j * LANES : (j + 1) * LANES] for j in range(cuts)], 0)

            both = jnp.concatenate([product(k, v), product(g, q)], 1)
            out = dot(swap_ref[...], both).astype(bf16)
            for s in range(2):
                o[run, :, s] = out[:, s * LANES : (s + 1) * LANES].reshape(split, kept, cuts, LANES)
        start(stores(step))
    for step in range(TOKEN_STEPS):
        wait(stores(step))


def gate(query, key_in, value, grad_out, n):
    channels, length = query.shape
    group = channels // n
    cuts = length // LANES
    swap = jnp.asarray(swap_table(group))
    sent = (n, SPLIT, 2, group // SPLIT, cuts, LANES)
    return pl.pallas_call(
        gate_kernel,
        in_specs=[ANY] * 4 + [VMEM],
        out_specs=ANY,
        out_shape=jax.ShapeDtypeStruct(sent, bf16),
        scratch_shapes=[pltpu.VMEM(query.shape, bf16)] * 4
        + [pltpu.VMEM(sent, bf16), pltpu.SemaphoreType.DMA((TOKEN_STEPS, 4)), pltpu.SemaphoreType.DMA((TOKEN_STEPS, 1))],
        compiler_params=params(0),
        cost_estimate=pl.CostEstimate(
            flops=2 * channels * length, bytes_accessed=12 * channels * length, transcendentals=0
        ),
        name="gate",
    )(query, key_in, value, grad_out, swap)


def finish_kernel(
    tok_ref, k_ref, v_ref, g_ref, swap_ref, gq_ref, gk_ref, gv_ref, tok, k, v, g, gq, gk, gv, in_sems, out_sems
):
    n, split, _, kept, cuts, _ = tok_ref.shape
    group = split * kept
    runs = n // TOKEN_STEPS

    def loads(step):
        rows = pl.ds(step * runs * group, runs * group)
        at = pl.ds(step * runs, runs)
        pairs = [(tok_ref.at[at], tok.at[at])]
        pairs += [(r.at[rows], s.at[rows]) for r, s in ((g_ref, g), (v_ref, v), (k_ref, k))]
        return copies(pairs, in_sems, step)

    def stores(step):
        rows = pl.ds(step * runs * group, runs * group)
        pairs = [(s.at[rows], r.at[rows]) for r, s in ((gq_ref, gq), (gk_ref, gk), (gv_ref, gv))]
        return copies(pairs, out_sems, step)

    for step in range(TOKEN_STEPS):
        start(loads(step))
    for step in range(TOKEN_STEPS):
        wait(loads(step))
        for run in range(step * runs, (step + 1) * runs):
            rows = slice(run * group, (run + 1) * group)
            both = jnp.concatenate([tok[run, :, s].reshape(group * cuts, LANES) for s in range(2)], 1)
            out = dot(swap_ref[...], both)
            for j in range(cuts):
                lanes = slice(j * LANES, (j + 1) * LANES)
                conv = out[j * group : (j + 1) * group, :LANES]
                dgated = out[j * group : (j + 1) * group, LANES:]
                gq[rows, lanes] = (g[rows, lanes].astype(f32) * conv).astype(bf16)
                gk[rows, lanes] = (dgated * v[rows, lanes].astype(f32)).astype(bf16)
                gv[rows, lanes] = (dgated * k[rows, lanes].astype(f32)).astype(bf16)
        start(stores(step))
    for step in range(TOKEN_STEPS):
        wait(stores(step))


def finish(tok, key_in, value, grad_out):
    group = tok.shape[1] * tok.shape[3]
    channels, length = key_in.shape
    swap = jnp.asarray(swap_table(group))
    return pl.pallas_call(
        finish_kernel,
        in_specs=[ANY] * 4 + [VMEM],
        out_specs=[ANY] * 3,
        out_shape=[jax.ShapeDtypeStruct((channels, length), bf16)] * 3,
        scratch_shapes=[pltpu.VMEM(tok.shape, bf16)]
        + [pltpu.VMEM(key_in.shape, bf16)] * 6
        + [pltpu.SemaphoreType.DMA((TOKEN_STEPS, 4)), pltpu.SemaphoreType.DMA((TOKEN_STEPS, 3))],
        compiler_params=params(0, 52 * 2**20),
        cost_estimate=pl.CostEstimate(
            flops=3 * channels * length, bytes_accessed=16 * channels * length, transcendentals=0
        ),
        name="finish",
    )(tok, key_in, value, grad_out, swap)


def turned(stage, turn_cos, turn_sin, rows, at):
    lanes = slice(at * LANES, (at + 1) * LANES)
    re, im = stage[:rows, lanes], stage[rows:, lanes]
    return jnp.concatenate([re * turn_cos + im * turn_sin, im * turn_cos - re * turn_sin], 1)


def filter_kernel(x_ref, w_ref, m_ref, tc_ref, ts_ref, out_ref, *, scale):
    pair, rows, _ = x_ref.shape
    x = jnp.concatenate([x_ref[i] for i in range(pair)], 1)
    high = x.astype(bf16)
    low = (x - high.astype(f32)).astype(bf16)
    stage = dot(w_ref[...], jnp.concatenate([high, high, low], 0))
    for i in range(pair):
        u = turned(stage, tc_ref[...], ts_ref[...], rows, i) * scale
        u_high = u.astype(bf16)
        u_low = (u - u_high.astype(f32)).astype(bf16)
        out_ref[i] = dot(jnp.concatenate([u_high, u_high, u_low], 1), m_ref[...])


def filter_spectrum(filt, t, scale):
    n, rows, _ = filt.shape
    pair = FILTER_PAIR
    tables = [t["w3"], t["m3"], t["turn_cos"], t["turn_sin"]]
    return pl.pallas_call(
        functools.partial(filter_kernel, scale=scale),
        grid=(n // pair,),
        in_specs=[pl.BlockSpec((pair, rows, LANES), lambda i: (i, 0, 0))] + [whole(x) for x in tables],
        out_specs=pl.BlockSpec((pair, rows, 2 * LANES), lambda i: (i, 0, 0)),
        out_shape=jax.ShapeDtypeStruct((n, rows, 2 * LANES), f32),
        compiler_params=params(1),
        cost_estimate=pl.CostEstimate(
            flops=12 * n * rows * LANES * 512, bytes_accessed=16 * n * rows * LANES, transcendentals=0
        ),
        name="filter_spectrum",
    )(filt, *tables)


def back(spec, mi_ref, wi_ref, bc, bs, pair, rows):
    parts = mi_ref.shape[0] // (2 * LANES)
    stage = dot(jnp.concatenate([spec] * parts, 1), mi_ref[...])
    re_parts, im_parts = [], []
    for i in range(pair):
        re = stage[i * rows : (i + 1) * rows, :LANES]
        im = stage[i * rows : (i + 1) * rows, LANES:]
        re_parts.append((re * bc - im * bs).astype(bf16))
        im_parts.append((re * bs + im * bc).astype(bf16))
    v = jnp.concatenate([jnp.concatenate(re_parts, 1), jnp.concatenate(im_parts, 1)], 0)
    return dot(wi_ref[...], jnp.concatenate([v] * parts, 0))


def product(ar, ai, br, bi):
    return jnp.concatenate([ar * br - ai * bi, ar * bi + ai * br], 1)


def channels_kernel(
    x_ref, f_ref, w_hbm, m_hbm, tc_hbm, ts_hbm, mi_hbm, wi_hbm, cross_ref, out_ref,
    x_buf, f_buf, cross_buf, out_buf, w_ref, m_ref, tc_ref, ts_ref, mi_ref, wi_ref,
    in_sems, out_sems, table_sems, *, scale,
):
    n, split, _, kept, cuts, _ = x_ref.shape
    steps, count = f_buf.shape[:2]
    rows = n * cuts

    def loads(step):
        at = pl.ds(step * count, count)
        return copies([(x_ref.at[:, :, :, at], x_buf.at[step]), (f_ref.at[at], f_buf.at[step])], in_sems, step)

    def stores(step):
        at = pl.ds(step * count, count)
        return copies(
            [(cross_buf.at[step], cross_ref.at[at]), (out_buf.at[step], out_ref.at[:, :, :, at])], out_sems, step
        )

    tables = copies(
        [(w_hbm, w_ref), (tc_hbm, tc_ref), (ts_hbm, ts_ref), (m_hbm, m_ref), (mi_hbm, mi_ref), (wi_hbm, wi_ref)],
        table_sems, 0,
    )
    start(loads(0))
    start(tables)
    for step in range(1, steps):
        start(loads(step))
    wait(tables)

    @pl.loop(0, steps)
    def _(step):
        wait(loads(step))
        places = [(s, m, i) for s in range(2) for m in range(split) for i in range(count)]
        x = jnp.concatenate([x_buf[step, :, m, s, i].reshape(rows, LANES) for s, m, i in places], 1)
        stage = dot(w_ref[...], x)
        u = jnp.concatenate(
            [turned(stage, tc_ref[...], ts_ref[...], rows, i).astype(bf16) for i in range(len(places))], 0
        )
        spec = dot(u, m_ref[...])
        block = count * rows
        half = split * block
        f = f_buf[step].reshape(block, 2 * LANES)
        fr, fi = f[:, :LANES], f[:, LANES:]
        convs, dgateds, cross = [], [], 0.0
        for m in range(split):
            at = m * block
            gr, gi = spec[at : at + block, :LANES], spec[at : at + block, LANES:]
            dr, di = spec[half + at : half + at + block, :LANES], spec[half + at : half + at + block, LANES:]
            convs.append(product(fr, fi, gr, gi).astype(bf16))
            dgateds.append(product(fr, -fi, dr, di).astype(bf16))
            cross = cross + product(gr, -gi, dr, di)
        cross_buf[step] = (cross * scale).astype(bf16).reshape(count, rows, 2 * LANES)
        made = back(jnp.concatenate(convs + dgateds, 0), mi_ref, wi_ref, tc_ref[...], ts_ref[...], len(places), rows)
        made = made.astype(bf16)
        for at, (s, m, i) in enumerate(places):
            out_buf[step, :, m, s, i] = made[:, at * LANES : (at + 1) * LANES].reshape(n, cuts, LANES)
        start(stores(step))

    for step in range(steps):
        wait(stores(step))


def channels(x, f, t, scale):
    n, split, _, kept, cuts, _ = x.shape
    rows = n * cuts
    count = FILTERS
    steps = kept // count
    tables = [t[k] for k in ("w", "m", "turn_cos", "turn_sin", *TOKEN_BACK)]
    spec = (count, rows, 2 * LANES)
    block = (steps, n, split, 2, count, cuts, LANES)
    return pl.pallas_call(
        functools.partial(channels_kernel, scale=scale),
        in_specs=[ANY] * (2 + len(tables)),
        out_specs=[ANY] * 2,
        out_shape=[jax.ShapeDtypeStruct((kept, rows, 2 * LANES), bf16), jax.ShapeDtypeStruct(x.shape, bf16)],
        scratch_shapes=[
            pltpu.VMEM(block, bf16),
            pltpu.VMEM((steps, *spec), f32),
            pltpu.VMEM((steps, *spec), bf16),
            pltpu.VMEM(block, bf16),
            *[pltpu.VMEM(v.shape, v.dtype) for v in tables],
            pltpu.SemaphoreType.DMA((steps, 2)),
            pltpu.SemaphoreType.DMA((steps, 2)),
            pltpu.SemaphoreType.DMA((1, len(tables))),
        ],
        compiler_params=params(0),
        cost_estimate=pl.CostEstimate(
            flops=24 * split * kept * rows * LANES * 512, bytes_accessed=8 * x.size, transcendentals=0
        ),
        name="channels",
    )(x, f, *tables)


def lags_kernel(place_ref, spec_ref, mi_hbm, wi_hbm, tc_hbm, ts_hbm, *refs):
    *out_refs, spec, out_buf, mi_ref, wi_ref, tc_ref, ts_ref, in_sems, out_sems = refs
    ring, halves, kept, cuts, _ = out_buf.shape
    rows = spec.shape[1]
    moves = copies(
        [(spec_ref, spec), (mi_hbm, mi_ref), (tc_hbm, tc_ref), (ts_hbm, ts_ref), (wi_hbm, wi_ref)], in_sems, 0
    )
    start(moves)
    wait(moves)
    out = back(spec[...].reshape(kept * rows, 2 * LANES), mi_ref, wi_ref, tc_ref[...], ts_ref[...], kept, rows)
    out = out.astype(bf16)
    for place in range(ring * halves):
        at = place * cuts
        z, half = order(place, ring * halves)
        to = ((z - place_ref[0]) & (ring - 1), half ^ place_ref[1])
        for i in range(kept):
            out_buf[*to, i] = out[at : at + cuts, i * LANES : (i + 1) * LANES]
    moves = copies([(out_buf.at[z], out_refs[z]) for z in range(ring)], out_sems, 0)
    start(moves)
    wait(moves)


def lags(place, spec, t, n_tp, cuts):
    kept, rows, _ = spec.shape
    tables = [t[k] for k in (*CROSS_BACK, "turn_cos", "turn_sin")]
    ring = n_tp // SPLIT
    out = (SPLIT, kept, cuts, LANES)
    return pl.pallas_call(
        lags_kernel,
        in_specs=[pl.BlockSpec(memory_space=pltpu.SMEM)] + [ANY] * (1 + len(tables)),
        out_specs=[ANY] * ring,
        out_shape=[jax.ShapeDtypeStruct(out, bf16)] * ring,
        scratch_shapes=[
            pltpu.VMEM(spec.shape, bf16),
            pltpu.VMEM((ring, *out), bf16),
            *[pltpu.VMEM(v.shape, v.dtype) for v in tables],
            pltpu.SemaphoreType.DMA((1, 1 + len(tables))),
            pltpu.SemaphoreType.DMA((1, ring)),
        ],
        compiler_params=params(0),
        cost_estimate=pl.CostEstimate(
            flops=12 * kept * rows * LANES * 512, bytes_accessed=4 * spec.size, transcendentals=0
        ),
        name="lags",
    )(place, spec, *tables)


def order(place, n):
    return place % (n // SPLIT), place // (n // SPLIT)


def sum_scattered(parts, n):
    ring = n // SPLIT
    total = parts[0].astype(f32)
    for step in sorted(range(1, ring), key=lambda step: -min(step, ring - step)):
        pairs = [(i, i // ring * ring + (i + step) % ring) for i in range(n)]
        total = total + lax.ppermute(parts[step], "tp", pairs).astype(f32)
    return total


def body(query, key_in, value, grad_out, filter_raw, *, n_ctx, n_tp):
    group, length = filter_raw.shape
    rows = length // LANES
    kept = group // SPLIT
    root = 1.0 / math.sqrt(length)
    t = {k: jnp.asarray(v) for k, v in make_tables(length).items()}
    ring = n_tp // SPLIT
    sharing = [[c * n_tp + half * ring + z for c in range(n_ctx) for half in range(SPLIT)] for z in range(ring)]

    def exchange(x):
        flat = x.reshape(n_ctx * SPLIT, *x.shape[2:])
        flat = lax.all_to_all(
            flat, ("ctx", "tp"), split_axis=0, concat_axis=0, tiled=True, axis_index_groups=sharing
        )
        return flat.reshape(x.shape)

    place = order(lax.axis_index("tp"), n_tp)
    half = place[1]
    got = exchange(gate(query, key_in, value, grad_out, n_ctx))
    where = jnp.stack(place).astype(jnp.int32)
    filters = lax.dynamic_slice_in_dim(filter_raw, half * kept, kept, 0)
    filt = filter_spectrum(filters.reshape(kept, rows, LANES), t, root / length)
    filt, where = lax.optimization_barrier((filt, where))
    cross, made = channels(got, filt, t, root / length)
    tok = exchange(made)
    parts = lags(where, cross, t, n_tp, rows // n_ctx)
    total = sum_scattered(parts, n_tp)
    far = lax.ppermute(total[1], "tp", [(i, (i + ring) % n_tp) for i in range(n_tp)])
    grad_query, grad_key, grad_value = finish(tok, key_in, value, grad_out)
    mine, grad_query = lax.optimization_barrier((total[0], grad_query))
    first = jnp.where(half == 0, mine, far)
    second = jnp.where(half == 0, far, mine)
    filter_grad = jnp.concatenate([first, second], 0).reshape(group, length // n_tp)
    return (grad_query, grad_key, grad_value, filter_grad)


def solution(mesh):
    placed = (P("tp", "ctx"), P("tp", "ctx"), P("tp", "ctx"), P("tp", "ctx"), P("ctx", None))
    return jax.shard_map(
        functools.partial(body, n_ctx=mesh.shape["ctx"], n_tp=mesh.shape["tp"]),
        mesh=mesh,
        in_specs=placed,
        out_specs=(P("tp", "ctx"), P("tp", "ctx"), P("tp", "ctx"), P("ctx", "tp")),
        check_vma=False,
    )
```

time: 102 us -> 93.8 us (0.920)
  Pallas kernels: 36.4 us -> 28 us
  starting transfers between devices: 28.6 us -> 33 us
  other arithmetic: 3.94 us -> 1.56 us
  local copies, waits for them, and re-layouts: 3.2 us -> 1.97 us
    pallas_call x1, Pallas kernels: 10.8 us -> 4.8 us  [filter_spectrum(): pl.pallas_call(functools.partial(filter_kernel, scale=scale), grid=(n //...]
    ppermute x6 -> x8, starting transfers between devices: 15.1 us -> 18.9 us  [the longest x7 16 us: sum_scattered(): total = total + lax.ppermute(parts[step], 'tp', pairs).astype(f32)]
    pallas_call x2, Pallas kernels: 17.4 us -> 14.8 us  [the longest x1 9.56 us: channels(): pl.pallas_call(functools.partial(channels_kernel, scale=scale), in_specs=...]
    convert_element_type x2 -> x0, other arithmetic: 2.24 us -> none  [sum_ring(): share = (stay[:, step].astype(f32) + got[:, step].astype(f32)).astype(bf16)]
    ppermute x6 -> x8, waiting for transfers between devices: 7.58 us -> 6.43 us  [the longest x7 6.43 us: sum_scattered(): total = total + lax.ppermute(parts[step], 'tp', pairs).astype(f32)]
    unnamed x12 -> x9, local copies, waits for them, and re-layouts: 2.52 us -> 1.96 us
  transfers between devices with their start and end apart: 8 -> 10, of which waited for: 5 -> 5; matrix products, arithmetic and copies ran while one was open for 6% -> 3% of each run, Pallas kernels for 20% -> 15%
where the time goes in v2:
time: 93.8 us; the launch traced here: 93.4 us
  starting transfers between devices  33 us (35%)
  waiting for transfers between devices  28.1 us (30%)
  Pallas kernels  28 us (30%)
  local copies, waits for them, and re-layouts  1.97 us (2%)
  other arithmetic  1.56 us (2%)
    all_to_all x2, waiting for transfers between devices, exchange(): lax.all_to_all(flat, ('ctx', 'tp'), split_axis=0, concat_axis=0, tiled=Tr...  21.7 us
    ppermute x7, starting transfers between devices, sum_scattered(): total = total + lax.ppermute(parts[step], 'tp', pairs).astype(f32)  16 us
    all_to_all x2, starting transfers between devices, exchange(): lax.all_to_all(flat, ('ctx', 'tp'), split_axis=0, concat_axis=0, tiled=Tr...  14.1 us
    pallas_call x1, Pallas kernels, channels(): pl.pallas_call(functools.partial(channels_kernel, scale=scale), in_specs=...  9.56 us
    ppermute x7, waiting for transfers between devices, sum_scattered(): total = total + lax.ppermute(parts[step], 'tp', pairs).astype(f32)  6.43 us
    pallas_call x1, Pallas kernels, lags(): pl.pallas_call(lags_kernel, in_specs=[pl.BlockSpec(memory_space=pltpu.SME...  5.23 us
    pallas_call x1, Pallas kernels, filter_spectrum(): pl.pallas_call(functools.partial(filter_kernel, scale=scale), grid=(n //...  4.8 us
    pallas_call x1, Pallas kernels, gate(): pl.pallas_call(gate_kernel, in_specs=[ANY] * 4 + [VMEM], out_specs=ANY, o...  4.62 us
  transfers between devices with their start and end apart: 10, of which 5 were waited for; matrix products, arithmetic and copies ran while one was open for 3% of the time, Pallas kernels for 15%

profile of v2, /device:TPU:1, one launch (start us, length us, event | category | flops | bytes accessed | tf_op | source)
XLA Modules:
  0.0 93.4 jit_solution(14371688614888810538)
XLA Ops:
  0.6 4.6 %gate.1 = bf16[16,2,2,8,16,128]{5,4,3,2,1,0:T(8,128)(2,1)} custom-call(bf16[256,2048]{1,0:T(8,128)(2,1)} %q_ref.1, bf16[256,2048]{1,0:T(8,128)(2,1)} %k_ref.3, bf16[256,2048]{1,0:T(8,128)(2,1)} %v_ref.3, bf16[256,2048]{1,0:T(8,128)(2,1)} %g_ref.3, bf16[256,256]{1,0:T(8,128)(2,1)} %constant.65.clone.swap_ref), custom_call_target="tpu_custom_call" | custom-call | flops 1048576 | bytes 6291456 | tf_op jit(solution)/shard_map/gate/pallas_call | solution.py:140
  5.3 8.7 %all-to-all-start = ((bf16[32,2,8,16,128]{4,3,2,1,0:T(8,128)(2,1)}), bf16[32,2,8,16,128]{4,3,2,1,0:T(8,128)(2,1)}, u32[]{:S(2)}, u32[]{:S(2)}) async-start(bf16[32,2,8,16,128]{4,3,2,1,0:T(8,128)(2,1)} %bitcast.19), calls=%async_computation | async-start | bytes 4194304 | tf_op jit(solution)/shard_map/all_to_all | solution.py:432
  14.1 1.2 %copy.25 = f32[1,8,256,128]{3,2,1,0:T(8,128)} copy(f32[1,8,256,128]{3,1,2,0:T(8,128)S(1)} %dynamic-slice_bitcast_fusion) | data formatting | bytes 2097152
  15.2 0.6 pad_add_fusion.place_ref
  15.8 4.8 %filter_spectrum.1.f_ref = f32[8,256,256]{2,1,0:T(8,128)} custom-call(f32[8,256,128]{2,1,0:T(8,128)} %bitcast.21, bf16[512,768]{1,0:T(8,128)(2,1)} %constant.55.clone.w_ref, bf16[768,256]{1,0:T(8,128)(2,1)} %constant.56.clone.m_ref, f32[256,128]{1,0:T(8,128)} %constant.63.clone.tc_ref.tc_hbm, f32[256,128]{1,0:T(8,128)} %constant.64.clone.ts_ref.ts_hbm), custom_call_target="tpu_custom_call" | custom-call | flops 1610612736 | bytes 4194304 | tf_op jit(solution)/shard_map/filter_spectrum/pallas_call | solution.py:237
  20.6 21.7 %all-to-all-done = bf16[32,2,8,16,128]{4,3,2,1,0:T(8,128)(2,1)} async-done(((bf16[32,2,8,16,128]{4,3,2,1,0:T(8,128)(2,1)}), bf16[32,2,8,16,128]{4,3,2,1,0:T(8,128)(2,1)}, u32[]{:S(2)}, u32[]{:S(2)}) %all-to-all-start) | async-done | bytes 2097184 | tf_op jit(solution)/shard_map/all_to_all | solution.py:432
  42.3 9.6 %channels.1 = (bf16[8,256,256]{2,1,0:T(8,128)(2,1)}, bf16[16,2,2,8,16,128]{5,4,3,2,1,0:T(8,128)(2,1)}) custom-call(bf16[16,2,2,8,16,128]{5,4,3,2,1,0:T(8,128)(2,1)} %bitcast.3.x_ref, f32[8,256,256]{2,1,0:T(8,128)} %filter_spectrum.1.f_ref, bf16[512,256]{1,0:T(8,128)(2,1)} %constant.57.clone.w_hbm, bf16[256,256]{1,0:T(8,128)(2,1)} %constant.58.clone.m_hbm, ...), custom_call_target="tpu_custom_call" | custom-call | flops 6442450944 | bytes 8388608 | tf_op jit(solution)/shard_map/channels/pallas_call | solution.py:338
  51.8 5.5 %all-to-all-start.1 = ((bf16[32,2,8,16,128]{4,3,2,1,0:T(8,128)(2,1)}), bf16[32,2,8,16,128]{4,3,2,1,0:T(8,128)(2,1)}, u32[]{:S(2)}, u32[]{:S(2)}) async-start(bf16[32,2,8,16,128]{4,3,2,1,0:T(8,128)(2,1)} %bitcast.20), calls=%async_computation.1 | async-start | bytes 4194304 | tf_op jit(solution)/shard_map/all_to_all | solution.py:432
  57.4 5.2 %lags.1 = (bf16[2,8,16,128]{3,2,1,0:T(8,128)(2,1)}, bf16[2,8,16,128]{3,2,1,0:T(8,128)(2,1)}, bf16[2,8,16,128]{3,2,1,0:T(8,128)(2,1)}, bf16[2,8,16,128]{3,2,1,0:T...) custom-call(s32[2]{0:T(128)} %pad_add_fusion.place_ref, ...), custom_call_target="tpu_custom_call" | custom-call | flops 1610612736 | bytes 2097152 | tf_op jit(solution)/shard_map/lags/pallas_call | solution.py:388
  62.6 7.0 %collective-permute-start = (bf16[2,8,16,128]{3,2,1,0:T(8,128)(2,1)}, bf16[2,8,16,128]{3,2,1,0:T(8,128)(2,1)S(1)}, u32[]{:S(2)}, u32[]{:S(2)}) collective-permute-start(bf16[2,8,16,128]{3,2,1,0:T(8,128)(2,1)} %get-tuple-element.25), channel_id=1, source_target_pairs={{0,4},{1,5},{2,6},{3,7},{4,0},{5,1},{6,2},{7,3},{8,12},{9,13},{10,... | collective-permute-start | bytes 196616 | tf_op jit(solution)/shard_map/ppermute | solution.py:417
  69.6 1.6 %collective-permute-start.1 = (bf16[2,8,16,128]{3,2,1,0:T(8,128)(2,1)}, bf16[2,8,16,128]{3,2,1,0:T(8,128)(2,1)S(1)}, u32[]{:S(2)}, u32[]{:S(2)}) collective-permute-start(bf16[2,8,16,128]{3,2,1,0:T(8,128)(2,1)} %get-tuple-element.26), channel_id=1, source_target_pairs={{0,3},{1,4},{2,5},{3,6},{4,7},{5,0},{6,1},{7,2},{8,11},{9,12},{10,... | collective-permute-start | bytes 196616 | tf_op jit(solution)/shard_map/ppermute | solution.py:417
  71.2 2.8 %collective-permute-start.2 = (bf16[2,8,16,128]{3,2,1,0:T(8,128)(2,1)}, bf16[2,8,16,128]{3,2,1,0:T(8,128)(2,1)S(1)}, u32[]{:S(2)}, u32[]{:S(2)}) collective-permute-start(bf16[2,8,16,128]{3,2,1,0:T(8,128)(2,1)} %get-tuple-element.27), channel_id=1, source_target_pairs={{0,5},{1,6},{2,7},{3,0},{4,1},{5,2},{6,3},{7,4},{8,13},{9,14},{10,... | collective-permute-start | bytes 196616 | tf_op jit(solution)/shard_map/ppermute | solution.py:417
  74.1 1.2 %collective-permute-start.3 = (bf16[2,8,16,128]{3,2,1,0:T(8,128)(2,1)}, bf16[2,8,16,128]{3,2,1,0:T(8,128)(2,1)S(1)}, u32[]{:S(2)}, u32[]{:S(2)}) collective-permute-start(bf16[2,8,16,128]{3,2,1,0:T(8,128)(2,1)} %get-tuple-element.28), channel_id=1, source_target_pairs={{0,2},{1,3},{2,4},{3,5},{4,6},{5,7},{6,0},{7,1},{8,10},{9,11},{10,... | collective-permute-start | bytes 196616 | tf_op jit(solution)/shard_map/ppermute | solution.py:417
  75.3 2.4 %collective-permute-start.4 = (bf16[2,8,16,128]{3,2,1,0:T(8,128)(2,1)}, bf16[2,8,16,128]{3,2,1,0:T(8,128)(2,1)S(1)}, u32[]{:S(2)}, u32[]{:S(2)}) collective-permute-start(bf16[2,8,16,128]{3,2,1,0:T(8,128)(2,1)} %get-tuple-element.29), channel_id=1, source_target_pairs={{0,6},{1,7},{2,0},{3,1},{4,2},{5,3},{6,4},{7,5},{8,14},{9,15},{10,... | collective-permute-start | bytes 196616 | tf_op jit(solution)/shard_map/ppermute | solution.py:417
  77.6 0.7 collective-permute-start.5
  78.4 1.7 %collective-permute-done.1 = bf16[2,8,16,128]{3,2,1,0:T(8,128)(2,1)S(1)} collective-permute-done((bf16[2,8,16,128]{3,2,1,0:T(8,128)(2,1)}, bf16[2,8,16,128]{3,2,1,0:T(8,128)(2,1)S(1)}, u32[]{:S(2)}, u32[]{:S(2)}) %collective-permute-start.1) | collective-permute-done | bytes 65568 | tf_op jit(solution)/shard_map/ppermute | solution.py:417
  80.1 0.3 collective-permute-start.6
  80.3 0.2 collective-permute-done.3
  80.5 2.4 %collective-permute-done.4 = bf16[2,8,16,128]{3,2,1,0:T(8,128)(2,1)S(1)} collective-permute-done((bf16[2,8,16,128]{3,2,1,0:T(8,128)(2,1)}, bf16[2,8,16,128]{3,2,1,0:T(8,128)(2,1)S(1)}, u32[]{:S(2)}, u32[]{:S(2)}) %collective-permute-start.4) | collective-permute-done | bytes 65568 | tf_op jit(solution)/shard_map/ppermute | solution.py:417
  82.9 2.1 %collective-permute-done.6 = bf16[2,8,16,128]{3,2,1,0:T(8,128)(2,1)S(1)} collective-permute-done((bf16[2,8,16,128]{3,2,1,0:T(8,128)(2,1)}, bf16[2,8,16,128]{3,2,1,0:T(8,128)(2,1)S(1)}, u32[]{:S(2)}, u32[]{:S(2)}) %collective-permute-start.6) | collective-permute-done | bytes 65568 | tf_op jit(solution)/shard_map/ppermute | solution.py:417
  85.1 0.9 convert_add_fusion
  86.0 2.8 %collective-permute-start.7 = (f32[8,16,128]{2,1,0:T(8,128)S(1)}, f32[8,16,128]{2,1,0:T(8,128)S(1)}, u32[]{:S(2)}, u32[]{:S(2)}) collective-permute-start(f32[8,16,128]{2,1,0:T(8,128)S(1)} %get-tuple-element.40), channel_id=1, source_target_pairs={{0,8},{1,9},{2,10},{3,11},{4,12},{5,13},{6,14},{7,15},{8,0},{9,1},... | collective-permute-start | bytes 196616 | tf_op jit(solution)/shard_map/ppermute | solution.py:448
  88.8 3.8 %finish.1 = (bf16[256,2048]{1,0:T(8,128)(2,1)}, bf16[256,2048]{1,0:T(8,128)(2,1)}, bf16[256,2048]{1,0:T(8,128)(2,1)}) custom-call(bf16[16,2,2,8,16,128]{5,4,3,2,1,0:T(8,128)(2,1)} %bitcast.6.tok_ref, bf16[256,2048]{1,0:T(8,128)(2,1)S(1)} %copy-done.1, bf16[256,2048]{1,0:T(8,128)(2,1)} %v_ref.3, bf16[256,2048]{1,0:T(8,128)(2,1)} %g_ref.3, ...), custom_call_target="tpu_custom_call" | custom-call | flops 1572864 | bytes 8388608 | tf_op jit(solution)/shard_map/finish/pallas_call | solution.py:198
  92.7 0.7 copy.26
  (15 shorter events, 0.1 us)
Async XLA Ops:
  0.6 13.3 %copy-start = (f32[16,32768]{1,0:T(8,128)S(1)}, f32[16,32768]{1,0:T(8,128)}, u32[]{:S(2)}) copy-start(f32[16,32768]{1,0:T(8,128)} %param.21) | copy-start | bytes 6291460
  5.3 37.0 %all-to-all-start = ((bf16[32,2,8,16,128]{4,3,2,1,0:T(8,128)(2,1)}), bf16[32,2,8,16,128]{4,3,2,1,0:T(8,128)(2,1)}, u32[]{:S(2)}, u32[]{:S(2)}) async-start(bf16[32,2,8,16,128]{4,3,2,1,0:T(8,128)(2,1)} %bitcast.19), calls=%async_computation | async-start | bytes 4194304 | tf_op jit(solution)/shard_map/all_to_all | solution.py:432
  51.8 37.0 %all-to-all-start.1 = ((bf16[32,2,8,16,128]{4,3,2,1,0:T(8,128)(2,1)}), bf16[32,2,8,16,128]{4,3,2,1,0:T(8,128)(2,1)}, u32[]{:S(2)}, u32[]{:S(2)}) async-start(bf16[32,2,8,16,128]{4,3,2,1,0:T(8,128)(2,1)} %bitcast.20), calls=%async_computation.1 | async-start | bytes 4194304 | tf_op jit(solution)/shard_map/all_to_all | solution.py:432
  57.3 31.5 %copy-start.1 = (bf16[256,2048]{1,0:T(8,128)(2,1)S(1)}, bf16[256,2048]{1,0:T(8,128)(2,1)}, u32[]{:S(2)}) copy-start(bf16[256,2048]{1,0:T(8,128)(2,1)} %k_ref.3) | copy-start | bytes 3145732
  57.3 31.5 %copy-start.2 = (bf16[256,256]{1,0:T(8,128)(2,1)S(1)}, bf16[256,256]{1,0:T(8,128)(2,1)}, u32[]{:S(2)}) copy-start(bf16[256,256]{1,0:T(8,128)(2,1)} %constant.65.clone.swap_ref) | copy-start | bytes 393220
  62.6 15.0 %collective-permute-start = (bf16[2,8,16,128]{3,2,1,0:T(8,128)(2,1)}, bf16[2,8,16,128]{3,2,1,0:T(8,128)(2,1)S(1)}, u32[]{:S(2)}, u32[]{:S(2)}) collective-permute-start(bf16[2,8,16,128]{3,2,1,0:T(8,128)(2,1)} %get-tuple-element.25), channel_id=1, source_target_pairs={{0,4},{1,5},{2,6},{3,7},{4,0},{5,1},{6,2},{7,3},{8,12},{9,13},{10,... | collective-permute-start | bytes 196616 | tf_op jit(solution)/shard_map/ppermute | solution.py:417
  69.6 10.5 %collective-permute-start.1 = (bf16[2,8,16,128]{3,2,1,0:T(8,128)(2,1)}, bf16[2,8,16,128]{3,2,1,0:T(8,128)(2,1)S(1)}, u32[]{:S(2)}, u32[]{:S(2)}) collective-permute-start(bf16[2,8,16,128]{3,2,1,0:T(8,128)(2,1)} %get-tuple-element.26), channel_id=1, source_target_pairs={{0,3},{1,4},{2,5},{3,6},{4,7},{5,0},{6,1},{7,2},{8,11},{9,12},{10,... | collective-permute-start | bytes 196616 | tf_op jit(solution)/shard_map/ppermute | solution.py:417
  71.2 9.1 %collective-permute-start.2 = (bf16[2,8,16,128]{3,2,1,0:T(8,128)(2,1)}, bf16[2,8,16,128]{3,2,1,0:T(8,128)(2,1)S(1)}, u32[]{:S(2)}, u32[]{:S(2)}) collective-permute-start(bf16[2,8,16,128]{3,2,1,0:T(8,128)(2,1)} %get-tuple-element.27), channel_id=1, source_target_pairs={{0,5},{1,6},{2,7},{3,0},{4,1},{5,2},{6,3},{7,4},{8,13},{9,14},{10,... | collective-permute-start | bytes 196616 | tf_op jit(solution)/shard_map/ppermute | solution.py:417
  74.1 6.5 %collective-permute-start.3 = (bf16[2,8,16,128]{3,2,1,0:T(8,128)(2,1)}, bf16[2,8,16,128]{3,2,1,0:T(8,128)(2,1)S(1)}, u32[]{:S(2)}, u32[]{:S(2)}) collective-permute-start(bf16[2,8,16,128]{3,2,1,0:T(8,128)(2,1)} %get-tuple-element.28), channel_id=1, source_target_pairs={{0,2},{1,3},{2,4},{3,5},{4,6},{5,7},{6,0},{7,1},{8,10},{9,11},{10,... | collective-permute-start | bytes 196616 | tf_op jit(solution)/shard_map/ppermute | solution.py:417
  75.3 7.7 %collective-permute-start.4 = (bf16[2,8,16,128]{3,2,1,0:T(8,128)(2,1)}, bf16[2,8,16,128]{3,2,1,0:T(8,128)(2,1)S(1)}, u32[]{:S(2)}, u32[]{:S(2)}) collective-permute-start(bf16[2,8,16,128]{3,2,1,0:T(8,128)(2,1)} %get-tuple-element.29), channel_id=1, source_target_pairs={{0,6},{1,7},{2,0},{3,1},{4,2},{5,3},{6,4},{7,5},{8,14},{9,15},{10,... | collective-permute-start | bytes 196616 | tf_op jit(solution)/shard_map/ppermute | solution.py:417
  77.6 5.3 %collective-permute-start.5 = (bf16[2,8,16,128]{3,2,1,0:T(8,128)(2,1)}, bf16[2,8,16,128]{3,2,1,0:T(8,128)(2,1)S(1)}, u32[]{:S(2)}, u32[]{:S(2)}) collective-permute-start(bf16[2,8,16,128]{3,2,1,0:T(8,128)(2,1)} %get-tuple-element.30), channel_id=1, source_target_pairs={{0,1},{1,2},{2,3},{3,4},{4,5},{5,6},{6,7},{7,0},{8,9},{9,10},{10,1... | collective-permute-start | bytes 196616 | tf_op jit(solution)/shard_map/ppermute | solution.py:417
  80.1 5.0 %collective-permute-start.6 = (bf16[2,8,16,128]{3,2,1,0:T(8,128)(2,1)}, bf16[2,8,16,128]{3,2,1,0:T(8,128)(2,1)S(1)}, u32[]{:S(2)}, u32[]{:S(2)}) collective-permute-start(bf16[2,8,16,128]{3,2,1,0:T(8,128)(2,1)} %get-tuple-element.31), channel_id=1, source_target_pairs={{0,7},{1,0},{2,1},{3,2},{4,3},{5,4},{6,5},{7,6},{8,15},{9,8},{10,9... | collective-permute-start | bytes 196616 | tf_op jit(solution)/shard_map/ppermute | solution.py:417
  86.0 6.6 %collective-permute-start.7 = (f32[8,16,128]{2,1,0:T(8,128)S(1)}, f32[8,16,128]{2,1,0:T(8,128)S(1)}, u32[]{:S(2)}, u32[]{:S(2)}) collective-permute-start(f32[8,16,128]{2,1,0:T(8,128)S(1)} %get-tuple-element.40), channel_id=1, source_target_pairs={{0,8},{1,9},{2,10},{3,11},{4,12},{5,13},{6,14},{7,15},{8,0},{9,1},... | collective-permute-start | bytes 196616 | tf_op jit(solution)/shard_map/ppermute | solution.py:448

commit v3 on v2

--- a/solution.py
+++ b/solution.py
@@ -13,10 +13,11 @@
 LANES = 128
 VMEM_LIMIT = 56 * 2**20
 SPLIT = 2
+GATE_STEPS = 2
 TOKEN_STEPS = 4
 FILTERS = 4
 FILTER_PAIR = 4
-CROSS_BACK = ("mi2", "wi2")
+CROSS_BACK = ("mi", "wi")
 TOKEN_BACK = ("mi", "wi")
 f32 = jnp.float32
 bf16 = jnp.bfloat16
@@ -97,10 +98,12 @@
 VMEM = pl.BlockSpec(memory_space=pltpu.VMEM)
 
 
-def gate_kernel(q_ref, k_ref, v_ref, g_ref, swap_ref, out_ref, q, k, v, g, o, in_sems, out_sems):
+def gate_kernel(
+    q_ref, k_ref, v_ref, g_ref, swap_hbm, out_ref, q, k, v, g, o, swap_ref, in_sems, out_sems, swap_sems
+):
     n, split, _, kept, cuts, _ = out_ref.shape
     group = split * kept
-    runs = n // TOKEN_STEPS
+    runs = n // GATE_STEPS
 
     def loads(step):
         rows = pl.ds(step * runs * group, runs * group)
@@ -111,15 +114,18 @@
         at = pl.ds(step * runs, runs)
         return copies([(o.at[at], out_ref.at[at])], out_sems, step)
 
-    for step in range(TOKEN_STEPS):
+    swap = copies([(swap_hbm, swap_ref)], swap_sems, 0)
+    start(swap)
+    for step in range(GATE_STEPS):
         start(loads(step))
-    for step in range(TOKEN_STEPS):
+    wait(swap)
+    for step in range(GATE_STEPS):
         wait(loads(step))
         for run in range(step * runs, (step + 1) * runs):
             rows = slice(run * group, (run + 1) * group)
 
             def product(x, y):
-                z = (x[rows, :].astype(f32) * y[rows, :].astype(f32)).astype(bf16)
+                z = x[rows, :] * y[rows, :]
                 return jnp.concatenate([z[:, j * LANES : (j + 1) * LANES] for j in range(cuts)], 0)
 
             both = jnp.concatenate([product(k, v), product(g, q)], 1)
@@ -127,7 +133,7 @@
             for s in range(2):
                 o[run, :, s] = out[:, s * LANES : (s + 1) * LANES].reshape(split, kept, cuts, LANES)
         start(stores(step))
-    for step in range(TOKEN_STEPS):
+    for step in range(GATE_STEPS):
         wait(stores(step))
 
 
@@ -139,11 +145,17 @@
     sent = (n, SPLIT, 2, group // SPLIT, cuts, LANES)
     return pl.pallas_call(
         gate_kernel,
-        in_specs=[ANY] * 4 + [VMEM],
+        in_specs=[ANY] * 5,
         out_specs=ANY,
         out_shape=jax.ShapeDtypeStruct(sent, bf16),
         scratch_shapes=[pltpu.VMEM(query.shape, bf16)] * 4
-        + [pltpu.VMEM(sent, bf16), pltpu.SemaphoreType.DMA((TOKEN_STEPS, 4)), pltpu.SemaphoreType.DMA((TOKEN_STEPS, 1))],
+        + [
+            pltpu.VMEM(sent, bf16),
+            pltpu.VMEM(swap.shape, bf16),
+            pltpu.SemaphoreType.DMA((GATE_STEPS, 4)),
+            pltpu.SemaphoreType.DMA((GATE_STEPS, 1)),
+            pltpu.SemaphoreType.DMA((1, 1)),
+        ],
         compiler_params=params(0),
         cost_estimate=pl.CostEstimate(
             flops=2 * channels * length, bytes_accessed=12 * channels * length, transcendentals=0
@@ -178,14 +190,14 @@
         for run in range(step * runs, (step + 1) * runs):
             rows = slice(run * group, (run + 1) * group)
             both = jnp.concatenate([tok[run, :, s].reshape(group * cuts, LANES) for s in range(2)], 1)
-            out = dot(swap_ref[...], both)
+            out = dot(swap_ref[...], both).astype(bf16)
             for j in range(cuts):
                 lanes = slice(j * LANES, (j + 1) * LANES)
                 conv = out[j * group : (j + 1) * group, :LANES]
                 dgated = out[j * group : (j + 1) * group, LANES:]
-                gq[rows, lanes] = (g[rows, lanes].astype(f32) * conv).astype(bf16)
-                gk[rows, lanes] = (dgated * v[rows, lanes].astype(f32)).astype(bf16)
-                gv[rows, lanes] = (dgated * k[rows, lanes].astype(f32)).astype(bf16)
+                gq[rows, lanes] = g[rows, lanes] * conv
+                gk[rows, lanes] = dgated * v[rows, lanes]
+                gv[rows, lanes] = dgated * k[rows, lanes]
         start(stores(step))
     for step in range(TOKEN_STEPS):
         wait(stores(step))
@@ -445,12 +457,11 @@
     tok = exchange(made)
     parts = lags(where, cross, t, n_tp, rows // n_ctx)
     total = sum_scattered(parts, n_tp)
+    total = total.reshape(SPLIT, kept, length // n_tp)
     far = lax.ppermute(total[1], "tp", [(i, (i + ring) % n_tp) for i in range(n_tp)])
     grad_query, grad_key, grad_value = finish(tok, key_in, value, grad_out)
     mine, grad_query = lax.optimization_barrier((total[0], grad_query))
-    first = jnp.where(half == 0, mine, far)
-    second = jnp.where(half == 0, far, mine)
-    filter_grad = jnp.concatenate([first, second], 0).reshape(group, length // n_tp)
+    filter_grad = jnp.where(jnp.arange(SPLIT)[:, None, None] == half, mine, far).reshape(group, length // n_tp)
     return (grad_query, grad_key, grad_value, filter_grad)
 
 

time: 93.8 us -> 92.3 us (0.984)
  Pallas kernels: 28 us -> 26.3 us
    pallas_call x1, Pallas kernels: 5.23 us -> 4.01 us  [lags(): pl.pallas_call(lags_kernel, in_specs=[pl.BlockSpec(memory_space=pltpu.SME...]
    unnamed x9 -> x11, local copies, waits for them, and re-layouts: 1.96 us -> 1.32 us
  transfers between devices with their start and end apart: 10 -> 10, of which waited for: 5 -> 5; matrix products, arithmetic and copies ran while one was open for 3% -> 3% of each run, Pallas kernels for 15% -> 14%
where the time goes in v3:
time: 92.3 us; the launch traced here: 92 us
  starting transfers between devices  33.1 us (36%)
  waiting for transfers between devices  28 us (30%)
  Pallas kernels  26.3 us (28%)
  other arithmetic  2.25 us (2%)
  local copies, waits for them, and re-layouts  1.48 us (2%)
    all_to_all x2, waiting for transfers between devices, exchange(): lax.all_to_all(flat, ('ctx', 'tp'), split_axis=0, concat_axis=0, tiled=Tr...  21.7 us
    ppermute x7, starting transfers between devices, sum_scattered(): total = total + lax.ppermute(parts[step], 'tp', pairs).astype(f32)  16.1 us
    all_to_all x2, starting transfers between devices, exchange(): lax.all_to_all(flat, ('ctx', 'tp'), split_axis=0, concat_axis=0, tiled=Tr...  14.1 us
    pallas_call x1, Pallas kernels, channels(): pl.pallas_call(functools.partial(channels_kernel, scale=scale), in_specs=...  9.55 us
    ppermute x7, waiting for transfers between devices, sum_scattered(): total = total + lax.ppermute(parts[step], 'tp', pairs).astype(f32)  6.3 us
    pallas_call x1, Pallas kernels, filter_spectrum(): pl.pallas_call(functools.partial(filter_kernel, scale=scale), grid=(n //...  4.8 us
    pallas_call x1, Pallas kernels, gate(): pl.pallas_call(gate_kernel, in_specs=[ANY] * 5, out_specs=ANY, out_shape=...  4.17 us
    pallas_call x1, Pallas kernels, lags(): pl.pallas_call(lags_kernel, in_specs=[pl.BlockSpec(memory_space=pltpu.SME...  4.01 us
  transfers between devices with their start and end apart: 10, of which 5 were waited for; matrix products, arithmetic and copies ran while one was open for 3% of the time, Pallas kernels for 14%

profile of v3, /device:TPU:1, one launch (start us, length us, event | category | flops | bytes accessed | tf_op | source)
XLA Modules:
  0.0 92.0 jit_solution(17729125354194356937)
XLA Ops:
  0.6 4.2 %gate.1 = bf16[16,2,2,8,16,128]{5,4,3,2,1,0:T(8,128)(2,1)} custom-call(bf16[256,2048]{1,0:T(8,128)(2,1)} %q_ref.1, bf16[256,2048]{1,0:T(8,128)(2,1)} %k_ref.3, bf16[256,2048]{1,0:T(8,128)(2,1)} %v_ref.3, bf16[256,2048]{1,0:T(8,128)(2,1)} %g_ref.3, bf16[256,256]{1,0:T(8,128)(2,1)} %constant.59.clone.swap_hbm.swap_ref), custom_call_target="tpu_custom_call" | custom-call | flops 1048576 | bytes 6291456 | tf_op jit(solution)/shard_map/gate/pallas_call | solution.py:146
  4.8 8.7 %all-to-all-start = ((bf16[32,2,8,16,128]{4,3,2,1,0:T(8,128)(2,1)}), bf16[32,2,8,16,128]{4,3,2,1,0:T(8,128)(2,1)}, u32[]{:S(2)}, u32[]{:S(2)}) async-start(bf16[32,2,8,16,128]{4,3,2,1,0:T(8,128)(2,1)} %bitcast.27), calls=%async_computation | async-start | bytes 4194304 | tf_op jit(solution)/shard_map/all_to_all | solution.py:444
  13.6 1.2 %copy.25 = f32[1,8,256,128]{3,2,1,0:T(8,128)} copy(f32[1,8,256,128]{3,1,2,0:T(8,128)S(1)} %dynamic-slice_bitcast_fusion) | data formatting | bytes 2097152
  14.8 0.6 pad_add_fusion.place_ref
  15.4 4.8 %filter_spectrum.1.f_ref = f32[8,256,256]{2,1,0:T(8,128)} custom-call(f32[8,256,128]{2,1,0:T(8,128)} %bitcast.29, bf16[512,768]{1,0:T(8,128)(2,1)} %constant.51.clone.w_ref, bf16[768,256]{1,0:T(8,128)(2,1)} %constant.52.clone.m_ref, f32[256,128]{1,0:T(8,128)} %constant.57.clone.tc_ref.tc_hbm, f32[256,128]{1,0:T(8,128)} %constant.58.clone.ts_ref.ts_hbm), custom_call_target="tpu_custom_call" | custom-call | flops 1610612736 | bytes 4194304 | tf_op jit(solution)/shard_map/filter_spectrum/pallas_call | solution.py:249
  20.2 21.7 %all-to-all-done = bf16[32,2,8,16,128]{4,3,2,1,0:T(8,128)(2,1)} async-done(((bf16[32,2,8,16,128]{4,3,2,1,0:T(8,128)(2,1)}), bf16[32,2,8,16,128]{4,3,2,1,0:T(8,128)(2,1)}, u32[]{:S(2)}, u32[]{:S(2)}) %all-to-all-start) | async-done | bytes 2097184 | tf_op jit(solution)/shard_map/all_to_all | solution.py:444
  41.8 9.6 %channels.1 = (bf16[8,256,256]{2,1,0:T(8,128)(2,1)}, bf16[16,2,2,8,16,128]{5,4,3,2,1,0:T(8,128)(2,1)}) custom-call(bf16[16,2,2,8,16,128]{5,4,3,2,1,0:T(8,128)(2,1)} %bitcast.3.x_ref, f32[8,256,256]{2,1,0:T(8,128)} %filter_spectrum.1.f_ref, bf16[512,256]{1,0:T(8,128)(2,1)} %constant.53.clone.w_hbm, bf16[256,256]{1,0:T(8,128)(2,1)} %constant.54.clone.m_hbm, ...), custom_call_target="tpu_custom_call" | custom-call | flops 6442450944 | bytes 8388608 | tf_op jit(solution)/shard_map/channels/pallas_call | solution.py:350
  51.4 5.5 %all-to-all-start.1 = ((bf16[32,2,8,16,128]{4,3,2,1,0:T(8,128)(2,1)}), bf16[32,2,8,16,128]{4,3,2,1,0:T(8,128)(2,1)}, u32[]{:S(2)}, u32[]{:S(2)}) async-start(bf16[32,2,8,16,128]{4,3,2,1,0:T(8,128)(2,1)} %bitcast.28), calls=%async_computation.1 | async-start | bytes 4194304 | tf_op jit(solution)/shard_map/all_to_all | solution.py:444
  56.9 4.0 %lags.1 = (bf16[2,8,16,128]{3,2,1,0:T(8,128)(2,1)}, bf16[2,8,16,128]{3,2,1,0:T(8,128)(2,1)}, bf16[2,8,16,128]{3,2,1,0:T(8,128)(2,1)}, bf16[2,8,16,128]{3,2,1,0:T...) custom-call(s32[2]{0:T(128)} %pad_add_fusion.place_ref, ...), custom_call_target="tpu_custom_call" | custom-call | flops 1610612736 | bytes 2097152 | tf_op jit(solution)/shard_map/lags/pallas_call | solution.py:400
  60.9 7.0 %collective-permute-start = (bf16[2,8,16,128]{3,2,1,0:T(8,128)(2,1)}, bf16[2,8,16,128]{3,2,1,0:T(8,128)(2,1)S(1)}, u32[]{:S(2)}, u32[]{:S(2)}) collective-permute-start(bf16[2,8,16,128]{3,2,1,0:T(8,128)(2,1)} %get-tuple-element.25), channel_id=1, source_target_pairs={{0,4},{1,5},{2,6},{3,7},{4,0},{5,1},{6,2},{7,3},{8,12},{9,13},{10,... | collective-permute-start | bytes 196616 | tf_op jit(solution)/shard_map/ppermute | solution.py:429
  67.9 1.6 %collective-permute-start.1 = (bf16[2,8,16,128]{3,2,1,0:T(8,128)(2,1)}, bf16[2,8,16,128]{3,2,1,0:T(8,128)(2,1)S(1)}, u32[]{:S(2)}, u32[]{:S(2)}) collective-permute-start(bf16[2,8,16,128]{3,2,1,0:T(8,128)(2,1)} %get-tuple-element.26), channel_id=1, source_target_pairs={{0,3},{1,4},{2,5},{3,6},{4,7},{5,0},{6,1},{7,2},{8,11},{9,12},{10,... | collective-permute-start | bytes 196616 | tf_op jit(solution)/shard_map/ppermute | solution.py:429
  69.6 2.8 %collective-permute-start.2 = (bf16[2,8,16,128]{3,2,1,0:T(8,128)(2,1)}, bf16[2,8,16,128]{3,2,1,0:T(8,128)(2,1)S(1)}, u32[]{:S(2)}, u32[]{:S(2)}) collective-permute-start(bf16[2,8,16,128]{3,2,1,0:T(8,128)(2,1)} %get-tuple-element.27), channel_id=1, source_target_pairs={{0,5},{1,6},{2,7},{3,0},{4,1},{5,2},{6,3},{7,4},{8,13},{9,14},{10,... | collective-permute-start | bytes 196616 | tf_op jit(solution)/shard_map/ppermute | solution.py:429
  72.4 1.2 %collective-permute-start.3 = (bf16[2,8,16,128]{3,2,1,0:T(8,128)(2,1)}, bf16[2,8,16,128]{3,2,1,0:T(8,128)(2,1)S(1)}, u32[]{:S(2)}, u32[]{:S(2)}) collective-permute-start(bf16[2,8,16,128]{3,2,1,0:T(8,128)(2,1)} %get-tuple-element.28), channel_id=1, source_target_pairs={{0,2},{1,3},{2,4},{3,5},{4,6},{5,7},{6,0},{7,1},{8,10},{9,11},{10,... | collective-permute-start | bytes 196616 | tf_op jit(solution)/shard_map/ppermute | solution.py:429
  73.6 2.4 %collective-permute-start.4 = (bf16[2,8,16,128]{3,2,1,0:T(8,128)(2,1)}, bf16[2,8,16,128]{3,2,1,0:T(8,128)(2,1)S(1)}, u32[]{:S(2)}, u32[]{:S(2)}) collective-permute-start(bf16[2,8,16,128]{3,2,1,0:T(8,128)(2,1)} %get-tuple-element.29), channel_id=1, source_target_pairs={{0,6},{1,7},{2,0},{3,1},{4,2},{5,3},{6,4},{7,5},{8,14},{9,15},{10,... | collective-permute-start | bytes 196616 | tf_op jit(solution)/shard_map/ppermute | solution.py:429
  76.0 0.7 collective-permute-start.5
  76.7 1.6 %collective-permute-done.1 = bf16[2,8,16,128]{3,2,1,0:T(8,128)(2,1)S(1)} collective-permute-done((bf16[2,8,16,128]{3,2,1,0:T(8,128)(2,1)}, bf16[2,8,16,128]{3,2,1,0:T(8,128)(2,1)S(1)}, u32[]{:S(2)}, u32[]{:S(2)}) %collective-permute-start.1) | collective-permute-done | bytes 65568 | tf_op jit(solution)/shard_map/ppermute | solution.py:429
  78.3 0.4 collective-permute-start.6
  78.7 0.2 collective-permute-done.3
  78.9 2.3 %collective-permute-done.4 = bf16[2,8,16,128]{3,2,1,0:T(8,128)(2,1)S(1)} collective-permute-done((bf16[2,8,16,128]{3,2,1,0:T(8,128)(2,1)}, bf16[2,8,16,128]{3,2,1,0:T(8,128)(2,1)S(1)}, u32[]{:S(2)}, u32[]{:S(2)}) %collective-permute-start.4) | collective-permute-done | bytes 65568 | tf_op jit(solution)/shard_map/ppermute | solution.py:429
  81.1 2.2 %collective-permute-done.6 = bf16[2,8,16,128]{3,2,1,0:T(8,128)(2,1)S(1)} collective-permute-done((bf16[2,8,16,128]{3,2,1,0:T(8,128)(2,1)}, bf16[2,8,16,128]{3,2,1,0:T(8,128)(2,1)S(1)}, u32[]{:S(2)}, u32[]{:S(2)}) %collective-permute-start.6) | collective-permute-done | bytes 65568 | tf_op jit(solution)/shard_map/ppermute | solution.py:429
  83.4 0.9 convert_add_fusion
  84.3 2.9 %collective-permute-start.7 = (f32[8,2048]{1,0:T(8,128)S(1)}, f32[8,2048]{1,0:T(8,128)S(1)}, u32[]{:S(2)}, u32[]{:S(2)}) collective-permute-start(f32[8,2048]{1,0:T(8,128)S(1)} %bitcast.31), channel_id=1, source_target_pairs={{0,8},{1,9},{2,10},{3,11},{4,12},{5,13},{6,14},{7,15},{8,0},{9,1},... | collective-permute-start | bytes 196616 | tf_op jit(solution)/shard_map/ppermute | solution.py:461
  87.4 3.8 %finish.1 = (bf16[256,2048]{1,0:T(8,128)(2,1)}, bf16[256,2048]{1,0:T(8,128)(2,1)}, bf16[256,2048]{1,0:T(8,128)(2,1)}) custom-call(bf16[16,2,2,8,16,128]{5,4,3,2,1,0:T(8,128)(2,1)} %bitcast.5.tok_ref, bf16[256,2048]{1,0:T(8,128)(2,1)S(1)} %copy-done.1, bf16[256,2048]{1,0:T(8,128)(2,1)} %v_ref.3, bf16[256,2048]{1,0:T(8,128)(2,1)} %g_ref.3, ...), custom_call_target="tpu_custom_call" | custom-call | flops 1572864 | bytes 8388608 | tf_op jit(solution)/shard_map/finish/pallas_call | solution.py:210
  91.2 0.7 bitcast_select_fusion
  (18 shorter events, 0.3 us)
Async XLA Ops:
  0.6 12.9 %copy-start = (f32[16,32768]{1,0:T(8,128)S(1)}, f32[16,32768]{1,0:T(8,128)}, u32[]{:S(2)}) copy-start(f32[16,32768]{1,0:T(8,128)} %param.19) | copy-start | bytes 6291460
  4.8 37.0 %all-to-all-start = ((bf16[32,2,8,16,128]{4,3,2,1,0:T(8,128)(2,1)}), bf16[32,2,8,16,128]{4,3,2,1,0:T(8,128)(2,1)}, u32[]{:S(2)}, u32[]{:S(2)}) async-start(bf16[32,2,8,16,128]{4,3,2,1,0:T(8,128)(2,1)} %bitcast.27), calls=%async_computation | async-start | bytes 4194304 | tf_op jit(solution)/shard_map/all_to_all | solution.py:444
  51.4 36.0 %all-to-all-start.1 = ((bf16[32,2,8,16,128]{4,3,2,1,0:T(8,128)(2,1)}), bf16[32,2,8,16,128]{4,3,2,1,0:T(8,128)(2,1)}, u32[]{:S(2)}, u32[]{:S(2)}) async-start(bf16[32,2,8,16,128]{4,3,2,1,0:T(8,128)(2,1)} %bitcast.28), calls=%async_computation.1 | async-start | bytes 4194304 | tf_op jit(solution)/shard_map/all_to_all | solution.py:444
  56.9 30.5 %copy-start.1 = (bf16[256,2048]{1,0:T(8,128)(2,1)S(1)}, bf16[256,2048]{1,0:T(8,128)(2,1)}, u32[]{:S(2)}) copy-start(bf16[256,2048]{1,0:T(8,128)(2,1)} %k_ref.3) | copy-start | bytes 3145732
  56.9 30.5 %copy-start.2 = (bf16[256,256]{1,0:T(8,128)(2,1)S(1)}, bf16[256,256]{1,0:T(8,128)(2,1)}, u32[]{:S(2)}) copy-start(bf16[256,256]{1,0:T(8,128)(2,1)} %constant.59.clone.swap_hbm.swap_ref) | copy-start | bytes 393220
  60.9 15.1 %collective-permute-start = (bf16[2,8,16,128]{3,2,1,0:T(8,128)(2,1)}, bf16[2,8,16,128]{3,2,1,0:T(8,128)(2,1)S(1)}, u32[]{:S(2)}, u32[]{:S(2)}) collective-permute-start(bf16[2,8,16,128]{3,2,1,0:T(8,128)(2,1)} %get-tuple-element.25), channel_id=1, source_target_pairs={{0,4},{1,5},{2,6},{3,7},{4,0},{5,1},{6,2},{7,3},{8,12},{9,13},{10,... | collective-permute-start | bytes 196616 | tf_op jit(solution)/shard_map/ppermute | solution.py:429
  67.9 10.4 %collective-permute-start.1 = (bf16[2,8,16,128]{3,2,1,0:T(8,128)(2,1)}, bf16[2,8,16,128]{3,2,1,0:T(8,128)(2,1)S(1)}, u32[]{:S(2)}, u32[]{:S(2)}) collective-permute-start(bf16[2,8,16,128]{3,2,1,0:T(8,128)(2,1)} %get-tuple-element.26), channel_id=1, source_target_pairs={{0,3},{1,4},{2,5},{3,6},{4,7},{5,0},{6,1},{7,2},{8,11},{9,12},{10,... | collective-permute-start | bytes 196616 | tf_op jit(solution)/shard_map/ppermute | solution.py:429
  69.6 9.1 %collective-permute-start.2 = (bf16[2,8,16,128]{3,2,1,0:T(8,128)(2,1)}, bf16[2,8,16,128]{3,2,1,0:T(8,128)(2,1)S(1)}, u32[]{:S(2)}, u32[]{:S(2)}) collective-permute-start(bf16[2,8,16,128]{3,2,1,0:T(8,128)(2,1)} %get-tuple-element.27), channel_id=1, source_target_pairs={{0,5},{1,6},{2,7},{3,0},{4,1},{5,2},{6,3},{7,4},{8,13},{9,14},{10,... | collective-permute-start | bytes 196616 | tf_op jit(solution)/shard_map/ppermute | solution.py:429
  72.4 6.5 %collective-permute-start.3 = (bf16[2,8,16,128]{3,2,1,0:T(8,128)(2,1)}, bf16[2,8,16,128]{3,2,1,0:T(8,128)(2,1)S(1)}, u32[]{:S(2)}, u32[]{:S(2)}) collective-permute-start(bf16[2,8,16,128]{3,2,1,0:T(8,128)(2,1)} %get-tuple-element.28), channel_id=1, source_target_pairs={{0,2},{1,3},{2,4},{3,5},{4,6},{5,7},{6,0},{7,1},{8,10},{9,11},{10,... | collective-permute-start | bytes 196616 | tf_op jit(solution)/shard_map/ppermute | solution.py:429
  73.6 7.6 %collective-permute-start.4 = (bf16[2,8,16,128]{3,2,1,0:T(8,128)(2,1)}, bf16[2,8,16,128]{3,2,1,0:T(8,128)(2,1)S(1)}, u32[]{:S(2)}, u32[]{:S(2)}) collective-permute-start(bf16[2,8,16,128]{3,2,1,0:T(8,128)(2,1)} %get-tuple-element.29), channel_id=1, source_target_pairs={{0,6},{1,7},{2,0},{3,1},{4,2},{5,3},{6,4},{7,5},{8,14},{9,15},{10,... | collective-permute-start | bytes 196616 | tf_op jit(solution)/shard_map/ppermute | solution.py:429
  76.0 5.2 %collective-permute-start.5 = (bf16[2,8,16,128]{3,2,1,0:T(8,128)(2,1)}, bf16[2,8,16,128]{3,2,1,0:T(8,128)(2,1)S(1)}, u32[]{:S(2)}, u32[]{:S(2)}) collective-permute-start(bf16[2,8,16,128]{3,2,1,0:T(8,128)(2,1)} %get-tuple-element.30), channel_id=1, source_target_pairs={{0,1},{1,2},{2,3},{3,4},{4,5},{5,6},{6,7},{7,0},{8,9},{9,10},{10,1... | collective-permute-start | bytes 196616 | tf_op jit(solution)/shard_map/ppermute | solution.py:429
  78.3 5.1 %collective-permute-start.6 = (bf16[2,8,16,128]{3,2,1,0:T(8,128)(2,1)}, bf16[2,8,16,128]{3,2,1,0:T(8,128)(2,1)S(1)}, u32[]{:S(2)}, u32[]{:S(2)}) collective-permute-start(bf16[2,8,16,128]{3,2,1,0:T(8,128)(2,1)} %get-tuple-element.31), channel_id=1, source_target_pairs={{0,7},{1,0},{2,1},{3,2},{4,3},{5,4},{6,5},{7,6},{8,15},{9,8},{10,9... | collective-permute-start | bytes 196616 | tf_op jit(solution)/shard_map/ppermute | solution.py:429
  84.3 6.9 %collective-permute-start.7 = (f32[8,2048]{1,0:T(8,128)S(1)}, f32[8,2048]{1,0:T(8,128)S(1)}, u32[]{:S(2)}, u32[]{:S(2)}) collective-permute-start(f32[8,2048]{1,0:T(8,128)S(1)} %bitcast.31), channel_id=1, source_target_pairs={{0,8},{1,9},{2,10},{3,11},{4,12},{5,13},{6,14},{7,15},{8,0},{9,1},... | collective-permute-start | bytes 196616 | tf_op jit(solution)/shard_map/ppermute | solution.py:461

commit v4 on v3

--- a/solution.py
+++ b/solution.py
@@ -362,7 +362,7 @@
             pltpu.SemaphoreType.DMA((steps, 2)),
             pltpu.SemaphoreType.DMA((1, len(tables))),
         ],
-        compiler_params=params(0),
+        compiler_params=params(0, 52 * 2**20),
         cost_estimate=pl.CostEstimate(
             flops=24 * split * kept * rows * LANES * 512, bytes_accessed=8 * x.size, transcendentals=0
         ),

time: 92.3 us -> 91.7 us (level)
  no operation moved by 1% of the time
where the time goes in v4:
time: 91.7 us; the launch traced here: 91.3 us
  starting transfers between devices  33.1 us (36%)
  waiting for transfers between devices  27.8 us (30%)
  Pallas kernels  25.8 us (28%)
  other arithmetic  2.29 us (2%)
  local copies, waits for them, and re-layouts  1.51 us (2%)
    all_to_all x2, waiting for transfers between devices, exchange(): lax.all_to_all(flat, ('ctx', 'tp'), split_axis=0, concat_axis=0, tiled=Tr...  21.5 us
    ppermute x7, starting transfers between devices, sum_scattered(): total = total + lax.ppermute(parts[step], 'tp', pairs).astype(f32)  16.1 us
    all_to_all x2, starting transfers between devices, exchange(): lax.all_to_all(flat, ('ctx', 'tp'), split_axis=0, concat_axis=0, tiled=Tr...  14.1 us
    pallas_call x1, Pallas kernels, channels(): pl.pallas_call(functools.partial(channels_kernel, scale=scale), in_specs=...  8.95 us
    ppermute x7, waiting for transfers between devices, sum_scattered(): total = total + lax.ppermute(parts[step], 'tp', pairs).astype(f32)  6.25 us
    pallas_call x1, Pallas kernels, filter_spectrum(): pl.pallas_call(functools.partial(filter_kernel, scale=scale), grid=(n //...  4.86 us
    pallas_call x1, Pallas kernels, gate(): pl.pallas_call(gate_kernel, in_specs=[ANY] * 5, out_specs=ANY, out_shape=...  4.14 us
    pallas_call x1, Pallas kernels, lags(): pl.pallas_call(lags_kernel, in_specs=[pl.BlockSpec(memory_space=pltpu.SME...  4.01 us
  transfers between devices with their start and end apart: 10, of which 5 were waited for; matrix products, arithmetic and copies ran while one was open for 3% of the time, Pallas kernels for 14%

profile of v4, /device:TPU:1, one launch (start us, length us, event | category | flops | bytes accessed | tf_op | source)
XLA Modules:
  0.0 91.3 jit_solution(17864390296188927669)
XLA Ops:
  0.6 4.1 %gate.1 = bf16[16,2,2,8,16,128]{5,4,3,2,1,0:T(8,128)(2,1)} custom-call(bf16[256,2048]{1,0:T(8,128)(2,1)} %q_ref.1, bf16[256,2048]{1,0:T(8,128)(2,1)} %k_ref.3, bf16[256,2048]{1,0:T(8,128)(2,1)} %v_ref.3, bf16[256,2048]{1,0:T(8,128)(2,1)} %g_ref.3, bf16[256,256]{1,0:T(8,128)(2,1)} %constant.59.clone.swap_hbm.swap_ref), custom_call_target="tpu_custom_call" | custom-call | flops 1048576 | bytes 6291456 | tf_op jit(solution)/shard_map/gate/pallas_call | solution.py:146
  4.8 8.7 %all-to-all-start = ((bf16[32,2,8,16,128]{4,3,2,1,0:T(8,128)(2,1)}), bf16[32,2,8,16,128]{4,3,2,1,0:T(8,128)(2,1)}, u32[]{:S(2)}, u32[]{:S(2)}) async-start(bf16[32,2,8,16,128]{4,3,2,1,0:T(8,128)(2,1)} %bitcast.27), calls=%async_computation | async-start | bytes 4194304 | tf_op jit(solution)/shard_map/all_to_all | solution.py:444
  13.6 1.2 %copy.25 = f32[1,8,256,128]{3,2,1,0:T(8,128)} copy(f32[1,8,256,128]{3,1,2,0:T(8,128)S(1)} %dynamic-slice_bitcast_fusion) | data formatting | bytes 2097152
  14.7 0.6 pad_add_fusion.place_ref
  15.4 4.9 %filter_spectrum.1.f_ref = f32[8,256,256]{2,1,0:T(8,128)} custom-call(f32[8,256,128]{2,1,0:T(8,128)} %bitcast.29, bf16[512,768]{1,0:T(8,128)(2,1)} %constant.51.clone.w_ref, bf16[768,256]{1,0:T(8,128)(2,1)} %constant.52.clone.m_ref, f32[256,128]{1,0:T(8,128)} %constant.57.clone.tc_ref.tc_hbm, f32[256,128]{1,0:T(8,128)} %constant.58.clone.ts_ref.ts_hbm), custom_call_target="tpu_custom_call" | custom-call | flops 1610612736 | bytes 4194304 | tf_op jit(solution)/shard_map/filter_spectrum/pallas_call | solution.py:249
  20.3 21.5 %all-to-all-done = bf16[32,2,8,16,128]{4,3,2,1,0:T(8,128)(2,1)} async-done(((bf16[32,2,8,16,128]{4,3,2,1,0:T(8,128)(2,1)}), bf16[32,2,8,16,128]{4,3,2,1,0:T(8,128)(2,1)}, u32[]{:S(2)}, u32[]{:S(2)}) %all-to-all-start) | async-done | bytes 2097184 | tf_op jit(solution)/shard_map/all_to_all | solution.py:444
  41.8 8.9 %channels.1 = (bf16[8,256,256]{2,1,0:T(8,128)(2,1)}, bf16[16,2,2,8,16,128]{5,4,3,2,1,0:T(8,128)(2,1)}) custom-call(bf16[16,2,2,8,16,128]{5,4,3,2,1,0:T(8,128)(2,1)} %bitcast.3.x_ref, f32[8,256,256]{2,1,0:T(8,128)} %filter_spectrum.1.f_ref, bf16[512,256]{1,0:T(8,128)(2,1)S(1)} %copy-done.4, bf16[256,256]{1,0:T(8,128)(2,1)S(1)} %copy-done.8, ...), custom_call_target="tpu_custom_call" | custom-call | flops 6442450944 | bytes 8388608 | tf_op jit(solution)/shard_map/channels/pallas_call | solution.py:350
  50.8 5.5 %all-to-all-start.1 = ((bf16[32,2,8,16,128]{4,3,2,1,0:T(8,128)(2,1)}), bf16[32,2,8,16,128]{4,3,2,1,0:T(8,128)(2,1)}, u32[]{:S(2)}, u32[]{:S(2)}) async-start(bf16[32,2,8,16,128]{4,3,2,1,0:T(8,128)(2,1)} %bitcast.28), calls=%async_computation.1 | async-start | bytes 4194304 | tf_op jit(solution)/shard_map/all_to_all | solution.py:444
  56.3 4.0 %lags.1 = (bf16[2,8,16,128]{3,2,1,0:T(8,128)(2,1)}, bf16[2,8,16,128]{3,2,1,0:T(8,128)(2,1)}, bf16[2,8,16,128]{3,2,1,0:T(8,128)(2,1)}, bf16[2,8,16,128]{3,2,1,0:T...) custom-call(s32[2]{0:T(128)} %pad_add_fusion.place_ref, ...), custom_call_target="tpu_custom_call" | custom-call | flops 1610612736 | bytes 2097152 | tf_op jit(solution)/shard_map/lags/pallas_call | solution.py:400
  60.3 7.0 %collective-permute-start = (bf16[2,8,16,128]{3,2,1,0:T(8,128)(2,1)}, bf16[2,8,16,128]{3,2,1,0:T(8,128)(2,1)S(1)}, u32[]{:S(2)}, u32[]{:S(2)}) collective-permute-start(bf16[2,8,16,128]{3,2,1,0:T(8,128)(2,1)} %get-tuple-element.25), channel_id=1, source_target_pairs={{0,4},{1,5},{2,6},{3,7},{4,0},{5,1},{6,2},{7,3},{8,12},{9,13},{10,... | collective-permute-start | bytes 196616 | tf_op jit(solution)/shard_map/ppermute | solution.py:429
  67.3 1.6 %collective-permute-start.1 = (bf16[2,8,16,128]{3,2,1,0:T(8,128)(2,1)}, bf16[2,8,16,128]{3,2,1,0:T(8,128)(2,1)S(1)}, u32[]{:S(2)}, u32[]{:S(2)}) collective-permute-start(bf16[2,8,16,128]{3,2,1,0:T(8,128)(2,1)} %get-tuple-element.26), channel_id=1, source_target_pairs={{0,3},{1,4},{2,5},{3,6},{4,7},{5,0},{6,1},{7,2},{8,11},{9,12},{10,... | collective-permute-start | bytes 196616 | tf_op jit(solution)/shard_map/ppermute | solution.py:429
  69.0 2.8 %collective-permute-start.2 = (bf16[2,8,16,128]{3,2,1,0:T(8,128)(2,1)}, bf16[2,8,16,128]{3,2,1,0:T(8,128)(2,1)S(1)}, u32[]{:S(2)}, u32[]{:S(2)}) collective-permute-start(bf16[2,8,16,128]{3,2,1,0:T(8,128)(2,1)} %get-tuple-element.27), channel_id=1, source_target_pairs={{0,5},{1,6},{2,7},{3,0},{4,1},{5,2},{6,3},{7,4},{8,13},{9,14},{10,... | collective-permute-start | bytes 196616 | tf_op jit(solution)/shard_map/ppermute | solution.py:429
  71.8 1.2 %collective-permute-start.3 = (bf16[2,8,16,128]{3,2,1,0:T(8,128)(2,1)}, bf16[2,8,16,128]{3,2,1,0:T(8,128)(2,1)S(1)}, u32[]{:S(2)}, u32[]{:S(2)}) collective-permute-start(bf16[2,8,16,128]{3,2,1,0:T(8,128)(2,1)} %get-tuple-element.28), channel_id=1, source_target_pairs={{0,2},{1,3},{2,4},{3,5},{4,6},{5,7},{6,0},{7,1},{8,10},{9,11},{10,... | collective-permute-start | bytes 196616 | tf_op jit(solution)/shard_map/ppermute | solution.py:429
  73.0 2.4 %collective-permute-start.4 = (bf16[2,8,16,128]{3,2,1,0:T(8,128)(2,1)}, bf16[2,8,16,128]{3,2,1,0:T(8,128)(2,1)S(1)}, u32[]{:S(2)}, u32[]{:S(2)}) collective-permute-start(bf16[2,8,16,128]{3,2,1,0:T(8,128)(2,1)} %get-tuple-element.29), channel_id=1, source_target_pairs={{0,6},{1,7},{2,0},{3,1},{4,2},{5,3},{6,4},{7,5},{8,14},{9,15},{10,... | collective-permute-start | bytes 196616 | tf_op jit(solution)/shard_map/ppermute | solution.py:429
  75.4 0.7 collective-permute-start.5
  76.1 1.6 %collective-permute-done.1 = bf16[2,8,16,128]{3,2,1,0:T(8,128)(2,1)S(1)} collective-permute-done((bf16[2,8,16,128]{3,2,1,0:T(8,128)(2,1)}, bf16[2,8,16,128]{3,2,1,0:T(8,128)(2,1)S(1)}, u32[]{:S(2)}, u32[]{:S(2)}) %collective-permute-start.1) | collective-permute-done | bytes 65568 | tf_op jit(solution)/shard_map/ppermute | solution.py:429
  77.7 0.4 collective-permute-start.6
  78.1 0.2 collective-permute-done.3
  78.3 2.2 %collective-permute-done.4 = bf16[2,8,16,128]{3,2,1,0:T(8,128)(2,1)S(1)} collective-permute-done((bf16[2,8,16,128]{3,2,1,0:T(8,128)(2,1)}, bf16[2,8,16,128]{3,2,1,0:T(8,128)(2,1)S(1)}, u32[]{:S(2)}, u32[]{:S(2)}) %collective-permute-start.4) | collective-permute-done | bytes 65568 | tf_op jit(solution)/shard_map/ppermute | solution.py:429
  80.5 2.3 %collective-permute-done.6 = bf16[2,8,16,128]{3,2,1,0:T(8,128)(2,1)S(1)} collective-permute-done((bf16[2,8,16,128]{3,2,1,0:T(8,128)(2,1)}, bf16[2,8,16,128]{3,2,1,0:T(8,128)(2,1)S(1)}, u32[]{:S(2)}, u32[]{:S(2)}) %collective-permute-start.6) | collective-permute-done | bytes 65568 | tf_op jit(solution)/shard_map/ppermute | solution.py:429
  82.7 0.9 convert_add_fusion
  83.7 2.8 %collective-permute-start.7 = (f32[8,2048]{1,0:T(8,128)S(1)}, f32[8,2048]{1,0:T(8,128)S(1)}, u32[]{:S(2)}, u32[]{:S(2)}) collective-permute-start(f32[8,2048]{1,0:T(8,128)S(1)} %bitcast.31), channel_id=1, source_target_pairs={{0,8},{1,9},{2,10},{3,11},{4,12},{5,13},{6,14},{7,15},{8,0},{9,1},... | collective-permute-start | bytes 196616 | tf_op jit(solution)/shard_map/ppermute | solution.py:461
  86.8 3.8 %finish.1 = (bf16[256,2048]{1,0:T(8,128)(2,1)}, bf16[256,2048]{1,0:T(8,128)(2,1)}, bf16[256,2048]{1,0:T(8,128)(2,1)}) custom-call(bf16[16,2,2,8,16,128]{5,4,3,2,1,0:T(8,128)(2,1)} %bitcast.5.tok_ref, bf16[256,2048]{1,0:T(8,128)(2,1)S(1)} %copy-done.1, bf16[256,2048]{1,0:T(8,128)(2,1)} %v_ref.3, bf16[256,2048]{1,0:T(8,128)(2,1)} %g_ref.3, ...), custom_call_target="tpu_custom_call" | custom-call | flops 1572864 | bytes 8388608 | tf_op jit(solution)/shard_map/finish/pallas_call | solution.py:210
  90.6 0.7 bitcast_select_fusion
  (30 shorter events, 0.4 us)
Async XLA Ops:
  0.6 12.9 %copy-start = (f32[16,32768]{1,0:T(8,128)S(1)}, f32[16,32768]{1,0:T(8,128)}, u32[]{:S(2)}) copy-start(f32[16,32768]{1,0:T(8,128)} %param.19) | copy-start | bytes 6291460
  4.8 37.0 %all-to-all-start = ((bf16[32,2,8,16,128]{4,3,2,1,0:T(8,128)(2,1)}), bf16[32,2,8,16,128]{4,3,2,1,0:T(8,128)(2,1)}, u32[]{:S(2)}, u32[]{:S(2)}) async-start(bf16[32,2,8,16,128]{4,3,2,1,0:T(8,128)(2,1)} %bitcast.27), calls=%async_computation | async-start | bytes 4194304 | tf_op jit(solution)/shard_map/all_to_all | solution.py:444
  15.4 26.4 %copy-start.3 = (bf16[256,512]{1,0:T(8,128)(2,1)S(1)}, bf16[256,512]{1,0:T(8,128)(2,1)}, u32[]{:S(2)}) copy-start(bf16[256,512]{1,0:T(8,128)(2,1)} %constant.56.clone.wi_hbm) | copy-start | bytes 786436
  15.4 26.4 %copy-start.4 = (bf16[512,256]{1,0:T(8,128)(2,1)S(1)}, bf16[512,256]{1,0:T(8,128)(2,1)}, u32[]{:S(2)}) copy-start(bf16[512,256]{1,0:T(8,128)(2,1)} %constant.53.clone.w_hbm) | copy-start | bytes 786436
  15.4 26.4 %copy-start.5 = (f32[256,128]{1,0:T(8,128)S(1)}, f32[256,128]{1,0:T(8,128)}, u32[]{:S(2)}) copy-start(f32[256,128]{1,0:T(8,128)} %constant.58.clone.ts_ref.ts_hbm) | copy-start | bytes 393220
  15.4 26.4 %copy-start.6 = (f32[256,128]{1,0:T(8,128)S(1)}, f32[256,128]{1,0:T(8,128)}, u32[]{:S(2)}) copy-start(f32[256,128]{1,0:T(8,128)} %constant.57.clone.tc_ref.tc_hbm) | copy-start | bytes 393220
  15.4 26.4 %copy-start.7 = (bf16[256,256]{1,0:T(8,128)(2,1)S(1)}, bf16[256,256]{1,0:T(8,128)(2,1)}, u32[]{:S(2)}) copy-start(bf16[256,256]{1,0:T(8,128)(2,1)} %constant.55.clone.mi_hbm) | copy-start | bytes 393220
  15.4 26.4 %copy-start.8 = (bf16[256,256]{1,0:T(8,128)(2,1)S(1)}, bf16[256,256]{1,0:T(8,128)(2,1)}, u32[]{:S(2)}) copy-start(bf16[256,256]{1,0:T(8,128)(2,1)} %constant.54.clone.m_hbm) | copy-start | bytes 393220
  50.8 35.9 %all-to-all-start.1 = ((bf16[32,2,8,16,128]{4,3,2,1,0:T(8,128)(2,1)}), bf16[32,2,8,16,128]{4,3,2,1,0:T(8,128)(2,1)}, u32[]{:S(2)}, u32[]{:S(2)}) async-start(bf16[32,2,8,16,128]{4,3,2,1,0:T(8,128)(2,1)} %bitcast.28), calls=%async_computation.1 | async-start | bytes 4194304 | tf_op jit(solution)/shard_map/all_to_all | solution.py:444
  56.3 30.5 %copy-start.1 = (bf16[256,2048]{1,0:T(8,128)(2,1)S(1)}, bf16[256,2048]{1,0:T(8,128)(2,1)}, u32[]{:S(2)}) copy-start(bf16[256,2048]{1,0:T(8,128)(2,1)} %k_ref.3) | copy-start | bytes 3145732
  56.3 30.5 %copy-start.2 = (bf16[256,256]{1,0:T(8,128)(2,1)S(1)}, bf16[256,256]{1,0:T(8,128)(2,1)}, u32[]{:S(2)}) copy-start(bf16[256,256]{1,0:T(8,128)(2,1)} %constant.59.clone.swap_hbm.swap_ref) | copy-start | bytes 393220
  60.3 15.1 %collective-permute-start = (bf16[2,8,16,128]{3,2,1,0:T(8,128)(2,1)}, bf16[2,8,16,128]{3,2,1,0:T(8,128)(2,1)S(1)}, u32[]{:S(2)}, u32[]{:S(2)}) collective-permute-start(bf16[2,8,16,128]{3,2,1,0:T(8,128)(2,1)} %get-tuple-element.25), channel_id=1, source_target_pairs={{0,4},{1,5},{2,6},{3,7},{4,0},{5,1},{6,2},{7,3},{8,12},{9,13},{10,... | collective-permute-start | bytes 196616 | tf_op jit(solution)/shard_map/ppermute | solution.py:429
  67.3 10.4 %collective-permute-start.1 = (bf16[2,8,16,128]{3,2,1,0:T(8,128)(2,1)}, bf16[2,8,16,128]{3,2,1,0:T(8,128)(2,1)S(1)}, u32[]{:S(2)}, u32[]{:S(2)}) collective-permute-start(bf16[2,8,16,128]{3,2,1,0:T(8,128)(2,1)} %get-tuple-element.26), channel_id=1, source_target_pairs={{0,3},{1,4},{2,5},{3,6},{4,7},{5,0},{6,1},{7,2},{8,11},{9,12},{10,... | collective-permute-start | bytes 196616 | tf_op jit(solution)/shard_map/ppermute | solution.py:429
  69.0 9.1 %collective-permute-start.2 = (bf16[2,8,16,128]{3,2,1,0:T(8,128)(2,1)}, bf16[2,8,16,128]{3,2,1,0:T(8,128)(2,1)S(1)}, u32[]{:S(2)}, u32[]{:S(2)}) collective-permute-start(bf16[2,8,16,128]{3,2,1,0:T(8,128)(2,1)} %get-tuple-element.27), channel_id=1, source_target_pairs={{0,5},{1,6},{2,7},{3,0},{4,1},{5,2},{6,3},{7,4},{8,13},{9,14},{10,... | collective-permute-start | bytes 196616 | tf_op jit(solution)/shard_map/ppermute | solution.py:429
  71.8 6.5 %collective-permute-start.3 = (bf16[2,8,16,128]{3,2,1,0:T(8,128)(2,1)}, bf16[2,8,16,128]{3,2,1,0:T(8,128)(2,1)S(1)}, u32[]{:S(2)}, u32[]{:S(2)}) collective-permute-start(bf16[2,8,16,128]{3,2,1,0:T(8,128)(2,1)} %get-tuple-element.28), channel_id=1, source_target_pairs={{0,2},{1,3},{2,4},{3,5},{4,6},{5,7},{6,0},{7,1},{8,10},{9,11},{10,... | collective-permute-start | bytes 196616 | tf_op jit(solution)/shard_map/ppermute | solution.py:429
  73.0 7.5 %collective-permute-start.4 = (bf16[2,8,16,128]{3,2,1,0:T(8,128)(2,1)}, bf16[2,8,16,128]{3,2,1,0:T(8,128)(2,1)S(1)}, u32[]{:S(2)}, u32[]{:S(2)}) collective-permute-start(bf16[2,8,16,128]{3,2,1,0:T(8,128)(2,1)} %get-tuple-element.29), channel_id=1, source_target_pairs={{0,6},{1,7},{2,0},{3,1},{4,2},{5,3},{6,4},{7,5},{8,14},{9,15},{10,... | collective-permute-start | bytes 196616 | tf_op jit(solution)/shard_map/ppermute | solution.py:429
  75.4 5.1 %collective-permute-start.5 = (bf16[2,8,16,128]{3,2,1,0:T(8,128)(2,1)}, bf16[2,8,16,128]{3,2,1,0:T(8,128)(2,1)S(1)}, u32[]{:S(2)}, u32[]{:S(2)}) collective-permute-start(bf16[2,8,16,128]{3,2,1,0:T(8,128)(2,1)} %get-tuple-element.30), channel_id=1, source_target_pairs={{0,1},{1,2},{2,3},{3,4},{4,5},{5,6},{6,7},{7,0},{8,9},{9,10},{10,1... | collective-permute-start | bytes 196616 | tf_op jit(solution)/shard_map/ppermute | solution.py:429
  77.7 5.0 %collective-permute-start.6 = (bf16[2,8,16,128]{3,2,1,0:T(8,128)(2,1)}, bf16[2,8,16,128]{3,2,1,0:T(8,128)(2,1)S(1)}, u32[]{:S(2)}, u32[]{:S(2)}) collective-permute-start(bf16[2,8,16,128]{3,2,1,0:T(8,128)(2,1)} %get-tuple-element.31), channel_id=1, source_target_pairs={{0,7},{1,0},{2,1},{3,2},{4,3},{5,4},{6,5},{7,6},{8,15},{9,8},{10,9... | collective-permute-start | bytes 196616 | tf_op jit(solution)/shard_map/ppermute | solution.py:429
  83.7 6.9 %collective-permute-start.7 = (f32[8,2048]{1,0:T(8,128)S(1)}, f32[8,2048]{1,0:T(8,128)S(1)}, u32[]{:S(2)}, u32[]{:S(2)}) collective-permute-start(f32[8,2048]{1,0:T(8,128)S(1)} %bitcast.31), channel_id=1, source_target_pairs={{0,8},{1,9},{2,10},{3,11},{4,12},{5,13},{6,14},{7,15},{8,0},{9,1},... | collective-permute-start | bytes 196616 | tf_op jit(solution)/shard_map/ppermute | solution.py:461

commit v5 on v4

--- a/solution.py
+++ b/solution.py
@@ -273,14 +273,10 @@
     return dot(wi_ref[...], jnp.concatenate([v] * parts, 0))
 
 
-def product(ar, ai, br, bi):
-    return jnp.concatenate([ar * br - ai * bi, ar * bi + ai * br], 1)
-
-
 def channels_kernel(
     x_ref, f_ref, w_hbm, m_hbm, tc_hbm, ts_hbm, mi_hbm, wi_hbm, cross_ref, out_ref,
     x_buf, f_buf, cross_buf, out_buf, w_ref, m_ref, tc_ref, ts_ref, mi_ref, wi_ref,
-    in_sems, out_sems, table_sems, *, scale,
+    in_sems, out_sems, table_sems,
 ):
     n, split, _, kept, cuts, _ = x_ref.shape
     steps, count = f_buf.shape[:2]
@@ -309,37 +305,37 @@
     @pl.loop(0, steps)
     def _(step):
         wait(loads(step))
-        places = [(s, m, i) for s in range(2) for m in range(split) for i in range(count)]
-        x = jnp.concatenate([x_buf[step, :, m, s, i].reshape(rows, LANES) for s, m, i in places], 1)
-        stage = dot(w_ref[...], x)
-        u = jnp.concatenate(
-            [turned(stage, tc_ref[...], ts_ref[...], rows, i).astype(bf16) for i in range(len(places))], 0
-        )
-        spec = dot(u, m_ref[...])
-        block = count * rows
-        half = split * block
-        f = f_buf[step].reshape(block, 2 * LANES)
-        fr, fi = f[:, :LANES], f[:, LANES:]
-        convs, dgateds, cross = [], [], 0.0
-        for m in range(split):
-            at = m * block
-            gr, gi = spec[at : at + block, :LANES], spec[at : at + block, LANES:]
-            dr, di = spec[half + at : half + at + block, :LANES], spec[half + at : half + at + block, LANES:]
-            convs.append(product(fr, fi, gr, gi).astype(bf16))
-            dgateds.append(product(fr, -fi, dr, di).astype(bf16))
-            cross = cross + product(gr, -gi, dr, di)
-        cross_buf[step] = (cross * scale).astype(bf16).reshape(count, rows, 2 * LANES)
-        made = back(jnp.concatenate(convs + dgateds, 0), mi_ref, wi_ref, tc_ref[...], ts_ref[...], len(places), rows)
+        places = [(m, i) for i in range(count) for m in range(split)]
+        us = []
+        for m, i in places:
+            x = jnp.concatenate([x_buf[step, :, m, s, i].reshape(rows, LANES) for s in range(2)], 1)
+            stage = dot(w_ref[...], x)
+            us += [turned(stage, tc_ref[...], ts_ref[...], rows, s).astype(bf16) for s in range(2)]
+        spec = dot(jnp.concatenate(us, 0), m_ref[...])
+        parts, cross = [], []
+        for at, (m, i) in enumerate(places):
+            fr, fi = f_buf[step, i, :, :LANES], f_buf[step, i, :, LANES:]
+            g, d = (spec[(2 * at + s) * rows : (2 * at + s + 1) * rows] for s in range(2))
+            gr, gi, dr, di = g[:, :LANES], g[:, LANES:], d[:, :LANES], d[:, LANES:]
+            cross.append((dr * gr + di * gi, di * gr - dr * gi))
+            parts.append(jnp.concatenate([fr * gr - fi * gi, fr * gi + fi * gr], 1).astype(bf16))
+            parts.append(jnp.concatenate([dr * fr + di * fi, di * fr - dr * fi], 1).astype(bf16))
+        for i in range(count):
+            terms = zip(*cross[i * split : (i + 1) * split])
+            cross_buf[step, i] = jnp.concatenate([sum(part) for part in terms], 1).astype(bf16)
+        made = back(jnp.concatenate(parts, 0), mi_ref, wi_ref, tc_ref[...], ts_ref[...], len(parts), rows)
         made = made.astype(bf16)
-        for at, (s, m, i) in enumerate(places):
-            out_buf[step, :, m, s, i] = made[:, at * LANES : (at + 1) * LANES].reshape(n, cuts, LANES)
+        for at, (m, i) in enumerate(places):
+            for s in range(2):
+                lanes = slice((2 * at + s) * LANES, (2 * at + s + 1) * LANES)
+                out_buf[step, :, m, s, i] = made[:, lanes].reshape(n, cuts, LANES)
         start(stores(step))
 
     for step in range(steps):
         wait(stores(step))
 
 
-def channels(x, f, t, scale):
+def channels(x, f, t):
     n, split, _, kept, cuts, _ = x.shape
     rows = n * cuts
     count = FILTERS
@@ -348,7 +344,7 @@
     spec = (count, rows, 2 * LANES)
     block = (steps, n, split, 2, count, cuts, LANES)
     return pl.pallas_call(
-        functools.partial(channels_kernel, scale=scale),
+        channels_kernel,
         in_specs=[ANY] * (2 + len(tables)),
         out_specs=[ANY] * 2,
         out_shape=[jax.ShapeDtypeStruct((kept, rows, 2 * LANES), bf16), jax.ShapeDtypeStruct(x.shape, bf16)],
@@ -370,7 +366,7 @@
     )(x, f, *tables)
 
 
-def lags_kernel(place_ref, spec_ref, mi_hbm, wi_hbm, tc_hbm, ts_hbm, *refs):
+def lags_kernel(place_ref, spec_ref, mi_hbm, wi_hbm, tc_hbm, ts_hbm, *refs, scale):
     *out_refs, spec, out_buf, mi_ref, wi_ref, tc_ref, ts_ref, in_sems, out_sems = refs
     ring, halves, kept, cuts, _ = out_buf.shape
     rows = spec.shape[1]
@@ -380,7 +376,7 @@
     start(moves)
     wait(moves)
     out = back(spec[...].reshape(kept * rows, 2 * LANES), mi_ref, wi_ref, tc_ref[...], ts_ref[...], kept, rows)
-    out = out.astype(bf16)
+    out = (out * scale).astype(bf16)
     for place in range(ring * halves):
         at = place * cuts
         z, half = order(place, ring * halves)
@@ -392,13 +388,13 @@
     wait(moves)
 
 
-def lags(place, spec, t, n_tp, cuts):
+def lags(place, spec, t, scale, n_tp, cuts):
     kept, rows, _ = spec.shape
     tables = [t[k] for k in (*CROSS_BACK, "turn_cos", "turn_sin")]
     ring = n_tp // SPLIT
     out = (SPLIT, kept, cuts, LANES)
     return pl.pallas_call(
-        lags_kernel,
+        functools.partial(lags_kernel, scale=scale),
         in_specs=[pl.BlockSpec(memory_space=pltpu.SMEM)] + [ANY] * (1 + len(tables)),
         out_specs=[ANY] * ring,
         out_shape=[jax.ShapeDtypeStruct(out, bf16)] * ring,
@@ -453,9 +449,9 @@
     filters = lax.dynamic_slice_in_dim(filter_raw, half * kept, kept, 0)
     filt = filter_spectrum(filters.reshape(kept, rows, LANES), t, root / length)
     filt, where = lax.optimization_barrier((filt, where))
-    cross, made = channels(got, filt, t, root / length)
+    cross, made = channels(got, filt, t)
     tok = exchange(made)
-    parts = lags(where, cross, t, n_tp, rows // n_ctx)
+    parts = lags(where, cross, t, root / length, n_tp, rows // n_ctx)
     total = sum_scattered(parts, n_tp)
     total = total.reshape(SPLIT, kept, length // n_tp)
     far = lax.ppermute(total[1], "tp", [(i, (i + ring) % n_tp) for i in range(n_tp)])

time: 91.7 us -> 91.5 us (level)
  no operation moved by 1% of the time
where the time goes in v5:
time: 91.5 us; the launch traced here: 91.1 us
  starting transfers between devices  33.1 us (36%)
  waiting for transfers between devices  27.8 us (30%)
  Pallas kernels  25.5 us (28%)
  other arithmetic  2.29 us (3%)
  local copies, waits for them, and re-layouts  1.51 us (2%)
    all_to_all x2, waiting for transfers between devices, exchange(): lax.all_to_all(flat, ('ctx', 'tp'), split_axis=0, concat_axis=0, tiled=Tr...  21.5 us
    ppermute x7, starting transfers between devices, sum_scattered(): total = total + lax.ppermute(parts[step], 'tp', pairs).astype(f32)  16.1 us
    all_to_all x2, starting transfers between devices, exchange(): lax.all_to_all(flat, ('ctx', 'tp'), split_axis=0, concat_axis=0, tiled=Tr...  14.1 us
    pallas_call x1, Pallas kernels, channels(): pl.pallas_call(channels_kernel, in_specs=[ANY] * (2 + len(tables)), out_s...  8.71 us
    ppermute x7, waiting for transfers between devices, sum_scattered(): total = total + lax.ppermute(parts[step], 'tp', pairs).astype(f32)  6.3 us
    pallas_call x1, Pallas kernels, filter_spectrum(): pl.pallas_call(functools.partial(filter_kernel, scale=scale), grid=(n //...  4.86 us
    pallas_call x1, Pallas kernels, gate(): pl.pallas_call(gate_kernel, in_specs=[ANY] * 5, out_specs=ANY, out_shape=...  4.14 us
    pallas_call x1, Pallas kernels, lags(): pl.pallas_call(functools.partial(lags_kernel, scale=scale), in_specs=[pl....  4.01 us
  transfers between devices with their start and end apart: 10, of which 5 were waited for; matrix products, arithmetic and copies ran while one was open for 3% of the time, Pallas kernels for 14%

profile of v5, /device:TPU:1, one launch (start us, length us, event | category | flops | bytes accessed | tf_op | source)
XLA Modules:
  0.0 91.1 jit_solution(3993728551509579300)
XLA Ops:
  0.6 4.1 %gate.1 = bf16[16,2,2,8,16,128]{5,4,3,2,1,0:T(8,128)(2,1)} custom-call(bf16[256,2048]{1,0:T(8,128)(2,1)} %q_ref.1, bf16[256,2048]{1,0:T(8,128)(2,1)} %k_ref.3, bf16[256,2048]{1,0:T(8,128)(2,1)} %v_ref.3, bf16[256,2048]{1,0:T(8,128)(2,1)} %g_ref.3, bf16[256,256]{1,0:T(8,128)(2,1)} %constant.59.clone.swap_hbm.swap_ref), custom_call_target="tpu_custom_call" | custom-call | flops 1048576 | bytes 6291456 | tf_op jit(solution)/shard_map/gate/pallas_call | solution.py:146
  4.8 8.7 %all-to-all-start = ((bf16[32,2,8,16,128]{4,3,2,1,0:T(8,128)(2,1)}), bf16[32,2,8,16,128]{4,3,2,1,0:T(8,128)(2,1)}, u32[]{:S(2)}, u32[]{:S(2)}) async-start(bf16[32,2,8,16,128]{4,3,2,1,0:T(8,128)(2,1)} %bitcast.27), calls=%async_computation | async-start | bytes 4194304 | tf_op jit(solution)/shard_map/all_to_all | solution.py:440
  13.6 1.2 %copy.25 = f32[1,8,256,128]{3,2,1,0:T(8,128)} copy(f32[1,8,256,128]{3,1,2,0:T(8,128)S(1)} %dynamic-slice_bitcast_fusion) | data formatting | bytes 2097152
  14.7 0.6 pad_add_fusion.place_ref
  15.4 4.9 %filter_spectrum.1.f_ref = f32[8,256,256]{2,1,0:T(8,128)} custom-call(f32[8,256,128]{2,1,0:T(8,128)} %bitcast.29, bf16[512,768]{1,0:T(8,128)(2,1)} %constant.51.clone.w_ref, bf16[768,256]{1,0:T(8,128)(2,1)} %constant.52.clone.m_ref, f32[256,128]{1,0:T(8,128)} %constant.57.clone.tc_ref.tc_hbm, f32[256,128]{1,0:T(8,128)} %constant.58.clone.ts_ref.ts_hbm), custom_call_target="tpu_custom_call" | custom-call | flops 1610612736 | bytes 4194304 | tf_op jit(solution)/shard_map/filter_spectrum/pallas_call | solution.py:249
  20.3 21.5 %all-to-all-done = bf16[32,2,8,16,128]{4,3,2,1,0:T(8,128)(2,1)} async-done(((bf16[32,2,8,16,128]{4,3,2,1,0:T(8,128)(2,1)}), bf16[32,2,8,16,128]{4,3,2,1,0:T(8,128)(2,1)}, u32[]{:S(2)}, u32[]{:S(2)}) %all-to-all-start) | async-done | bytes 2097184 | tf_op jit(solution)/shard_map/all_to_all | solution.py:440
  41.8 8.7 %channels.1 = (bf16[8,256,256]{2,1,0:T(8,128)(2,1)}, bf16[16,2,2,8,16,128]{5,4,3,2,1,0:T(8,128)(2,1)}) custom-call(bf16[16,2,2,8,16,128]{5,4,3,2,1,0:T(8,128)(2,1)} %bitcast.3.x_ref, f32[8,256,256]{2,1,0:T(8,128)} %filter_spectrum.1.f_ref, bf16[512,256]{1,0:T(8,128)(2,1)S(1)} %copy-done.4, bf16[256,256]{1,0:T(8,128)(2,1)S(1)} %copy-done.8, ...), custom_call_target="tpu_custom_call" | custom-call | flops 6442450944 | bytes 8388608 | tf_op jit(solution)/shard_map/channels/pallas_call | solution.py:346
  50.6 5.5 %all-to-all-start.1 = ((bf16[32,2,8,16,128]{4,3,2,1,0:T(8,128)(2,1)}), bf16[32,2,8,16,128]{4,3,2,1,0:T(8,128)(2,1)}, u32[]{:S(2)}, u32[]{:S(2)}) async-start(bf16[32,2,8,16,128]{4,3,2,1,0:T(8,128)(2,1)} %bitcast.28), calls=%async_computation.1 | async-start | bytes 4194304 | tf_op jit(solution)/shard_map/all_to_all | solution.py:440
  56.1 4.0 %lags.1 = (bf16[2,8,16,128]{3,2,1,0:T(8,128)(2,1)}, bf16[2,8,16,128]{3,2,1,0:T(8,128)(2,1)}, bf16[2,8,16,128]{3,2,1,0:T(8,128)(2,1)}, bf16[2,8,16,128]{3,2,1,0:T...) custom-call(s32[2]{0:T(128)} %pad_add_fusion.place_ref, ...), custom_call_target="tpu_custom_call" | custom-call | flops 1610612736 | bytes 2097152 | tf_op jit(solution)/shard_map/lags/pallas_call | solution.py:396
  60.1 7.0 %collective-permute-start = (bf16[2,8,16,128]{3,2,1,0:T(8,128)(2,1)}, bf16[2,8,16,128]{3,2,1,0:T(8,128)(2,1)S(1)}, u32[]{:S(2)}, u32[]{:S(2)}) collective-permute-start(bf16[2,8,16,128]{3,2,1,0:T(8,128)(2,1)} %get-tuple-element.25), channel_id=1, source_target_pairs={{0,4},{1,5},{2,6},{3,7},{4,0},{5,1},{6,2},{7,3},{8,12},{9,13},{10,... | collective-permute-start | bytes 196616 | tf_op jit(solution)/shard_map/ppermute | solution.py:425
  67.1 1.6 %collective-permute-start.1 = (bf16[2,8,16,128]{3,2,1,0:T(8,128)(2,1)}, bf16[2,8,16,128]{3,2,1,0:T(8,128)(2,1)S(1)}, u32[]{:S(2)}, u32[]{:S(2)}) collective-permute-start(bf16[2,8,16,128]{3,2,1,0:T(8,128)(2,1)} %get-tuple-element.26), channel_id=1, source_target_pairs={{0,3},{1,4},{2,5},{3,6},{4,7},{5,0},{6,1},{7,2},{8,11},{9,12},{10,... | collective-permute-start | bytes 196616 | tf_op jit(solution)/shard_map/ppermute | solution.py:425
  68.7 2.8 %collective-permute-start.2 = (bf16[2,8,16,128]{3,2,1,0:T(8,128)(2,1)}, bf16[2,8,16,128]{3,2,1,0:T(8,128)(2,1)S(1)}, u32[]{:S(2)}, u32[]{:S(2)}) collective-permute-start(bf16[2,8,16,128]{3,2,1,0:T(8,128)(2,1)} %get-tuple-element.27), channel_id=1, source_target_pairs={{0,5},{1,6},{2,7},{3,0},{4,1},{5,2},{6,3},{7,4},{8,13},{9,14},{10,... | collective-permute-start | bytes 196616 | tf_op jit(solution)/shard_map/ppermute | solution.py:425
  71.6 1.2 %collective-permute-start.3 = (bf16[2,8,16,128]{3,2,1,0:T(8,128)(2,1)}, bf16[2,8,16,128]{3,2,1,0:T(8,128)(2,1)S(1)}, u32[]{:S(2)}, u32[]{:S(2)}) collective-permute-start(bf16[2,8,16,128]{3,2,1,0:T(8,128)(2,1)} %get-tuple-element.28), channel_id=1, source_target_pairs={{0,2},{1,3},{2,4},{3,5},{4,6},{5,7},{6,0},{7,1},{8,10},{9,11},{10,... | collective-permute-start | bytes 196616 | tf_op jit(solution)/shard_map/ppermute | solution.py:425
  72.8 2.4 %collective-permute-start.4 = (bf16[2,8,16,128]{3,2,1,0:T(8,128)(2,1)}, bf16[2,8,16,128]{3,2,1,0:T(8,128)(2,1)S(1)}, u32[]{:S(2)}, u32[]{:S(2)}) collective-permute-start(bf16[2,8,16,128]{3,2,1,0:T(8,128)(2,1)} %get-tuple-element.29), channel_id=1, source_target_pairs={{0,6},{1,7},{2,0},{3,1},{4,2},{5,3},{6,4},{7,5},{8,14},{9,15},{10,... | collective-permute-start | bytes 196616 | tf_op jit(solution)/shard_map/ppermute | solution.py:425
  75.1 0.7 collective-permute-start.5
  75.9 1.6 %collective-permute-done.1 = bf16[2,8,16,128]{3,2,1,0:T(8,128)(2,1)S(1)} collective-permute-done((bf16[2,8,16,128]{3,2,1,0:T(8,128)(2,1)}, bf16[2,8,16,128]{3,2,1,0:T(8,128)(2,1)S(1)}, u32[]{:S(2)}, u32[]{:S(2)}) %collective-permute-start.1) | collective-permute-done | bytes 65568 | tf_op jit(solution)/shard_map/ppermute | solution.py:425
  77.5 0.4 collective-permute-start.6
  77.8 0.2 collective-permute-done.3
  78.0 2.3 %collective-permute-done.4 = bf16[2,8,16,128]{3,2,1,0:T(8,128)(2,1)S(1)} collective-permute-done((bf16[2,8,16,128]{3,2,1,0:T(8,128)(2,1)}, bf16[2,8,16,128]{3,2,1,0:T(8,128)(2,1)S(1)}, u32[]{:S(2)}, u32[]{:S(2)}) %collective-permute-start.4) | collective-permute-done | bytes 65568 | tf_op jit(solution)/shard_map/ppermute | solution.py:425
  80.3 2.2 %collective-permute-done.6 = bf16[2,8,16,128]{3,2,1,0:T(8,128)(2,1)S(1)} collective-permute-done((bf16[2,8,16,128]{3,2,1,0:T(8,128)(2,1)}, bf16[2,8,16,128]{3,2,1,0:T(8,128)(2,1)S(1)}, u32[]{:S(2)}, u32[]{:S(2)}) %collective-permute-start.6) | collective-permute-done | bytes 65568 | tf_op jit(solution)/shard_map/ppermute | solution.py:425
  82.5 0.9 %convert_add_fusion = f32[2,8,16,128]{3,2,1,0:T(8,128)S(1)} fusion(bf16[2,8,16,128]{3,2,1,0:T(8,128)(2,1)S(1)} %collective-permute-done.6, bf16[2,8,16,128]{3,2,1,0:T(8,128)(2,1)S(1)} %collective-permute-done.5, bf16[2,8,16,128]{3,2,1,0:T(8,128)(2,1)S(1)} %collective-permute-done.4, bf16[2,8,16,128]{3,2,1,0:T(8,128)(2,1)S(1)} %collective-permute-done.3, ...), kind=kLoop, calls=%fused_computation.3 | loop fusion | flops 491520 | bytes 655360 | tf_op jit(solution)/shard_map/add | solution.py:425
  83.5 2.9 %collective-permute-start.7 = (f32[8,2048]{1,0:T(8,128)S(1)}, f32[8,2048]{1,0:T(8,128)S(1)}, u32[]{:S(2)}, u32[]{:S(2)}) collective-permute-start(f32[8,2048]{1,0:T(8,128)S(1)} %bitcast.31), channel_id=1, source_target_pairs={{0,8},{1,9},{2,10},{3,11},{4,12},{5,13},{6,14},{7,15},{8,0},{9,1},... | collective-permute-start | bytes 196616 | tf_op jit(solution)/shard_map/ppermute | solution.py:457
  86.6 3.8 %finish.1 = (bf16[256,2048]{1,0:T(8,128)(2,1)}, bf16[256,2048]{1,0:T(8,128)(2,1)}, bf16[256,2048]{1,0:T(8,128)(2,1)}) custom-call(bf16[16,2,2,8,16,128]{5,4,3,2,1,0:T(8,128)(2,1)} %bitcast.5.tok_ref, bf16[256,2048]{1,0:T(8,128)(2,1)S(1)} %copy-done.1, bf16[256,2048]{1,0:T(8,128)(2,1)} %v_ref.3, bf16[256,2048]{1,0:T(8,128)(2,1)} %g_ref.3, ...), custom_call_target="tpu_custom_call" | custom-call | flops 1572864 | bytes 8388608 | tf_op jit(solution)/shard_map/finish/pallas_call | solution.py:210
  90.4 0.7 bitcast_select_fusion
  (30 shorter events, 0.4 us)
Async XLA Ops:
  0.6 12.9 %copy-start = (f32[16,32768]{1,0:T(8,128)S(1)}, f32[16,32768]{1,0:T(8,128)}, u32[]{:S(2)}) copy-start(f32[16,32768]{1,0:T(8,128)} %param.19) | copy-start | bytes 6291460
  4.8 37.0 %all-to-all-start = ((bf16[32,2,8,16,128]{4,3,2,1,0:T(8,128)(2,1)}), bf16[32,2,8,16,128]{4,3,2,1,0:T(8,128)(2,1)}, u32[]{:S(2)}, u32[]{:S(2)}) async-start(bf16[32,2,8,16,128]{4,3,2,1,0:T(8,128)(2,1)} %bitcast.27), calls=%async_computation | async-start | bytes 4194304 | tf_op jit(solution)/shard_map/all_to_all | solution.py:440
  15.4 26.4 %copy-start.3 = (bf16[256,512]{1,0:T(8,128)(2,1)S(1)}, bf16[256,512]{1,0:T(8,128)(2,1)}, u32[]{:S(2)}) copy-start(bf16[256,512]{1,0:T(8,128)(2,1)} %constant.56.clone.wi_hbm) | copy-start | bytes 786436
  15.4 26.4 %copy-start.4 = (bf16[512,256]{1,0:T(8,128)(2,1)S(1)}, bf16[512,256]{1,0:T(8,128)(2,1)}, u32[]{:S(2)}) copy-start(bf16[512,256]{1,0:T(8,128)(2,1)} %constant.53.clone.w_hbm) | copy-start | bytes 786436
  15.4 26.4 %copy-start.5 = (f32[256,128]{1,0:T(8,128)S(1)}, f32[256,128]{1,0:T(8,128)}, u32[]{:S(2)}) copy-start(f32[256,128]{1,0:T(8,128)} %constant.58.clone.ts_ref.ts_hbm) | copy-start | bytes 393220
  15.4 26.4 %copy-start.6 = (f32[256,128]{1,0:T(8,128)S(1)}, f32[256,128]{1,0:T(8,128)}, u32[]{:S(2)}) copy-start(f32[256,128]{1,0:T(8,128)} %constant.57.clone.tc_ref.tc_hbm) | copy-start | bytes 393220
  15.4 26.4 %copy-start.7 = (bf16[256,256]{1,0:T(8,128)(2,1)S(1)}, bf16[256,256]{1,0:T(8,128)(2,1)}, u32[]{:S(2)}) copy-start(bf16[256,256]{1,0:T(8,128)(2,1)} %constant.55.clone.mi_hbm) | copy-start | bytes 393220
  15.4 26.4 %copy-start.8 = (bf16[256,256]{1,0:T(8,128)(2,1)S(1)}, bf16[256,256]{1,0:T(8,128)(2,1)}, u32[]{:S(2)}) copy-start(bf16[256,256]{1,0:T(8,128)(2,1)} %constant.54.clone.m_hbm) | copy-start | bytes 393220
  50.6 36.0 %all-to-all-start.1 = ((bf16[32,2,8,16,128]{4,3,2,1,0:T(8,128)(2,1)}), bf16[32,2,8,16,128]{4,3,2,1,0:T(8,128)(2,1)}, u32[]{:S(2)}, u32[]{:S(2)}) async-start(bf16[32,2,8,16,128]{4,3,2,1,0:T(8,128)(2,1)} %bitcast.28), calls=%async_computation.1 | async-start | bytes 4194304 | tf_op jit(solution)/shard_map/all_to_all | solution.py:440
  56.0 30.5 %copy-start.1 = (bf16[256,2048]{1,0:T(8,128)(2,1)S(1)}, bf16[256,2048]{1,0:T(8,128)(2,1)}, u32[]{:S(2)}) copy-start(bf16[256,2048]{1,0:T(8,128)(2,1)} %k_ref.3) | copy-start | bytes 3145732
  56.1 30.5 %copy-start.2 = (bf16[256,256]{1,0:T(8,128)(2,1)S(1)}, bf16[256,256]{1,0:T(8,128)(2,1)}, u32[]{:S(2)}) copy-start(bf16[256,256]{1,0:T(8,128)(2,1)} %constant.59.clone.swap_hbm.swap_ref) | copy-start | bytes 393220
  60.1 15.1 %collective-permute-start = (bf16[2,8,16,128]{3,2,1,0:T(8,128)(2,1)}, bf16[2,8,16,128]{3,2,1,0:T(8,128)(2,1)S(1)}, u32[]{:S(2)}, u32[]{:S(2)}) collective-permute-start(bf16[2,8,16,128]{3,2,1,0:T(8,128)(2,1)} %get-tuple-element.25), channel_id=1, source_target_pairs={{0,4},{1,5},{2,6},{3,7},{4,0},{5,1},{6,2},{7,3},{8,12},{9,13},{10,... | collective-permute-start | bytes 196616 | tf_op jit(solution)/shard_map/ppermute | solution.py:425
  67.1 10.4 %collective-permute-start.1 = (bf16[2,8,16,128]{3,2,1,0:T(8,128)(2,1)}, bf16[2,8,16,128]{3,2,1,0:T(8,128)(2,1)S(1)}, u32[]{:S(2)}, u32[]{:S(2)}) collective-permute-start(bf16[2,8,16,128]{3,2,1,0:T(8,128)(2,1)} %get-tuple-element.26), channel_id=1, source_target_pairs={{0,3},{1,4},{2,5},{3,6},{4,7},{5,0},{6,1},{7,2},{8,11},{9,12},{10,... | collective-permute-start | bytes 196616 | tf_op jit(solution)/shard_map/ppermute | solution.py:425
  68.7 9.1 %collective-permute-start.2 = (bf16[2,8,16,128]{3,2,1,0:T(8,128)(2,1)}, bf16[2,8,16,128]{3,2,1,0:T(8,128)(2,1)S(1)}, u32[]{:S(2)}, u32[]{:S(2)}) collective-permute-start(bf16[2,8,16,128]{3,2,1,0:T(8,128)(2,1)} %get-tuple-element.27), channel_id=1, source_target_pairs={{0,5},{1,6},{2,7},{3,0},{4,1},{5,2},{6,3},{7,4},{8,13},{9,14},{10,... | collective-permute-start | bytes 196616 | tf_op jit(solution)/shard_map/ppermute | solution.py:425
  71.6 6.5 %collective-permute-start.3 = (bf16[2,8,16,128]{3,2,1,0:T(8,128)(2,1)}, bf16[2,8,16,128]{3,2,1,0:T(8,128)(2,1)S(1)}, u32[]{:S(2)}, u32[]{:S(2)}) collective-permute-start(bf16[2,8,16,128]{3,2,1,0:T(8,128)(2,1)} %get-tuple-element.28), channel_id=1, source_target_pairs={{0,2},{1,3},{2,4},{3,5},{4,6},{5,7},{6,0},{7,1},{8,10},{9,11},{10,... | collective-permute-start | bytes 196616 | tf_op jit(solution)/shard_map/ppermute | solution.py:425
  72.8 7.6 %collective-permute-start.4 = (bf16[2,8,16,128]{3,2,1,0:T(8,128)(2,1)}, bf16[2,8,16,128]{3,2,1,0:T(8,128)(2,1)S(1)}, u32[]{:S(2)}, u32[]{:S(2)}) collective-permute-start(bf16[2,8,16,128]{3,2,1,0:T(8,128)(2,1)} %get-tuple-element.29), channel_id=1, source_target_pairs={{0,6},{1,7},{2,0},{3,1},{4,2},{5,3},{6,4},{7,5},{8,14},{9,15},{10,... | collective-permute-start | bytes 196616 | tf_op jit(solution)/shard_map/ppermute | solution.py:425
  75.1 5.2 %collective-permute-start.5 = (bf16[2,8,16,128]{3,2,1,0:T(8,128)(2,1)}, bf16[2,8,16,128]{3,2,1,0:T(8,128)(2,1)S(1)}, u32[]{:S(2)}, u32[]{:S(2)}) collective-permute-start(bf16[2,8,16,128]{3,2,1,0:T(8,128)(2,1)} %get-tuple-element.30), channel_id=1, source_target_pairs={{0,1},{1,2},{2,3},{3,4},{4,5},{5,6},{6,7},{7,0},{8,9},{9,10},{10,1... | collective-permute-start | bytes 196616 | tf_op jit(solution)/shard_map/ppermute | solution.py:425
  77.5 5.1 %collective-permute-start.6 = (bf16[2,8,16,128]{3,2,1,0:T(8,128)(2,1)}, bf16[2,8,16,128]{3,2,1,0:T(8,128)(2,1)S(1)}, u32[]{:S(2)}, u32[]{:S(2)}) collective-permute-start(bf16[2,8,16,128]{3,2,1,0:T(8,128)(2,1)} %get-tuple-element.31), channel_id=1, source_target_pairs={{0,7},{1,0},{2,1},{3,2},{4,3},{5,4},{6,5},{7,6},{8,15},{9,8},{10,9... | collective-permute-start | bytes 196616 | tf_op jit(solution)/shard_map/ppermute | solution.py:425
  83.5 6.9 %collective-permute-start.7 = (f32[8,2048]{1,0:T(8,128)S(1)}, f32[8,2048]{1,0:T(8,128)S(1)}, u32[]{:S(2)}, u32[]{:S(2)}) collective-permute-start(f32[8,2048]{1,0:T(8,128)S(1)} %bitcast.31), channel_id=1, source_target_pairs={{0,8},{1,9},{2,10},{3,11},{4,12},{5,13},{6,14},{7,15},{8,0},{9,1},... | collective-permute-start | bytes 196616 | tf_op jit(solution)/shard_map/ppermute | solution.py:457

commit v6 on v5

--- a/solution.py
+++ b/solution.py
@@ -14,7 +14,7 @@
 VMEM_LIMIT = 56 * 2**20
 SPLIT = 2
 GATE_STEPS = 2
-TOKEN_STEPS = 4
+FINISH_ENDS = (4, 9, 13, 16)
 FILTERS = 4
 FILTER_PAIR = 4
 CROSS_BACK = ("mi", "wi")
@@ -169,25 +169,26 @@
 ):
     n, split, _, kept, cuts, _ = tok_ref.shape
     group = split * kept
-    runs = n // TOKEN_STEPS
+    ends = [n * part // 16 for part in FINISH_ENDS]
+    begins = [0, *ends[:-1]]
 
     def loads(step):
-        rows = pl.ds(step * runs * group, runs * group)
-        at = pl.ds(step * runs, runs)
+        rows = pl.ds(begins[step] * group, (ends[step] - begins[step]) * group)
+        at = pl.ds(begins[step], ends[step] - begins[step])
         pairs = [(tok_ref.at[at], tok.at[at])]
         pairs += [(r.at[rows], s.at[rows]) for r, s in ((g_ref, g), (v_ref, v), (k_ref, k))]
         return copies(pairs, in_sems, step)
 
     def stores(step):
-        rows = pl.ds(step * runs * group, runs * group)
+        rows = pl.ds(begins[step] * group, (ends[step] - begins[step]) * group)
         pairs = [(s.at[rows], r.at[rows]) for r, s in ((gq_ref, gq), (gk_ref, gk), (gv_ref, gv))]
         return copies(pairs, out_sems, step)
 
-    for step in range(TOKEN_STEPS):
+    for step in range(len(FINISH_ENDS)):
         start(loads(step))
-    for step in range(TOKEN_STEPS):
+    for step in range(len(FINISH_ENDS)):
         wait(loads(step))
-        for run in range(step * runs, (step + 1) * runs):
+        for run in range(begins[step], ends[step]):
             rows = slice(run * group, (run + 1) * group)
             both = jnp.concatenate([tok[run, :, s].reshape(group * cuts, LANES) for s in range(2)], 1)
             out = dot(swap_ref[...], both).astype(bf16)
@@ -199,7 +200,7 @@
                 gk[rows, lanes] = dgated * v[rows, lanes]
                 gv[rows, lanes] = dgated * k[rows, lanes]
         start(stores(step))
-    for step in range(TOKEN_STEPS):
+    for step in range(len(FINISH_ENDS)):
         wait(stores(step))
 
 
@@ -214,7 +215,7 @@
         out_shape=[jax.ShapeDtypeStruct((channels, length), bf16)] * 3,
         scratch_shapes=[pltpu.VMEM(tok.shape, bf16)]
         + [pltpu.VMEM(key_in.shape, bf16)] * 6
-        + [pltpu.SemaphoreType.DMA((TOKEN_STEPS, 4)), pltpu.SemaphoreType.DMA((TOKEN_STEPS, 3))],
+        + [pltpu.SemaphoreType.DMA((len(FINISH_ENDS), 4)), pltpu.SemaphoreType.DMA((len(FINISH_ENDS), 3))],
         compiler_params=params(0, 52 * 2**20),
         cost_estimate=pl.CostEstimate(
             flops=3 * channels * length, bytes_accessed=16 * channels * length, transcendentals=0

time: 91.5 us -> 91.5 us (level)
  no operation moved by 1% of the time
where the time goes in v6:
time: 91.5 us; the launch traced here: 91.1 us
  starting transfers between devices  33.1 us (36%)
  waiting for transfers between devices  27.8 us (30%)
  Pallas kernels  25.5 us (28%)
  other arithmetic  2.29 us (3%)
  local copies, waits for them, and re-layouts  1.51 us (2%)
    all_to_all x2, waiting for transfers between devices, exchange(): lax.all_to_all(flat, ('ctx', 'tp'), split_axis=0, concat_axis=0, tiled=Tr...  21.5 us
    ppermute x7, starting transfers between devices, sum_scattered(): total = total + lax.ppermute(parts[step], 'tp', pairs).astype(f32)  16.1 us
    all_to_all x2, starting transfers between devices, exchange(): lax.all_to_all(flat, ('ctx', 'tp'), split_axis=0, concat_axis=0, tiled=Tr...  14.1 us
    pallas_call x1, Pallas kernels, channels(): pl.pallas_call(channels_kernel, in_specs=[ANY] * (2 + len(tables)), out_s...  8.71 us
    ppermute x7, waiting for transfers between devices, sum_scattered(): total = total + lax.ppermute(parts[step], 'tp', pairs).astype(f32)  6.3 us
    pallas_call x1, Pallas kernels, filter_spectrum(): pl.pallas_call(functools.partial(filter_kernel, scale=scale), grid=(n //...  4.86 us
    pallas_call x1, Pallas kernels, gate(): pl.pallas_call(gate_kernel, in_specs=[ANY] * 5, out_specs=ANY, out_shape=...  4.14 us
    pallas_call x1, Pallas kernels, lags(): pl.pallas_call(functools.partial(lags_kernel, scale=scale), in_specs=[pl....  4.01 us
  transfers between devices with their start and end apart: 10, of which 5 were waited for; matrix products, arithmetic and copies ran while one was open for 3% of the time, Pallas kernels for 14%

profile of v6, /device:TPU:1, one launch (start us, length us, event | category | flops | bytes accessed | tf_op | source)
XLA Modules:
  0.0 91.1 jit_solution(9910941506158846896)
XLA Ops:
  0.6 4.1 %gate.1 = bf16[16,2,2,8,16,128]{5,4,3,2,1,0:T(8,128)(2,1)} custom-call(bf16[256,2048]{1,0:T(8,128)(2,1)} %q_ref.1, bf16[256,2048]{1,0:T(8,128)(2,1)} %k_ref.3, bf16[256,2048]{1,0:T(8,128)(2,1)} %v_ref.3, bf16[256,2048]{1,0:T(8,128)(2,1)} %g_ref.3, bf16[256,256]{1,0:T(8,128)(2,1)} %constant.59.clone.swap_hbm.swap_ref), custom_call_target="tpu_custom_call" | custom-call | flops 1048576 | bytes 6291456 | tf_op jit(solution)/shard_map/gate/pallas_call | solution.py:146
  4.8 8.7 %all-to-all-start = ((bf16[32,2,8,16,128]{4,3,2,1,0:T(8,128)(2,1)}), bf16[32,2,8,16,128]{4,3,2,1,0:T(8,128)(2,1)}, u32[]{:S(2)}, u32[]{:S(2)}) async-start(bf16[32,2,8,16,128]{4,3,2,1,0:T(8,128)(2,1)} %bitcast.27), calls=%async_computation | async-start | bytes 4194304 | tf_op jit(solution)/shard_map/all_to_all | solution.py:441
  13.6 1.2 %copy.25 = f32[1,8,256,128]{3,2,1,0:T(8,128)} copy(f32[1,8,256,128]{3,1,2,0:T(8,128)S(1)} %dynamic-slice_bitcast_fusion) | data formatting | bytes 2097152
  14.7 0.6 pad_add_fusion.place_ref
  15.4 4.9 %filter_spectrum.1.f_ref = f32[8,256,256]{2,1,0:T(8,128)} custom-call(f32[8,256,128]{2,1,0:T(8,128)} %bitcast.29, bf16[512,768]{1,0:T(8,128)(2,1)} %constant.51.clone.w_ref, bf16[768,256]{1,0:T(8,128)(2,1)} %constant.52.clone.m_ref, f32[256,128]{1,0:T(8,128)} %constant.57.clone.tc_ref.tc_hbm, f32[256,128]{1,0:T(8,128)} %constant.58.clone.ts_ref.ts_hbm), custom_call_target="tpu_custom_call" | custom-call | flops 1610612736 | bytes 4194304 | tf_op jit(solution)/shard_map/filter_spectrum/pallas_call | solution.py:250
  20.3 21.5 %all-to-all-done = bf16[32,2,8,16,128]{4,3,2,1,0:T(8,128)(2,1)} async-done(((bf16[32,2,8,16,128]{4,3,2,1,0:T(8,128)(2,1)}), bf16[32,2,8,16,128]{4,3,2,1,0:T(8,128)(2,1)}, u32[]{:S(2)}, u32[]{:S(2)}) %all-to-all-start) | async-done | bytes 2097184 | tf_op jit(solution)/shard_map/all_to_all | solution.py:441
  41.8 8.7 %channels.1 = (bf16[8,256,256]{2,1,0:T(8,128)(2,1)}, bf16[16,2,2,8,16,128]{5,4,3,2,1,0:T(8,128)(2,1)}) custom-call(bf16[16,2,2,8,16,128]{5,4,3,2,1,0:T(8,128)(2,1)} %bitcast.3.x_ref, f32[8,256,256]{2,1,0:T(8,128)} %filter_spectrum.1.f_ref, bf16[512,256]{1,0:T(8,128)(2,1)S(1)} %copy-done.4, bf16[256,256]{1,0:T(8,128)(2,1)S(1)} %copy-done.8, ...), custom_call_target="tpu_custom_call" | custom-call | flops 6442450944 | bytes 8388608 | tf_op jit(solution)/shard_map/channels/pallas_call | solution.py:347
  50.6 5.5 %all-to-all-start.1 = ((bf16[32,2,8,16,128]{4,3,2,1,0:T(8,128)(2,1)}), bf16[32,2,8,16,128]{4,3,2,1,0:T(8,128)(2,1)}, u32[]{:S(2)}, u32[]{:S(2)}) async-start(bf16[32,2,8,16,128]{4,3,2,1,0:T(8,128)(2,1)} %bitcast.28), calls=%async_computation.1 | async-start | bytes 4194304 | tf_op jit(solution)/shard_map/all_to_all | solution.py:441
  56.1 4.0 %lags.1 = (bf16[2,8,16,128]{3,2,1,0:T(8,128)(2,1)}, bf16[2,8,16,128]{3,2,1,0:T(8,128)(2,1)}, bf16[2,8,16,128]{3,2,1,0:T(8,128)(2,1)}, bf16[2,8,16,128]{3,2,1,0:T...) custom-call(s32[2]{0:T(128)} %pad_add_fusion.place_ref, ...), custom_call_target="tpu_custom_call" | custom-call | flops 1610612736 | bytes 2097152 | tf_op jit(solution)/shard_map/lags/pallas_call | solution.py:397
  60.1 7.0 %collective-permute-start = (bf16[2,8,16,128]{3,2,1,0:T(8,128)(2,1)}, bf16[2,8,16,128]{3,2,1,0:T(8,128)(2,1)S(1)}, u32[]{:S(2)}, u32[]{:S(2)}) collective-permute-start(bf16[2,8,16,128]{3,2,1,0:T(8,128)(2,1)} %get-tuple-element.25), channel_id=1, source_target_pairs={{0,4},{1,5},{2,6},{3,7},{4,0},{5,1},{6,2},{7,3},{8,12},{9,13},{10,... | collective-permute-start | bytes 196616 | tf_op jit(solution)/shard_map/ppermute | solution.py:426
  67.1 1.6 %collective-permute-start.1 = (bf16[2,8,16,128]{3,2,1,0:T(8,128)(2,1)}, bf16[2,8,16,128]{3,2,1,0:T(8,128)(2,1)S(1)}, u32[]{:S(2)}, u32[]{:S(2)}) collective-permute-start(bf16[2,8,16,128]{3,2,1,0:T(8,128)(2,1)} %get-tuple-element.26), channel_id=1, source_target_pairs={{0,3},{1,4},{2,5},{3,6},{4,7},{5,0},{6,1},{7,2},{8,11},{9,12},{10,... | collective-permute-start | bytes 196616 | tf_op jit(solution)/shard_map/ppermute | solution.py:426
  68.7 2.8 %collective-permute-start.2 = (bf16[2,8,16,128]{3,2,1,0:T(8,128)(2,1)}, bf16[2,8,16,128]{3,2,1,0:T(8,128)(2,1)S(1)}, u32[]{:S(2)}, u32[]{:S(2)}) collective-permute-start(bf16[2,8,16,128]{3,2,1,0:T(8,128)(2,1)} %get-tuple-element.27), channel_id=1, source_target_pairs={{0,5},{1,6},{2,7},{3,0},{4,1},{5,2},{6,3},{7,4},{8,13},{9,14},{10,... | collective-permute-start | bytes 196616 | tf_op jit(solution)/shard_map/ppermute | solution.py:426
  71.6 1.2 %collective-permute-start.3 = (bf16[2,8,16,128]{3,2,1,0:T(8,128)(2,1)}, bf16[2,8,16,128]{3,2,1,0:T(8,128)(2,1)S(1)}, u32[]{:S(2)}, u32[]{:S(2)}) collective-permute-start(bf16[2,8,16,128]{3,2,1,0:T(8,128)(2,1)} %get-tuple-element.28), channel_id=1, source_target_pairs={{0,2},{1,3},{2,4},{3,5},{4,6},{5,7},{6,0},{7,1},{8,10},{9,11},{10,... | collective-permute-start | bytes 196616 | tf_op jit(solution)/shard_map/ppermute | solution.py:426
  72.8 2.4 %collective-permute-start.4 = (bf16[2,8,16,128]{3,2,1,0:T(8,128)(2,1)}, bf16[2,8,16,128]{3,2,1,0:T(8,128)(2,1)S(1)}, u32[]{:S(2)}, u32[]{:S(2)}) collective-permute-start(bf16[2,8,16,128]{3,2,1,0:T(8,128)(2,1)} %get-tuple-element.29), channel_id=1, source_target_pairs={{0,6},{1,7},{2,0},{3,1},{4,2},{5,3},{6,4},{7,5},{8,14},{9,15},{10,... | collective-permute-start | bytes 196616 | tf_op jit(solution)/shard_map/ppermute | solution.py:426
  75.1 0.7 collective-permute-start.5
  75.9 1.6 %collective-permute-done.1 = bf16[2,8,16,128]{3,2,1,0:T(8,128)(2,1)S(1)} collective-permute-done((bf16[2,8,16,128]{3,2,1,0:T(8,128)(2,1)}, bf16[2,8,16,128]{3,2,1,0:T(8,128)(2,1)S(1)}, u32[]{:S(2)}, u32[]{:S(2)}) %collective-permute-start.1) | collective-permute-done | bytes 65568 | tf_op jit(solution)/shard_map/ppermute | solution.py:426
  77.5 0.4 collective-permute-start.6
  77.8 0.2 collective-permute-done.3
  78.0 2.3 %collective-permute-done.4 = bf16[2,8,16,128]{3,2,1,0:T(8,128)(2,1)S(1)} collective-permute-done((bf16[2,8,16,128]{3,2,1,0:T(8,128)(2,1)}, bf16[2,8,16,128]{3,2,1,0:T(8,128)(2,1)S(1)}, u32[]{:S(2)}, u32[]{:S(2)}) %collective-permute-start.4) | collective-permute-done | bytes 65568 | tf_op jit(solution)/shard_map/ppermute | solution.py:426
  80.3 2.2 %collective-permute-done.6 = bf16[2,8,16,128]{3,2,1,0:T(8,128)(2,1)S(1)} collective-permute-done((bf16[2,8,16,128]{3,2,1,0:T(8,128)(2,1)}, bf16[2,8,16,128]{3,2,1,0:T(8,128)(2,1)S(1)}, u32[]{:S(2)}, u32[]{:S(2)}) %collective-permute-start.6) | collective-permute-done | bytes 65568 | tf_op jit(solution)/shard_map/ppermute | solution.py:426
  82.5 0.9 %convert_add_fusion = f32[2,8,16,128]{3,2,1,0:T(8,128)S(1)} fusion(bf16[2,8,16,128]{3,2,1,0:T(8,128)(2,1)S(1)} %collective-permute-done.6, bf16[2,8,16,128]{3,2,1,0:T(8,128)(2,1)S(1)} %collective-permute-done.5, bf16[2,8,16,128]{3,2,1,0:T(8,128)(2,1)S(1)} %collective-permute-done.4, bf16[2,8,16,128]{3,2,1,0:T(8,128)(2,1)S(1)} %collective-permute-done.3, ...), kind=kLoop, calls=%fused_computation.3 | loop fusion | flops 491520 | bytes 655360 | tf_op jit(solution)/shard_map/add | solution.py:426
  83.5 2.9 %collective-permute-start.7 = (f32[8,2048]{1,0:T(8,128)S(1)}, f32[8,2048]{1,0:T(8,128)S(1)}, u32[]{:S(2)}, u32[]{:S(2)}) collective-permute-start(f32[8,2048]{1,0:T(8,128)S(1)} %bitcast.31), channel_id=1, source_target_pairs={{0,8},{1,9},{2,10},{3,11},{4,12},{5,13},{6,14},{7,15},{8,0},{9,1},... | collective-permute-start | bytes 196616 | tf_op jit(solution)/shard_map/ppermute | solution.py:458
  86.6 3.8 %finish.1 = (bf16[256,2048]{1,0:T(8,128)(2,1)}, bf16[256,2048]{1,0:T(8,128)(2,1)}, bf16[256,2048]{1,0:T(8,128)(2,1)}) custom-call(bf16[16,2,2,8,16,128]{5,4,3,2,1,0:T(8,128)(2,1)} %bitcast.5.tok_ref, bf16[256,2048]{1,0:T(8,128)(2,1)S(1)} %copy-done.1, bf16[256,2048]{1,0:T(8,128)(2,1)} %v_ref.3, bf16[256,2048]{1,0:T(8,128)(2,1)} %g_ref.3, ...), custom_call_target="tpu_custom_call" | custom-call | flops 1572864 | bytes 8388608 | tf_op jit(solution)/shard_map/finish/pallas_call | solution.py:211
  90.4 0.7 bitcast_select_fusion
  (30 shorter events, 0.4 us)
Async XLA Ops:
  0.6 12.9 %copy-start = (f32[16,32768]{1,0:T(8,128)S(1)}, f32[16,32768]{1,0:T(8,128)}, u32[]{:S(2)}) copy-start(f32[16,32768]{1,0:T(8,128)} %param.19) | copy-start | bytes 6291460
  4.8 37.0 %all-to-all-start = ((bf16[32,2,8,16,128]{4,3,2,1,0:T(8,128)(2,1)}), bf16[32,2,8,16,128]{4,3,2,1,0:T(8,128)(2,1)}, u32[]{:S(2)}, u32[]{:S(2)}) async-start(bf16[32,2,8,16,128]{4,3,2,1,0:T(8,128)(2,1)} %bitcast.27), calls=%async_computation | async-start | bytes 4194304 | tf_op jit(solution)/shard_map/all_to_all | solution.py:441
  15.4 26.4 %copy-start.3 = (bf16[256,512]{1,0:T(8,128)(2,1)S(1)}, bf16[256,512]{1,0:T(8,128)(2,1)}, u32[]{:S(2)}) copy-start(bf16[256,512]{1,0:T(8,128)(2,1)} %constant.56.clone.wi_hbm) | copy-start | bytes 786436
  15.4 26.4 %copy-start.4 = (bf16[512,256]{1,0:T(8,128)(2,1)S(1)}, bf16[512,256]{1,0:T(8,128)(2,1)}, u32[]{:S(2)}) copy-start(bf16[512,256]{1,0:T(8,128)(2,1)} %constant.53.clone.w_hbm) | copy-start | bytes 786436
  15.4 26.4 %copy-start.5 = (f32[256,128]{1,0:T(8,128)S(1)}, f32[256,128]{1,0:T(8,128)}, u32[]{:S(2)}) copy-start(f32[256,128]{1,0:T(8,128)} %constant.58.clone.ts_ref.ts_hbm) | copy-start | bytes 393220
  15.4 26.4 %copy-start.6 = (f32[256,128]{1,0:T(8,128)S(1)}, f32[256,128]{1,0:T(8,128)}, u32[]{:S(2)}) copy-start(f32[256,128]{1,0:T(8,128)} %constant.57.clone.tc_ref.tc_hbm) | copy-start | bytes 393220
  15.4 26.4 %copy-start.7 = (bf16[256,256]{1,0:T(8,128)(2,1)S(1)}, bf16[256,256]{1,0:T(8,128)(2,1)}, u32[]{:S(2)}) copy-start(bf16[256,256]{1,0:T(8,128)(2,1)} %constant.55.clone.mi_hbm) | copy-start | bytes 393220
  15.4 26.4 %copy-start.8 = (bf16[256,256]{1,0:T(8,128)(2,1)S(1)}, bf16[256,256]{1,0:T(8,128)(2,1)}, u32[]{:S(2)}) copy-start(bf16[256,256]{1,0:T(8,128)(2,1)} %constant.54.clone.m_hbm) | copy-start | bytes 393220
  50.6 36.0 %all-to-all-start.1 = ((bf16[32,2,8,16,128]{4,3,2,1,0:T(8,128)(2,1)}), bf16[32,2,8,16,128]{4,3,2,1,0:T(8,128)(2,1)}, u32[]{:S(2)}, u32[]{:S(2)}) async-start(bf16[32,2,8,16,128]{4,3,2,1,0:T(8,128)(2,1)} %bitcast.28), calls=%async_computation.1 | async-start | bytes 4194304 | tf_op jit(solution)/shard_map/all_to_all | solution.py:441
  56.0 30.5 %copy-start.1 = (bf16[256,2048]{1,0:T(8,128)(2,1)S(1)}, bf16[256,2048]{1,0:T(8,128)(2,1)}, u32[]{:S(2)}) copy-start(bf16[256,2048]{1,0:T(8,128)(2,1)} %k_ref.3) | copy-start | bytes 3145732
  56.1 30.5 %copy-start.2 = (bf16[256,256]{1,0:T(8,128)(2,1)S(1)}, bf16[256,256]{1,0:T(8,128)(2,1)}, u32[]{:S(2)}) copy-start(bf16[256,256]{1,0:T(8,128)(2,1)} %constant.59.clone.swap_hbm.swap_ref) | copy-start | bytes 393220
  60.1 15.1 %collective-permute-start = (bf16[2,8,16,128]{3,2,1,0:T(8,128)(2,1)}, bf16[2,8,16,128]{3,2,1,0:T(8,128)(2,1)S(1)}, u32[]{:S(2)}, u32[]{:S(2)}) collective-permute-start(bf16[2,8,16,128]{3,2,1,0:T(8,128)(2,1)} %get-tuple-element.25), channel_id=1, source_target_pairs={{0,4},{1,5},{2,6},{3,7},{4,0},{5,1},{6,2},{7,3},{8,12},{9,13},{10,... | collective-permute-start | bytes 196616 | tf_op jit(solution)/shard_map/ppermute | solution.py:426
  67.1 10.4 %collective-permute-start.1 = (bf16[2,8,16,128]{3,2,1,0:T(8,128)(2,1)}, bf16[2,8,16,128]{3,2,1,0:T(8,128)(2,1)S(1)}, u32[]{:S(2)}, u32[]{:S(2)}) collective-permute-start(bf16[2,8,16,128]{3,2,1,0:T(8,128)(2,1)} %get-tuple-element.26), channel_id=1, source_target_pairs={{0,3},{1,4},{2,5},{3,6},{4,7},{5,0},{6,1},{7,2},{8,11},{9,12},{10,... | collective-permute-start | bytes 196616 | tf_op jit(solution)/shard_map/ppermute | solution.py:426
  68.7 9.1 %collective-permute-start.2 = (bf16[2,8,16,128]{3,2,1,0:T(8,128)(2,1)}, bf16[2,8,16,128]{3,2,1,0:T(8,128)(2,1)S(1)}, u32[]{:S(2)}, u32[]{:S(2)}) collective-permute-start(bf16[2,8,16,128]{3,2,1,0:T(8,128)(2,1)} %get-tuple-element.27), channel_id=1, source_target_pairs={{0,5},{1,6},{2,7},{3,0},{4,1},{5,2},{6,3},{7,4},{8,13},{9,14},{10,... | collective-permute-start | bytes 196616 | tf_op jit(solution)/shard_map/ppermute | solution.py:426
  71.6 6.5 %collective-permute-start.3 = (bf16[2,8,16,128]{3,2,1,0:T(8,128)(2,1)}, bf16[2,8,16,128]{3,2,1,0:T(8,128)(2,1)S(1)}, u32[]{:S(2)}, u32[]{:S(2)}) collective-permute-start(bf16[2,8,16,128]{3,2,1,0:T(8,128)(2,1)} %get-tuple-element.28), channel_id=1, source_target_pairs={{0,2},{1,3},{2,4},{3,5},{4,6},{5,7},{6,0},{7,1},{8,10},{9,11},{10,... | collective-permute-start | bytes 196616 | tf_op jit(solution)/shard_map/ppermute | solution.py:426
  72.8 7.6 %collective-permute-start.4 = (bf16[2,8,16,128]{3,2,1,0:T(8,128)(2,1)}, bf16[2,8,16,128]{3,2,1,0:T(8,128)(2,1)S(1)}, u32[]{:S(2)}, u32[]{:S(2)}) collective-permute-start(bf16[2,8,16,128]{3,2,1,0:T(8,128)(2,1)} %get-tuple-element.29), channel_id=1, source_target_pairs={{0,6},{1,7},{2,0},{3,1},{4,2},{5,3},{6,4},{7,5},{8,14},{9,15},{10,... | collective-permute-start | bytes 196616 | tf_op jit(solution)/shard_map/ppermute | solution.py:426
  75.1 5.2 %collective-permute-start.5 = (bf16[2,8,16,128]{3,2,1,0:T(8,128)(2,1)}, bf16[2,8,16,128]{3,2,1,0:T(8,128)(2,1)S(1)}, u32[]{:S(2)}, u32[]{:S(2)}) collective-permute-start(bf16[2,8,16,128]{3,2,1,0:T(8,128)(2,1)} %get-tuple-element.30), channel_id=1, source_target_pairs={{0,1},{1,2},{2,3},{3,4},{4,5},{5,6},{6,7},{7,0},{8,9},{9,10},{10,1... | collective-permute-start | bytes 196616 | tf_op jit(solution)/shard_map/ppermute | solution.py:426
  77.5 5.1 %collective-permute-start.6 = (bf16[2,8,16,128]{3,2,1,0:T(8,128)(2,1)}, bf16[2,8,16,128]{3,2,1,0:T(8,128)(2,1)S(1)}, u32[]{:S(2)}, u32[]{:S(2)}) collective-permute-start(bf16[2,8,16,128]{3,2,1,0:T(8,128)(2,1)} %get-tuple-element.31), channel_id=1, source_target_pairs={{0,7},{1,0},{2,1},{3,2},{4,3},{5,4},{6,5},{7,6},{8,15},{9,8},{10,9... | collective-permute-start | bytes 196616 | tf_op jit(solution)/shard_map/ppermute | solution.py:426
  83.5 6.8 %collective-permute-start.7 = (f32[8,2048]{1,0:T(8,128)S(1)}, f32[8,2048]{1,0:T(8,128)S(1)}, u32[]{:S(2)}, u32[]{:S(2)}) collective-permute-start(f32[8,2048]{1,0:T(8,128)S(1)} %bitcast.31), channel_id=1, source_target_pairs={{0,8},{1,9},{2,10},{3,11},{4,12},{5,13},{6,14},{7,15},{8,0},{9,1},... | collective-permute-start | bytes 196616 | tf_op jit(solution)/shard_map/ppermute | solution.py:458
